TPU v7x, 128 devices: a whole 4x4x4 slice. The times are simulated.
128 devices in a mesh: sub: 4 (over y_lo, core), pul: 32 (over y_hi, z, x).
Axes of the slice: x: 4, y: 4 (y_hi: 2, y_lo: 2; y = y_hi * 2 + y_lo), z: 4, core: 2. Of those that a mesh axis runs over, the one named last changes fastest.
Arguments:
- raw_echo: bfloat16 [2, 4, 4096, 16384], P(None, 'sub', None, 'pul'), may hold values from -3 to 3
- range_phase: float32 [4096], replicated, may hold values from -3.140625 to 3.140625
- kappa: float32 [4096], P('pul'), may hold values from 0.5 to 4
- doppler: float32 [4, 16384], replicated, may hold values from -3.140625 to 3.140625
- migration: int32 [128, 16384], P('pul'), may hold values from 0 to 8, as said below
Outputs:
- image: bfloat16 [2, 4096, 16384], P(None, 'pul', 'sub')
Inputs may be any that keep to these rules, and one draw needn't show every extreme that they name: `migration`: shifts are whole range bins; the value 8 occurs.
All inputs are finite; a program needn't handle non-finite values.
Results may differ from a plain program's by a relative error of at most 0.02.
Values may be sent and summed in bfloat16 or wider, within the bound.
No kernel may reach another device: no remote copies, remote signals or barrier semaphores. Data moves between devices by JAX's collectives and lax.ppermute only.
A program may use at most 192 MiB of HBM per device.

v0:
```python
import math

import jax
import jax.numpy as jnp
from jax import lax
from jax.sharding import PartitionSpec as P

MAXS = 8
RBLK = 32


def shifted_2(value, axis, steps):
    count = lax.axis_size(axis)
    leading, last = (max(0, -steps), min(count, count - steps))
    return lax.ppermute(value, axis, [(source, source + steps) for source in range(leading, last)])


def factor_pair(length):
    inner_len = 1
    for candidate in range(1, math.isqrt(length) + 1):
        if length % candidate == 0:
            inner_len = candidate
    return (inner_len, length // inner_len)


def fourier_table(length, direction):
    indices = jnp.arange(length, dtype=jnp.int32)
    product = indices[:, None] * indices[None, :] % length
    angles = direction * 2.0 * math.pi / length * product.astype(jnp.float32)
    cosine = jnp.cos(angles)
    sine_part = jnp.sin(angles)
    upper_half = jnp.stack([cosine, -sine_part], axis=1)
    lower_half = jnp.stack([sine_part, cosine], axis=1)
    return jnp.stack([upper_half, lower_half], axis=0).astype(jnp.bfloat16)


def twiddle(outer_len, inner_len, direction):
    length = outer_len * inner_len
    row_ids = jnp.arange(outer_len, dtype=jnp.int32)[:, None]
    col_ids = jnp.arange(inner_len, dtype=jnp.int32)[None, :]
    angles = direction * 2.0 * math.pi / length * (row_ids * col_ids % length).astype(jnp.float32)
    scaling = 1.0 / math.sqrt(length)
    return (jnp.cos(angles) * scaling, jnp.sin(angles) * scaling)


def complex_times(pair, cosine, sine_part):
    real_part = pair[0] * cosine - pair[1] * sine_part
    imag_part = pair[0] * sine_part + pair[1] * cosine
    return jnp.stack([real_part, imag_part], axis=0)


def forward_steps(values, outer_len, inner_len):
    lead_len = values.shape[1]
    tail_len = values.shape[3]
    grid_view = values.reshape(2, lead_len, outer_len, inner_len, tail_len)
    first_pass = jnp.einsum(
        "dkcm,camib->dakib",
        fourier_table(outer_len, -1),
        grid_view,
        preferred_element_type=jnp.float32,
    )
    cosine, sine_part = twiddle(outer_len, inner_len, -1)
    middle = complex_times(first_pass, cosine[:, :, None], sine_part[:, :, None]).astype(
        jnp.bfloat16
    )
    return jnp.einsum(
        "dkcm,caqmb->daqkb",
        fourier_table(inner_len, -1),
        middle,
        preferred_element_type=jnp.float32,
    )


def backward_steps(spectrum):
    lead_len, outer_len, inner_len, tail_len = (
        spectrum.shape[1],
        spectrum.shape[2],
        spectrum.shape[3],
        spectrum.shape[4],
    )
    first_pass = jnp.einsum(
        "dkcm,caqmb->daqkb",
        fourier_table(inner_len, 1),
        spectrum,
        preferred_element_type=jnp.float32,
    )
    cosine, sine_part = twiddle(outer_len, inner_len, 1)
    middle = complex_times(first_pass, cosine[:, :, None], sine_part[:, :, None]).astype(
        jnp.bfloat16
    )
    result = jnp.einsum(
        "dkcm,camib->dakib", fourier_table(outer_len, 1), middle, preferred_element_type=jnp.float32
    )
    return result.reshape(2, lead_len, outer_len * inner_len, tail_len)


def forward_rows(values, outer_len, inner_len):
    row_count = values.shape[1]
    grid_view = values.reshape(2, row_count, outer_len, inner_len)
    first_pass = jnp.einsum(
        "dkcm,camj->dakj",
        fourier_table(outer_len, -1),
        grid_view,
        preferred_element_type=jnp.float32,
    )
    cosine, sine_part = twiddle(outer_len, inner_len, -1)
    middle = complex_times(first_pass, cosine, sine_part).astype(jnp.bfloat16)
    return jnp.einsum(
        "dkcj,caqj->daqk", fourier_table(inner_len, -1), middle, preferred_element_type=jnp.float32
    )


def backward_rows(spectrum):
    row_count, outer_len, inner_len = (spectrum.shape[1], spectrum.shape[2], spectrum.shape[3])
    first_pass = jnp.einsum(
        "dkcm,caqm->daqk", fourier_table(inner_len, 1), spectrum, preferred_element_type=jnp.float32
    )
    cosine, sine_part = twiddle(outer_len, inner_len, 1)
    middle = complex_times(first_pass, cosine, sine_part).astype(jnp.bfloat16)
    result = jnp.einsum(
        "dkcm,cami->daki", fourier_table(outer_len, 1), middle, preferred_element_type=jnp.float32
    )
    return result.reshape(2, row_count, outer_len * inner_len)


def reorder_last(values, inner_len, outer_len):
    lead_shape = values.shape[:-1]
    grid_view = values.reshape(lead_shape + (inner_len, outer_len))
    return jnp.swapaxes(grid_view, -1, -2).reshape(lead_shape + (inner_len * outer_len,))


def apply_migration(extended, shift_perm, own_rows):
    lead = extended.shape[:2]
    pulse_len = extended.shape[-1]
    block_count = own_rows // RBLK
    block_shift = shift_perm[:, None, :]
    shifted = jnp.zeros(lead + (block_count, RBLK, pulse_len), extended.dtype)
    for offset in range(MAXS + 1):
        window = extended[:, :, offset : offset + own_rows, :].reshape(
            lead + (block_count, RBLK, pulse_len)
        )
        shifted = jnp.where(block_shift == offset, window, shifted)
    return shifted.reshape(lead + (own_rows, pulse_len))


def on_device(raw_echo, range_phase, kappa, doppler, migration):
    range_len = raw_echo.shape[2]
    pulse_dev = raw_echo.shape[3]
    pul_count = lax.axis_size("pul")
    pulse_len = pulse_dev * pul_count
    range_inner, range_outer = factor_pair(range_len)
    pulse_inner, pulse_outer = factor_pair(pulse_len)
    sub_index = lax.axis_index("sub")
    freq_perm = forward_steps(raw_echo, range_outer, range_inner)
    phase_perm = reorder_last(range_phase, range_inner, range_outer).reshape(
        range_outer, range_inner
    )
    range_cos = jnp.cos(phase_perm)[None, :, :, None]
    range_sin = jnp.sin(phase_perm)[None, :, :, None]
    ranged = complex_times(freq_perm, range_cos, range_sin).astype(jnp.bfloat16)
    compressed = backward_steps(ranged).astype(jnp.bfloat16).reshape(2, range_len, pulse_dev)
    turned = lax.all_to_all(compressed, "pul", split_axis=1, concat_axis=2, tiled=True)
    own_rows = turned.shape[1]
    turned = turned.reshape(2, 1, own_rows, pulse_len)
    doppler_rows = lax.dynamic_slice_in_dim(doppler, sub_index, 1, 0)
    groups = turned.shape[1]
    spectrum = forward_rows(
        turned.reshape(2, groups * own_rows, pulse_len), pulse_outer, pulse_inner
    )
    spectrum = spectrum.astype(jnp.bfloat16).reshape(2, groups, own_rows, pulse_len)
    rim_rows = spectrum[:, :, :MAXS, :]
    halo_rows = shifted_2(rim_rows, "pul", -1)
    extended = jnp.concatenate([spectrum, halo_rows], axis=2)
    shift_perm = reorder_last(migration, pulse_inner, pulse_outer)
    shifted = apply_migration(extended, shift_perm, own_rows)
    doppler_perm = reorder_last(doppler_rows, pulse_inner, pulse_outer)
    phases = kappa[None, :, None] * doppler_perm[:, None, :]
    filtered = complex_times(shifted.astype(jnp.float32), jnp.cos(phases), jnp.sin(phases)).astype(
        jnp.bfloat16
    )
    filtered = filtered.reshape(2, groups * own_rows, pulse_outer, pulse_inner)
    sub_image = backward_rows(filtered).reshape(2, groups, own_rows, pulse_len).astype(jnp.bfloat16)
    terms = sub_image[:, 0].astype(jnp.float32)
    return lax.psum_scatter(terms.astype(jnp.bfloat16), "sub", scatter_dimension=2, tiled=True)


def solution(mesh):
    placed = (P(None, "sub", None, "pul"), P(), P("pul"), P(), P("pul", None))
    return jax.shard_map(
        on_device, mesh=mesh, in_specs=placed, out_specs=P(None, "pul", "sub"), check_vma=False
    )
```

profile of v0, /device:TPU:7, one launch (start us, length us, event | category | flops | bytes accessed | tf_op | source)
XLA Modules:
  0.0 602.5 jit_solution(5352508574509728632)
XLA Ops:
  7.0 14.0 %fusion.44 = f32[2,64,64,512,1]{3,1,4,2,0:T(8,128)S(1)} fusion(bf16[2,64,64,512]{3,2,1,0:T(8,128)(2,1)} %bitcast.330, bf16[1,64,2,64]{3,1,2,0:T(8,128)(2,1)S(1)} %get-tuple-element.29, bf16[1,64,2,64]{3,1,2,0:T(8,128)(2,1)S(1)} %get-tuple-element.28), kind=kOutput, calls=%fused_computation.82 | convolution fusion | flops 1073807360 | bytes 25198592 | tf_op jit(solution)/shard_map/dkcm,camib->dakib/dot_general | solution.py:56
  21.0 2.1 fusion.52
  23.1 2.6 fusion.53
  25.7 6.2 %maximum_bitcast_fusion = bf16[2,64,64,512,1]{3,1,2,0,4:T(8,128)(2,1)} fusion(bf16[1,64,64,512]{3,1,2,0:T(8,128)(2,1)} %fusion.53, bf16[1,64,64,512]{3,1,2,0:T(8,128)(2,1)S(1)} %fusion.52), kind=kLoop, calls=%fused_computation.50 | loop fusion | flops 4194304 | bytes 16777216 | tf_op jit(solution)/shard_map/stack | solution.py:49
  31.9 17.9 %convolution_bitcast_fusion.3 = f32[2,1,64,64,512]{4,3,0,2,1:T(8,128)} fusion(bf16[2,64,64,512,1]{3,1,2,0,4:T(8,128)(2,1)} %maximum_bitcast_fusion, bf16[1,64,2,64]{3,1,2,0:T(8,128)(2,1)S(1)} %get-tuple-element.29, bf16[1,64,2,64]{3,1,2,0:T(8,128)(2,1)S(1)} %get-tuple-element.28), kind=kOutput, calls=%fused_computation.26 | convolution fusion | flops 1073807360 | bytes 25198592 | tf_op jit(solution)/shard_map/dkcm,caqmb->daqkb/dot_general | solution.py:66
  50.2 8.7 %fusion.54 = bf16[1,64,64,512]{3,2,1,0:T(8,128)(2,1)} fusion(f32[2,1,64,64,512]{4,3,0,2,1:T(8,128)} %convolution_bitcast_fusion.3, f32[64,64]{1,0:T(8,128)S(1)} %copy.197, f32[64,64]{1,0:T(8,128)S(1)} %copy.196), kind=kLoop, calls=%fused_computation.94 | loop fusion | flops 8388608 | bytes 21004288 | tf_op jit(solution)/shard_map/stack | solution.py:49
  58.9 3.4 copy-done.2
  62.3 2.8 fusion.55
  65.9 5.1 convolution_bitcast_fusion.2
  72.7 3.0 fusion.57
  75.8 6.2 %maximum_bitcast_fusion.2 = bf16[2,64,64,512,1]{3,2,1,0,4:T(8,128)(2,1)} fusion(bf16[1,64,64,512]{3,2,1,0:T(8,128)(2,1)} %fusion.57, bf16[1,64,64,512]{3,2,1,0:T(8,128)(2,1)S(1)} %fusion.56), kind=kLoop, calls=%fused_computation.52 | loop fusion | flops 4194304 | bytes 16777216 | tf_op jit(solution)/shard_map/stack | solution.py:49
  82.0 16.9 %fusion.47 = bf16[2,1,64,64,512]{4,2,0,3,1:T(8,128)(2,1)} fusion(bf16[2,64,64,512,1]{3,2,1,0,4:T(8,128)(2,1)} %maximum_bitcast_fusion.2, bf16[1,64,2,64]{3,1,2,0:T(8,128)(2,1)S(1)} %get-tuple-element.25, bf16[1,64,2,64]{3,1,2,0:T(8,128)(2,1)S(1)} %get-tuple-element.24), kind=kOutput, calls=%fused_computation.89 | convolution fusion | flops 1078001664 | bytes 16809984 | tf_op jit(solution)/shard_map/dkcm,camib->dakib/dot_general | solution.py:91
  98.9 11.4 %copy.209 = bf16[2,1,64,64,512]{4,3,2,0,1:T(8,128)(2,1)} copy(bf16[2,1,64,64,512]{4,2,0,3,1:T(8,128)(2,1)} %fusion.47) | data formatting | bytes 16777216 | tf_op jit(solution)/shard_map/convert_element_type | solution.py:161
  110.3 16.4 %copy.210 = bf16[2,4096,512]{2,0,1:T(2,128)(2,1)} copy(bf16[2,4096,512]{2,1,0:T(8,128)(2,1)} %bitcast.325) | data formatting | bytes 16777216 | tf_op jit(solution)/shard_map/convert_element_type | solution.py:161
  126.7 10.9 %all-to-all-start = ((bf16[2,4096,512]{2,0,1:T(2,128)(2,1)}), bf16[2,4096,512]{2,0,1:T(2,128)(2,1)}, u32[]{:S(2)}, u32[]{:S(2)}) async-start(bf16[2,4096,512]{2,0,1:T(2,128)(2,1)} %copy.210), calls=%async_computation | async-start | bytes 16777216 | tf_op jit(solution)/shard_map/all_to_all | solution.py:162
  138.7 2.0 broadcast_in_dim.125
  140.7 6.0 copy.219
  147.0 2.0 broadcast_in_dim.128
  149.0 5.9 copy.221
  155.2 2.0 broadcast_in_dim.131
  157.2 5.9 copy.223
  163.4 2.0 broadcast_in_dim.134
  165.4 5.9 copy.225
  173.7 5.9 copy.227
  181.9 5.9 copy.229
  190.1 5.9 copy.231
  198.3 5.9 copy.233
  206.5 6.3 %copy.188 = pred[128,16384]{0,1:T(8,128)(4,1)} copy(pred[128,16384]{1,0:T(8,128)(4,1)} %bitcast.339) | data formatting | bytes 4194304 | tf_op jit(solution)/shard_map/jit(_where)/broadcast_in_dim | solution.py:142
  213.8 46.4 %all-to-all-done = bf16[2,4096,512]{2,0,1:T(2,128)(2,1)} async-done(((bf16[2,4096,512]{2,0,1:T(2,128)(2,1)}), bf16[2,4096,512]{2,0,1:T(2,128)(2,1)}, u32[]{:S(2)}, u32[]{:S(2)}) %all-to-all-start) | async-done | bytes 8388640 | tf_op jit(solution)/shard_map/all_to_all | solution.py:162
  260.2 7.9 %copy.211 = bf16[2,4096,512]{2,1,0:T(8,128)(2,1)} copy(bf16[2,4096,512]{2,0,1:T(2,128)(2,1)} %all-to-all-done) | data formatting | bytes 16777216 | tf_op jit(solution)/shard_map/all_to_all | solution.py:162
  268.2 12.0 %copy.212 = bf16[2,128,32,512]{1,3,2,0:T(8,128)(2,1)} copy(bf16[2,128,32,512]{3,1,2,0:T(8,128)(2,1)} %bitcast.326) | data formatting | bytes 16777216 | tf_op jit(solution)/shard_map/all_to_all | solution.py:162
  280.2 13.5 %copy.251 = bf16[2,128,128,128,1]{2,3,0,4,1:T(8,128)(2,1)} copy(bf16[2,128,128,128,1]{1,3,2,0,4:T(8,128)(2,1)} %bitcast.327) | data formatting | bytes 16777216 | tf_op jit(solution)/shard_map/reshape;reshape;reshape | solution.py:99
  293.7 4.8 convolution_bitcast_fusion.1
  298.5 3.9 subtract_convert_fusion.1
  302.4 7.9 %fusion.50 = bf16[2,128,128,128]{3,2,0,1:T(8,128)(2,1)} fusion(bf16[1,128,128,128]{2,3,0,1:T(8,128)(2,1)} %get-tuple-element.8, bf16[1,128,128,128]{2,3,0,1:T(8,128)(2,1)S(1)} %get-tuple-element.7, bf16[1,128,2,128]{3,1,2,0:T(8,128)(2,1)S(1)} %get-tuple-element.23, bf16[1,128,2,128]{3,1,2,0:T(8,128)(2,1)S(1)} %get-tuple-element.22), kind=kOutput, calls=%fused_computation.90 | convolution fusion | flops 2168717312 | bytes 16908288 | tf_op jit(solution)/shard_map/dkcj,caqj->daqk/dot_general | solution.py:108
  310.3 12.5 %reshape.756 = bf16[2,1,128,16384]{3,0,2,1:T(2,128)(2,1)} reshape(bf16[2,128,128,128]{3,2,0,1:T(8,128)(2,1)} %fusion.50) | data formatting | bytes 16777216 | tf_op jit(solution)/shard_map/reshape | solution.py:170
  327.8 21.3 %copy.216 = bf16[2,1,128,16384]{2,3,1,0:T(8,128)(2,1)} copy(bf16[2,1,128,16384]{3,0,2,1:T(2,128)(2,1)} %reshape.756) | data formatting | bytes 16777216 | tf_op jit(solution)/shard_map/reshape | solution.py:170
  349.1 5.7 copy.217
  354.7 66.8 %fusion.16 = f32[2,1,128,16384]{2,3,1,0:T(8,128)} fusion(bf16[2,1,128,16384]{2,3,1,0:T(8,128)(2,1)} %copy.216, bf16[2,1,8,16384]{2,3,1,0:T(8,128)(2,1)} %copy.217, pred[128,16384]{0,1:T(8,128)(4,1)} %copy.233, pred[128,16384]{0,1:T(8,128)(4,1)} %copy.231, pred[128,16384]{0,1:T(8,128)(4,1)} %copy.229, pred[128,16384]{0,1:T(8,128)(4,1)} %copy.227, ...), kind=kLoop, calls=%fused_computation.39 | loop fusion | flops 176160768 | bytes 44564480 | tf_op jit(solution)/shard_map/convert_element_type | solution.py:178
  421.5 38.8 %fusion.5 = (bf16[1,1,128,16384]{2,3,1,0:T(8,128)(2,1)}, bf16[1,1,128,16384]{2,3,1,0:T(8,128)(2,1)}) fusion(f32[2,1,128,16384]{2,3,1,0:T(8,128)} %fusion.16, f32[16384]{0:T(1024)S(1)} %bitcast.340, f32[128]{0:T(128)S(1)} %copy-done.5), kind=kLoop, calls=%fused_computation.28 | loop fusion | flops 18874368 | bytes 25231872 | tf_op jit(solution)/shard_map/convert.13
  460.4 6.7 %copy.236 = bf16[1,128,128,128]{3,2,0,1:T(8,128)(2,1)} copy(bf16[1,128,128,128]{1,3,2,0:T(8,128)(2,1)} %bitcast.329) | data formatting | bytes 8388608 | tf_op jit(solution)/shard_map/stack | solution.py:49
  467.1 6.8 %copy.237 = bf16[1,128,128,128]{3,2,0,1:T(8,128)(2,1)} copy(bf16[1,128,128,128]{1,3,2,0:T(8,128)(2,1)} %bitcast.328) | data formatting | bytes 8388608 | tf_op jit(solution)/shard_map/stack | solution.py:49
  473.8 4.9 convolution_bitcast_fusion
  478.7 4.1 subtract_convert_fusion
  482.7 7.9 %fusion.51 = bf16[2,128,128,128]{2,3,0,1:T(8,128)(2,1)} fusion(bf16[1,128,128,128]{3,2,0,1:T(8,128)(2,1)} %get-tuple-element.6, bf16[1,128,128,128]{3,2,0,1:T(8,128)(2,1)S(1)} %get-tuple-element.5, bf16[1,128,2,128]{3,1,2,0:T(8,128)(2,1)S(1)} %get-tuple-element.21, bf16[1,128,2,128]{3,1,2,0:T(8,128)(2,1)S(1)} %get-tuple-element.20), kind=kOutput, calls=%fused_computation.91 | convolution fusion | flops 2168717312 | bytes 16908288 | tf_op jit(solution)/shard_map/dkcm,cami->daki/dot_general | solution.py:120
  490.6 13.6 %copy.241 = bf16[2,128,128,128]{1,3,2,0:T(8,128)(2,1)} copy(bf16[2,128,128,128]{2,3,0,1:T(8,128)(2,1)} %fusion.51) | data formatting | bytes 16777216 | tf_op jit(solution)/shard_map/convert_element_type | solution.py:182
  504.2 87.1 %reduce-scatter.2.cloned.1.call-done = bf16[2,128,4096]{1,2,0:T(8,128)(2,1)} async-done(((bf16[2,128,16384]{1,2,0:T(8,128)(2,1)}), bf16[2,128,4096]{1,2,0:T(8,128)(2,1)}) %reduce-scatter.2.cloned.1.call-update) | async-done | bytes 2097168 | tf_op jit(solution)/shard_map/reduce_scatter | solution.py:184
  591.3 4.1 copy.242
  (76 shorter events, 22.5 us)
Async XLA Ops:
  6.5 206.3 %copy-start = (f32[4,16384]{1,0:T(4,128)S(1)}, f32[4,16384]{1,0:T(4,128)}, u32[]{:S(2)}) copy-start(f32[4,16384]{1,0:T(4,128)} %param.8) | copy-start | bytes 786436
  31.9 17.9 %copy-start.4 = (f32[4096]{0:T(1024)S(1)}, f32[4096]{0:T(1024)}, u32[]{:S(2)}) copy-start(f32[4096]{0:T(1024)} %param.6) | copy-start | bytes 49156
  50.2 12.2 %copy-start.2 = (f32[2,1,64,64,512]{4,3,0,2,1:T(8,128)S(1)}, f32[2,1,64,64,512]{4,3,0,2,1:T(8,128)}, u32[]{:S(2)}) copy-start(f32[2,1,64,64,512]{4,3,0,2,1:T(8,128)} %convolution_bitcast_fusion.3) | copy-start | bytes 50331652
  126.7 11.0 %copy-start.3 = (s32[4,16384]{1,0:T(4,128)S(1)}, s32[4,16384]{1,0:T(4,128)}, u32[]{:S(2)}) copy-start(s32[4,16384]{1,0:T(4,128)} %param.9) | copy-start | bytes 786436
  126.7 133.6 %all-to-all-start = ((bf16[2,4096,512]{2,0,1:T(2,128)(2,1)}), bf16[2,4096,512]{2,0,1:T(2,128)(2,1)}, u32[]{:S(2)}, u32[]{:S(2)}) async-start(bf16[2,4096,512]{2,0,1:T(2,128)(2,1)} %copy.210), calls=%async_computation | async-start | bytes 16777216 | tf_op jit(solution)/shard_map/all_to_all | solution.py:162
  137.6 453.8 %reduce-scatter.2.cloned.1.call-start = ((), (), s32[]{:S(2)}) async-start(), calls=%async_computation.2 | async-start | bytes 10485760 | tf_op jit(solution)/shard_map/reduce_scatter | solution.py:184
  324.5 24.5 %collective-permute-start = (bf16[2,1,8,16384]{3,2,1,0:T(8,128)(2,1)S(1)}, bf16[2,1,8,16384]{3,2,1,0:T(8,128)(2,1)S(1)}, u32[]{:S(2)}, u32[]{:S(2)}) collective-permute-start(bf16[2,1,8,16384]{3,2,1,0:T(8,128)(2,1)S(1)} %copy.273), channel_id=1, source_target_pairs={{1,0},{2,1},{3,2},{4,3},{5,4},{6,5},{7,6},{8,7},{9,8},{10,9},{11,1... | collective-permute-start | bytes 1572872 | tf_op jit(solution)/shard_map/ppermute | solution.py:15
  354.7 66.8 %copy-start.5 = (f32[128]{0:T(128)S(1)}, f32[128]{0:T(128)}, u32[]{:S(2)}) copy-start(f32[128]{0:T(128)} %param.7) | copy-start | bytes 1540
  490.6 104.8 %copy-start.1 = (f32[4,16384]{1,0:T(4,128)S(1)}, f32[4,16384]{1,0:T(4,128)}, u32[]{:S(2)}) copy-start(f32[4,16384]{1,0:T(4,128)} %param.8) | copy-start | bytes 786436
Sparse Core Ops, SparseCore 0:
  504.4 86.9 reduce-scatter.1
where the time goes:
time: 614 us; the launch traced here: 602 us
  local copies, waits for them, and re-layouts  212 us (35%)
  other arithmetic  151 us (25%)
  waiting for transfers between devices  133 us (22%)
  matrix products  79.3 us (13%)
  between operations  14.1 us (2%)
  starting transfers between devices  12.8 us (2%)
    reduce_scatter x1, waiting for transfers between devices, on_device(): lax.psum_scatter(terms.astype(jnp.bfloat16), 'sub', scatter_dimension=2,...  87.1 us
    broadcast_in_dim x18, local copies, waits for them, and re-layouts, apply_migration(): shifted = jnp.where(block_shift == offset, window, shifted)  71.7 us
    convert_element_type x1, other arithmetic, on_device(): shifted.astype(jnp.float32)  66.8 us
    another operation x11, other arithmetic  48.5 us
    all_to_all x1, waiting for transfers between devices, on_device(): lax.all_to_all(compressed, 'pul', split_axis=1, concat_axis=2, tiled=True)  46.4 us
    reshape x2, local copies, waits for them, and re-layouts, on_device(): spectrum.astype(jnp.bfloat16).reshape(2, groups, own_rows, pulse_len)  33.8 us
    another operation x8, other arithmetic, complex_times(): return jnp.stack([real_part, imag_part], axis=0)  33.3 us
    convert_element_type x2, local copies, waits for them, and re-layouts, on_device(): backward_steps(ranged).astype(jnp.bfloat16).reshape(2, range_len, pulse_dev)  27.8 us
  transfers between devices with their start and end apart: 3, of which 2 were waited for; matrix products, arithmetic and copies ran while one was open for 16% of the time, Pallas kernels for 0%

commit v1 on v0

v1 whole, which is shorter than its diff:
```python
import functools
import math

import jax
import jax.numpy as jnp
import numpy as np
from jax import lax
from jax.experimental import pallas as pl
from jax.experimental.pallas import tpu as pltpu
from jax.sharding import PartitionSpec as P

MAXS = 8
RBLK = 32
LANES = 128
CHUNKS = 2
VMEM = 56 * 1024 * 1024
F32 = jnp.float32
BF16 = jnp.bfloat16


def realified(table):
    return np.block([[table.real, -table.imag], [table.imag, table.real]])


def unit_table(rows, cols, length, direction):
    product = np.outer(np.asarray(rows), np.asarray(cols)) % length
    return np.exp(direction * 2j * np.pi * product / length)


def as_bf16(table):
    return np.asarray(table, np.float32).astype(BF16)


def range_middle(range_phase, size):
    length = size * size
    k2 = np.arange(size)[:, None, None]
    j1 = np.arange(size)[None, :, None]
    k1 = np.arange(size)[None, None, :]
    wave = np.exp(2j * np.pi * ((j1 * (k2 + size * k1)) % length) / length) / size
    wave_r, wave_i = wave.real.astype(np.float32), wave.imag.astype(np.float32)
    right = np.concatenate(
        [
            np.concatenate([wave_r, -wave_i], axis=2),
            np.concatenate([wave_i, wave_r], axis=2),
        ],
        axis=1,
    )
    phase = range_phase.reshape(size, size).T
    cosine, sine = jnp.cos(phase)[:, None, :], jnp.sin(phase)[:, None, :]
    left_r = wave_r * cosine - wave_i * sine
    left_i = wave_r * sine + wave_i * cosine
    left = jnp.concatenate(
        [
            jnp.concatenate([left_r, -left_i], axis=2),
            jnp.concatenate([left_i, left_r], axis=2),
        ],
        axis=1,
    ).astype(BF16)
    middle = jnp.einsum("kae,kbe->kab", left, as_bf16(right), preferred_element_type=F32)
    return middle.astype(BF16)


def range_kernel(size, x_ref, w_ref, t_ref, v_ref, o_ref, one, two):
    length = size * size
    halves = x_ref.shape[2] // LANES
    both = 2 * size

    def cast(step, carry):
        for h in range(halves):
            for c in range(2):
                one[h, pl.ds(c * length + 128 * step, 128), :] = x_ref[
                    c, pl.ds(pl.multiple_of(128 * step, 128), 128), h * LANES : (h + 1) * LANES
                ].astype(F32)
        return carry

    lax.fori_loop(0, length // 128, cast, 0)

    def strided(source, target, table):
        def body(step, carry):
            for u in range(4):
                j1 = step * 4 + u
                value = jnp.concatenate(
                    [source[h, pl.ds(j1, both, stride=size), :] for h in range(halves)], axis=1
                ).astype(BF16)
                out = jnp.dot(table, value, preferred_element_type=F32)
                for h in range(halves):
                    target[h, pl.ds(j1, both, stride=size), :] = out[
                        :, h * LANES : (h + 1) * LANES
                    ]
            return carry

        lax.fori_loop(0, size // 4, body, 0)

    strided(one, two, w_ref[...])

    def inner(step, carry):
        for u in range(4):
            k2 = step * 4 + u
            value = jnp.concatenate(
                [
                    jnp.concatenate(
                        [
                            two[h, pl.ds(pl.multiple_of((c * size + k2) * size, size), size), :]
                            for c in range(2)
                        ],
                        axis=0,
                    )
                    for h in range(halves)
                ],
                axis=1,
            ).astype(BF16)
            out = jnp.dot(t_ref[k2], value, preferred_element_type=F32)
            for h in range(halves):
                for d in range(2):
                    one[h, pl.ds(pl.multiple_of((d * size + k2) * size, size), size), :] = out[
                        d * size : (d + 1) * size, h * LANES : (h + 1) * LANES
                    ]
        return carry

    lax.fori_loop(0, size // 4, inner, 0)
    strided(one, two, v_ref[...])
    blocks, rows = o_ref.shape[0], o_ref.shape[2]

    def give(step, carry):
        for u in range(4):
            block = step * 4 + u
            for d in range(2):
                for h in range(halves):
                    o_ref[block, d, :, h * LANES : (h + 1) * LANES] = two[
                        h, pl.ds(pl.multiple_of(d * length + block * rows, rows), rows), :
                    ].astype(BF16)
        return carry

    lax.fori_loop(0, blocks // 4, give, 0)


def range_compress(echo, middle, chunk, width, blocks):
    length = echo.shape[1]
    size = math.isqrt(length)
    index = np.arange(size)
    forward = as_bf16(realified(unit_table(index, index, size, -1)))
    backward = as_bf16(realified(unit_table(index, index, size, 1)))
    rows = length // blocks
    whole = lambda *shape: pl.BlockSpec(shape, lambda i: (0,) * len(shape))
    return pl.pallas_call(
        functools.partial(range_kernel, size),
        grid=(1,),
        in_specs=[
            pl.BlockSpec((2, length, width), lambda i: (0, 0, chunk)),
            whole(2 * size, 2 * size),
            whole(size, 2 * size, 2 * size),
            whole(2 * size, 2 * size),
        ],
        out_specs=whole(blocks, 2, rows, width),
        out_shape=jax.ShapeDtypeStruct((blocks, 2, rows, width), BF16),
        scratch_shapes=[
            pltpu.VMEM((width // LANES, 2 * length, LANES), F32),
            pltpu.VMEM((width // LANES, 2 * length, LANES), F32),
        ],
        compiler_params=pltpu.CompilerParams(vmem_limit_bytes=VMEM),
        name="range_compress",
    )(echo, forward, middle, backward)


def doppler_kernel(rows, *refs):
    parts = refs[:CHUNKS]
    w_ref, cos_ref, sin_ref, u_ref, o_ref, held = refs[CHUNKS:]
    sources = parts[0].shape[0]
    halves = parts[0].shape[4] // LANES
    size = cos_ref.shape[0]

    def cast(source, carry):
        for q in range(CHUNKS):
            for c in range(2):
                for h in range(halves):
                    base = ((c * CHUNKS + q) * halves + h) * sources
                    held[pl.ds(pl.multiple_of((base + source) * rows, rows), rows), :] = parts[q][
                        source, 0, c, :, h * LANES : (h + 1) * LANES
                    ].astype(F32)
        return carry

    lax.fori_loop(0, sources, cast, 0)

    def body(step, carry):
        pair = [step * 2, step * 2 + 1]
        value = jnp.concatenate(
            [held[pl.ds(row, 2 * size, stride=rows), :] for row in pair], axis=1
        ).astype(BF16)
        first = jnp.dot(w_ref[...], value, preferred_element_type=F32)
        stacked = []
        for i in range(2):
            real = first[:size, i * LANES : (i + 1) * LANES]
            imag = first[size:, i * LANES : (i + 1) * LANES]
            stacked.append(
                jnp.concatenate(
                    [
                        real * cos_ref[...] - imag * sin_ref[...],
                        real * sin_ref[...] + imag * cos_ref[...],
                    ],
                    axis=1,
                ).astype(BF16)
            )
        second = jnp.dot(
            jnp.concatenate(stacked, axis=0), u_ref[...], preferred_element_type=F32
        ).astype(BF16)
        for i in range(2):
            for d in range(2):
                o_ref[0, pair[i], d] = second[i * size : (i + 1) * size, d * LANES : (d + 1) * LANES]
        return carry

    lax.fori_loop(0, rows // 2, body, 0)


def doppler_tables(size, direction):
    index = np.arange(size)
    table = unit_table(index, index, size, direction)
    turn = unit_table(index, index, size * size, direction) / size
    return table, turn.real.astype(np.float32), turn.imag.astype(np.float32)


def doppler_forward(parts, part, rows, size):
    sources, subs, _, _, width = parts[0].shape
    halves = width // LANES
    table, turn_cos, turn_sin = doppler_tables(size, -1)
    per_source = size // sources
    order = np.asarray(
        [
            per_source * source + q * halves + h
            for q in range(CHUNKS)
            for h in range(halves)
            for source in range(sources)
        ]
    )
    outer = as_bf16(realified(table[:, order]))
    inner = as_bf16(realified(table).T)
    whole = lambda *shape: pl.BlockSpec(shape, lambda i: (0,) * len(shape))
    piece = pl.BlockSpec((sources, 1, 2, rows, width), lambda i: (0, i, 0, part, 0))
    return pl.pallas_call(
        functools.partial(doppler_kernel, rows),
        grid=(subs,),
        in_specs=[piece] * CHUNKS
        + [
            whole(2 * size, 2 * size),
            whole(size, size),
            whole(size, size),
            whole(2 * size, 2 * size),
        ],
        out_specs=pl.BlockSpec((1, rows, 2, size, size), lambda i: (i, 0, 0, 0, 0)),
        out_shape=jax.ShapeDtypeStruct((subs, rows, 2, size, size), BF16),
        scratch_shapes=[pltpu.VMEM((2 * size * rows, LANES), F32)],
        compiler_params=pltpu.CompilerParams(vmem_limit_bytes=VMEM),
        name="doppler_forward",
    )(*parts, outer, turn_cos, turn_sin, inner)


def turn_polynomials():
    nodes = 0.25 * (1 - np.cos((np.arange(64) + 0.5) * np.pi / 64)) / 2
    roots = np.sqrt(nodes)
    sine = np.polynomial.polynomial.polyfit(nodes, np.sin(2 * np.pi * roots) / roots, 6)
    cosine = np.polynomial.polynomial.polyfit(nodes, np.cos(2 * np.pi * roots), 6)
    return [round(float(v), 7) for v in sine], [round(float(v), 7) for v in cosine]


def turns(cycles):
    sine_terms, cosine_terms = turn_polynomials()
    part = cycles - jnp.floor(cycles + 0.5)
    square = part * part
    sine = jnp.full_like(square, sine_terms[-1])
    cosine = jnp.full_like(square, cosine_terms[-1])
    for term in reversed(sine_terms[:-1]):
        sine = sine * square + term
    for term in reversed(cosine_terms[:-1]):
        cosine = cosine * square + term
    return cosine, sine * part


def image_kernel(kappa_ref, *refs):
    low, high, rim, shift_ref, phase_ref, w_ref, cos_ref, sin_ref, u_ref, o_ref = refs[:10]
    moved, summed, middle, turned = refs[10:]
    step = pl.program_id(0)
    subs, half = low.shape[0], low.shape[1]
    rows = 2 * half
    tile = low.shape[3]
    size = w_ref.shape[0] // 2
    shift = shift_ref[...]
    bits = [(shift & 1) > 0, (shift & 2) > 0, (shift & 4) > 0, (shift & 8) > 0]

    def aperture(index, carry):
        for d in range(2):
            values = [low[index, r, d].astype(F32) for r in range(half)]
            values += [high[index, r, d].astype(F32) for r in range(half)]
            values += [rim[index, r, d].astype(F32) for r in range(MAXS)]
            four = [jnp.where(bits[2], values[r + 4], values[r]) for r in range(rows + 3)]
            two = [jnp.where(bits[1], four[r + 2], four[r]) for r in range(rows + 1)]
            one = [jnp.where(bits[0], two[r + 1], two[r]) for r in range(rows)]
            for r in range(rows):
                moved[index, d, r] = jnp.where(bits[3], values[r + 8], one[r])
        return carry

    lax.fori_loop(0, subs, aperture, 0)

    def row_sum(row, carry):
        factor = kappa_ref[row]
        real = jnp.zeros((tile, size), F32)
        imag = jnp.zeros((tile, size), F32)
        for index in range(subs):
            cosine, sine = turns(factor * phase_ref[index])
            a, b = moved[index, 0, row], moved[index, 1, row]
            real = real + (a * cosine - b * sine)
            imag = imag + (a * sine + b * cosine)
        summed[pl.ds(pl.multiple_of(row * tile, tile), tile), :] = jnp.concatenate(
            [real, imag], axis=1
        ).astype(BF16)
        return carry

    lax.fori_loop(0, rows, row_sum, 0)
    first = jnp.dot(summed[...], u_ref[...], preferred_element_type=F32)
    for r in range(rows):
        real = first[r * tile : (r + 1) * tile, :size]
        imag = first[r * tile : (r + 1) * tile, size:]
        where = pl.ds(pl.multiple_of(step * tile, tile), tile)
        middle[r, 0, where, :] = (real * cos_ref[...] - imag * sin_ref[...]).astype(BF16)
        middle[r, 1, where, :] = (real * sin_ref[...] + imag * cos_ref[...]).astype(BF16)

    @pl.when(step == pl.num_programs(0) - 1)
    def _():
        def body(pair, carry):
            value = jnp.concatenate(
                [
                    jnp.concatenate([middle[pair * 2 + i, c] for c in range(2)], axis=0)
                    for i in range(2)
                ],
                axis=1,
            )
            out = jnp.dot(w_ref[...], value, preferred_element_type=F32)
            for i in range(2):
                turned[pl.ds(pair * 2 + i, 2 * size, stride=rows), :] = out[
                    :, i * LANES : (i + 1) * LANES
                ]
            return carry

        lax.fori_loop(0, rows // 2, body, 0)
        groups = o_ref.shape[0]
        per_group = size // groups

        def give(group, carry):
            for d in range(2):
                for j in range(per_group):
                    line = (d * size + group * per_group + j) * rows
                    o_ref[group, d, :, j * LANES : (j + 1) * LANES] = turned[
                        pl.ds(pl.multiple_of(line, rows), rows), :
                    ].astype(BF16)
            return carry

        lax.fori_loop(0, groups, give, 0)


def image_rows(kappa, low, high, rim, shift, phase, groups):
    subs, half, _, size, _ = low.shape
    rows = 2 * half
    tile = 16
    table, turn_cos, turn_sin = doppler_tables(size, 1)
    outer = as_bf16(realified(table))
    inner = as_bf16(realified(table).T)
    whole = lambda *shape: pl.BlockSpec(shape, lambda i: (0,) * len(shape))
    lines = pl.BlockSpec((tile, size), lambda i: (i, 0))
    width = size * size // groups
    return pl.pallas_call(
        image_kernel,
        grid=(size // tile,),
        in_specs=[
            pl.BlockSpec(memory_space=pltpu.SMEM),
            pl.BlockSpec((subs, half, 2, tile, size), lambda i: (0, 0, 0, i, 0)),
            pl.BlockSpec((subs, half, 2, tile, size), lambda i: (0, 0, 0, i, 0)),
            pl.BlockSpec((subs, MAXS, 2, tile, size), lambda i: (0, 0, 0, i, 0)),
            lines,
            pl.BlockSpec((subs, tile, size), lambda i: (0, i, 0)),
            whole(2 * size, 2 * size),
            lines,
            lines,
            whole(2 * size, 2 * size),
        ],
        out_specs=whole(groups, 2, rows, width),
        out_shape=jax.ShapeDtypeStruct((groups, 2, rows, width), BF16),
        scratch_shapes=[
            pltpu.VMEM((subs, 2, rows, tile, size), F32),
            pltpu.VMEM((rows * tile, 2 * size), BF16),
            pltpu.VMEM((rows, 2, size, size), BF16),
            pltpu.VMEM((2 * size * rows, LANES), F32),
        ],
        compiler_params=pltpu.CompilerParams(vmem_limit_bytes=VMEM),
        name="image_rows",
    )(kappa, low, high, rim, shift, phase, outer, turn_cos, turn_sin, inner)


def on_device(raw_echo, range_phase, kappa, doppler, migration):
    _, _, range_len, pulse_dev = raw_echo.shape
    puls, subs = lax.axis_size("pul"), lax.axis_size("sub")
    blocks = puls * subs
    rows = range_len // blocks
    pulse_len = pulse_dev * puls
    size = math.isqrt(pulse_len)
    sub_index = lax.axis_index("sub")
    middle = range_middle(range_phase, math.isqrt(range_len))
    echo = raw_echo.reshape(2, range_len, pulse_dev)
    width = pulse_dev // CHUNKS
    parts = []
    for chunk in range(CHUNKS):
        sent = range_compress(echo, middle, chunk, width, blocks)
        got = lax.all_to_all(sent, ("pul", "sub"), 0, 0, tiled=True)
        parts.append(got.reshape(puls, subs, 2, rows, width))
    own_shift = lax.dynamic_slice_in_dim(migration, sub_index, 1, 0)
    shift = own_shift.reshape(size, size).T
    phase = jnp.swapaxes(doppler.reshape(subs, size, size), 1, 2) * (0.5 / math.pi)
    own_kappa = lax.dynamic_slice_in_dim(kappa, sub_index * rows, rows, 0)
    half = rows // 2
    low = doppler_forward(parts, 0, half, size)
    place = lambda block: (block % subs) * puls + block // subs
    pairs = [(place(block), place(block - 1)) for block in range(1, blocks)]
    rim = lax.ppermute(low[:, :MAXS], ("sub", "pul"), pairs)
    high = doppler_forward(parts, 1, half, size)
    sent = image_rows(own_kappa, low, high, rim, shift, phase, subs)
    return lax.all_to_all(sent, "sub", 0, 2, tiled=True).reshape(2, rows * subs, pulse_len // subs)


def solution(mesh):
    placed = (P(None, "sub", None, "pul"), P(), P("pul"), P(), P("pul", None))
    return jax.shard_map(
        on_device, mesh=mesh, in_specs=placed, out_specs=P(None, "pul", "sub"), check_vma=False
    )
```

time: 614 us -> 270 us (0.44); the launches traced: 602 us -> 270 us
  local copies, waits for them, and re-layouts: 212 us -> 9.39 us
  other arithmetic: 151 us -> 3.39 us
  Pallas kernels: 0 us -> 122 us
  waiting for transfers between devices: 133 us -> 27.7 us
  blocking collectives: 0 us -> 90.9 us
  matrix products: 79.3 us -> 2.84 us
  between operations: 14.1 us -> 0.09 us
    pallas_call x0 -> x5, Pallas kernels: none -> 122 us  [the longest x2 61.7 us: range_compress(): pl.pallas_call(functools.partial(range_kernel, size), grid=(1,), in_specs...]
    all_to_all x0 -> x2, blocking collectives: none -> 90.9 us  [the longest x1 59.9 us: on_device(): got = lax.all_to_all(sent, ('pul', 'sub'), 0, 0, tiled=True)]
    reduce_scatter x1 -> x0, waiting for transfers between devices: 87.1 us -> none  [on_device(): lax.psum_scatter(terms.astype(jnp.bfloat16), 'sub', scatter_dimension=2,...]
    another operation x23 -> x1, other arithmetic: 81.9 us -> 3.32 us
    dot_general x8 -> x1, matrix products: 79.3 us -> 2.84 us  [range_middle(): jnp.einsum('kae,kbe->kab', left, as_bf16(right), preferred_element_type=F32)]
    broadcast_in_dim x18 -> x0, local copies, waits for them, and re-layouts: 71.7 us -> none  [apply_migration(): shifted = jnp.where(block_shift == offset, window, shifted)]
    convert_element_type x1 -> x0, other arithmetic: 66.8 us -> none  [on_device(): shifted.astype(jnp.float32)]
    convert_element_type x3 -> x0, local copies, waits for them, and re-layouts: 41.4 us -> none  [the longest x2 27.8 us: on_device(): backward_steps(ranged).astype(jnp.bfloat16).reshape(2, range_len, pulse_dev)]
  transfers between devices with their start and end apart: 3 -> 2, of which waited for: 2 -> 2; matrix products, arithmetic and copies ran while one was open for 16% -> 1% of each run, Pallas kernels for 0% -> 18%
where the time goes in v1:
time: 270 us
  Pallas kernels  122 us (45%)
  blocking collectives  90.9 us (34%)
  waiting for transfers between devices  27.7 us (10%)
  starting transfers between devices  13.8 us (5%)
  local copies, waits for them, and re-layouts  9.39 us (3%)
  other arithmetic  3.39 us (1%)
  matrix products  2.84 us (1%)
    pallas_call x2, Pallas kernels, range_compress(): pl.pallas_call(functools.partial(range_kernel, size), grid=(1,), in_specs...  61.7 us
    all_to_all x1, blocking collectives, on_device(): got = lax.all_to_all(sent, ('pul', 'sub'), 0, 0, tiled=True)  59.9 us
    pallas_call x2, Pallas kernels, doppler_forward(): pl.pallas_call(functools.partial(doppler_kernel, rows), grid=(subs,), in_...  33.1 us
    all_to_all x1, blocking collectives, on_device(): lax.all_to_all(sent, 'sub', 0, 2, tiled=True)  31 us
    pallas_call x1, Pallas kernels, image_rows(): pl.pallas_call(image_kernel, grid=(size // tile,), in_specs=[pl.BlockSpec...  27 us
    all_to_all x1, waiting for transfers between devices, on_device(): got = lax.all_to_all(sent, ('pul', 'sub'), 0, 0, tiled=True)  21.6 us
    all_to_all x1, starting transfers between devices, on_device(): got = lax.all_to_all(sent, ('pul', 'sub'), 0, 0, tiled=True)  11.2 us
    ppermute x1, waiting for transfers between devices, on_device(): rim = lax.ppermute(low[:, :MAXS], ('sub', 'pul'), pairs)  6.12 us
  transfers between devices with their start and end apart: 2, of which 2 were waited for; matrix products, arithmetic and copies ran while one was open for 1% of the time, Pallas kernels for 18%

profile of v1, /device:TPU:7, one launch (start us, length us, event | category | flops | bytes accessed | tf_op | source)
XLA Modules:
  0.0 269.9 jit_solution(1772558980451127785)
XLA Ops:
  0.0 0.0 copy-start
  0.0 0.8 fusion.13
  0.8 0.1 sin.10
  0.9 0.1 copy.26
  1.0 0.1 cos.10
  1.1 0.1 copy.25
  1.1 0.0 copy-start.4
  1.2 3.3 %negate_convert_fusion = (bf16[64,64,64]{2,1,0:T(8,128)(2,1)S(1)}, bf16[64,64,64]{2,1,0:T(8,128)(2,1)S(1)}, bf16[64,64,64]{2,1,0:T(8,128)(2,1)S(1)}) fusion(f32[64,64,64]{2,1,0:T(8,128)} %constant.41.clone, f32[64,64,64]{2,1,0:T(8,128)} %constant.40.clone, f32[64,64]{1,0:T(8,128)S(1)} %copy.26, f32[64,64]{1,0:T(8,128)S(1)} %copy.25), kind=kLoop, calls=%fused_computation.8 | loop fusion | flops 2621440 | bytes 3702784 | tf_op jit(solution)/shard_map/convert.5
  4.5 0.0 copy-done.4
  4.5 2.8 %fusion.9.t_ref = bf16[64,128,128]{2,1,0:T(8,128)(2,1)} fusion(bf16[64,128,128]{2,1,0:T(8,128)(2,1)S(1)} %copy-done.4, bf16[64,64,64]{2,1,0:T(8,128)(2,1)S(1)} %get-tuple-element.7, bf16[64,64,64]{2,1,0:T(8,128)(2,1)S(1)} %get-tuple-element.6, bf16[64,64,64]{2,1,0:T(8,128)(2,1)S(1)} %get-tuple-element.5), kind=kOutput, calls=%fused_computation.12 | convolution fusion | flops 277872640 | bytes 5767168 | tf_op jit(solution)/shard_map/kae,kbe->kab/dot_general | solution.py:59
  7.3 30.9 %range_compress.2 = bf16[128,2,32,256]{3,2,1,0:T(8,128)(2,1)} custom-call(bf16[2,4096,512]{2,1,0:T(8,128)(2,1)} %bitcast.20, bf16[128,128]{1,0:T(8,128)(2,1)} %constant.43.clone.w_ref, bf16[64,128,128]{2,1,0:T(8,128)(2,1)} %fusion.9.t_ref, bf16[128,128]{1,0:T(8,128)(2,1)} %constant.44.clone.v_ref), custom_call_target="tpu_custom_call" | custom-call | tf_op jit(solution)/shard_map/range_compress/pallas_call | solution.py:145
  38.2 11.2 %all-to-all-start = ((bf16[128,2,32,256]{3,2,1,0:T(8,128)(2,1)}), bf16[128,2,32,256]{3,2,1,0:T(8,128)(2,1)}, u32[]{:S(2)}, u32[]{:S(2)}) async-start(bf16[128,2,32,256]{3,2,1,0:T(8,128)(2,1)} %range_compress.2), calls=%async_computation | async-start | bytes 8388608 | tf_op jit(solution)/shard_map/all_to_all | solution.py:410
  49.4 30.9 %range_compress.3 = bf16[128,2,32,256]{3,2,1,0:T(8,128)(2,1)} custom-call(bf16[2,4096,512]{2,1,0:T(8,128)(2,1)} %bitcast.21, bf16[128,128]{1,0:T(8,128)(2,1)} %constant.43.clone.w_ref, bf16[64,128,128]{2,1,0:T(8,128)(2,1)} %fusion.9.t_ref, bf16[128,128]{1,0:T(8,128)(2,1)} %constant.44.clone.v_ref), custom_call_target="tpu_custom_call" | custom-call | tf_op jit(solution)/shard_map/range_compress/pallas_call | solution.py:145
  80.3 21.6 %all-to-all-done = bf16[128,2,32,256]{3,2,1,0:T(8,128)(2,1)} async-done(((bf16[128,2,32,256]{3,2,1,0:T(8,128)(2,1)}), bf16[128,2,32,256]{3,2,1,0:T(8,128)(2,1)}, u32[]{:S(2)}, u32[]{:S(2)}) %all-to-all-start) | async-done | bytes 4194336 | tf_op jit(solution)/shard_map/all_to_all | solution.py:410
  101.9 59.9 %all_to_all.25 = bf16[128,2,32,256]{3,2,1,0:T(8,128)(2,1)} all-to-all(bf16[128,2,32,256]{3,2,1,0:T(8,128)(2,1)} %range_compress.3), channel_id=1, replica_groups=mesh['sub'=4,'pul'=32] {'pul','sub'}, dimensions={0} | all-to-all | bytes 8388608 | tf_op jit(solution)/shard_map/all_to_all | solution.py:410
  161.8 16.6 %doppler_forward.2.refs_0_ = bf16[4,16,2,128,128]{4,3,2,1,0:T(8,128)(2,1)} custom-call(bf16[32,4,2,32,256]{4,3,2,1,0:T(8,128)(2,1)} %bitcast.3.refs_0_, bf16[32,4,2,32,256]{4,3,2,1,0:T(8,128)(2,1)} %bitcast.18, bf16[256,256]{1,0:T(8,128)(2,1)} %constant.45.clone.refs_2_, f32[128,128]{1,0:T(8,128)} %constant.46.clone.refs_3_.refs_6_, ...), custom_call_target="tpu_custom_call" | custom-call | tf_op jit(solution)/shard_map/doppler_forward/pallas_call | solution.py:238
  178.3 0.0 copy-start.2
  178.3 0.0 copy-start.3
  178.3 3.2 %slice.4 = bf16[4,8,2,128,128]{4,3,2,1,0:T(8,128)(2,1)} slice(bf16[4,16,2,128,128]{4,3,2,1,0:T(8,128)(2,1)} %doppler_forward.2.refs_0_), slice={[0:4], [0:8], [0:2], [0:128], [0:128]} | slice | bytes 4194304 | tf_op jit(solution)/shard_map/slice | solution.py:420
  181.5 2.5 collective-permute-start
  184.1 0.0 copy-done
  184.1 0.1 constant_dynamic-slice_fusion
  184.2 0.7 copy.27
  184.9 0.0 copy-done.2
  184.9 0.1 multiply_bitcast_fusion
  185.0 0.8 copy.28
  185.8 0.0 copy-done.3
  185.8 0.6 dynamic_slice.6.kappa_ref
  186.4 16.5 %doppler_forward.3.refs_1_ = bf16[4,16,2,128,128]{4,3,2,1,0:T(8,128)(2,1)} custom-call(bf16[32,4,2,32,256]{4,3,2,1,0:T(8,128)(2,1)} %bitcast.3.refs_0_, bf16[32,4,2,32,256]{4,3,2,1,0:T(8,128)(2,1)} %bitcast.19, bf16[256,256]{1,0:T(8,128)(2,1)} %constant.45.clone.refs_2_, f32[128,128]{1,0:T(8,128)} %constant.46.clone.refs_3_.refs_6_, ...), custom_call_target="tpu_custom_call" | custom-call | tf_op jit(solution)/shard_map/doppler_forward/pallas_call | solution.py:238
  203.0 6.1 %collective-permute-done.refs_2_ = bf16[4,8,2,128,128]{4,3,2,1,0:T(8,128)(2,1)S(1)} collective-permute-done((bf16[4,8,2,128,128]{4,3,2,1,0:T(8,128)(2,1)}, bf16[4,8,2,128,128]{4,3,2,1,0:T(8,128)(2,1)S(1)}, u32[]{:S(2)}, u32[]{:S(2)}) %collective-permute-start) | collective-permute-done | bytes 2097184 | tf_op jit(solution)/shard_map/ppermute | solution.py:420
  209.1 0.0 copy-start.1
  209.1 1.3 copy-done.1
  210.4 27.0 %image_rows.1 = bf16[4,2,32,4096]{3,2,1,0:T(8,128)(2,1)} custom-call(f32[32]{0:T(128)} %dynamic_slice.6.kappa_ref, bf16[4,16,2,128,128]{4,3,2,1,0:T(8,128)(2,1)} %doppler_forward.2.refs_0_, bf16[4,16,2,128,128]{4,3,2,1,0:T(8,128)(2,1)} %doppler_forward.3.refs_1_, bf16[4,8,2,128,128]{4,3,2,1,0:T(8,128)(2,1)} %copy-done.1, s32[128,128]{1,0:T(8,128)} %bitcast.25, ...), custom_call_target="tpu_custom_call" | custom-call | tf_op jit(solution)/shard_map/image_rows/pallas_call | solution.py:368
  237.4 31.0 %all_to_all.26 = bf16[4,2,32,4096]{3,2,1,0:T(8,128)(2,1)S(1)} all-to-all(bf16[4,2,32,4096]{3,2,1,0:T(8,128)(2,1)} %image_rows.1), channel_id=1, replica_groups=mesh['sub'=4,'pul'=32] {'sub'}, dimensions={0} | all-to-all | bytes 4194304 | tf_op jit(solution)/shard_map/all_to_all | solution.py:423
  268.5 1.5 copy.29
  (1 shorter events, 0.0 us)
Async XLA Ops:
  0.0 184.1 %copy-start = (s32[4,16384]{1,0:T(4,128)S(1)}, s32[4,16384]{1,0:T(4,128)}, u32[]{:S(2)}) copy-start(s32[4,16384]{1,0:T(4,128)} %param.28) | copy-start | bytes 786436
  1.1 3.4 %copy-start.4 = (bf16[64,128,128]{2,1,0:T(8,128)(2,1)S(1)}, bf16[64,128,128]{2,1,0:T(8,128)(2,1)}, u32[]{:S(2)}) copy-start(bf16[64,128,128]{2,1,0:T(8,128)(2,1)} %constant.42.clone) | copy-start | bytes 6291460
  38.2 63.7 %all-to-all-start = ((bf16[128,2,32,256]{3,2,1,0:T(8,128)(2,1)}), bf16[128,2,32,256]{3,2,1,0:T(8,128)(2,1)}, u32[]{:S(2)}, u32[]{:S(2)}) async-start(bf16[128,2,32,256]{3,2,1,0:T(8,128)(2,1)} %range_compress.2), calls=%async_computation | async-start | bytes 8388608 | tf_op jit(solution)/shard_map/all_to_all | solution.py:410
  178.3 6.6 %copy-start.2 = (f32[4,16384]{1,0:T(4,128)S(1)}, f32[4,16384]{1,0:T(4,128)}, u32[]{:S(2)}) copy-start(f32[4,16384]{1,0:T(4,128)} %param.27) | copy-start | bytes 786436
  178.3 7.5 %copy-start.3 = (f32[128]{0:T(128)S(1)}, f32[128]{0:T(128)}, u32[]{:S(2)}) copy-start(f32[128]{0:T(128)} %param.26) | copy-start | bytes 1540
  181.5 27.6 %collective-permute-start = (bf16[4,8,2,128,128]{4,3,2,1,0:T(8,128)(2,1)}, bf16[4,8,2,128,128]{4,3,2,1,0:T(8,128)(2,1)S(1)}, u32[]{:S(2)}, u32[]{:S(2)}) collective-permute-start(bf16[4,8,2,128,128]{4,3,2,1,0:T(8,128)(2,1)} %slice.4), channel_id=1, source_target_pairs={{32,0},{64,32},{96,64},{1,96},{33,1},{65,33},{97,65},{2,97},{34,2}... | collective-permute-start | bytes 6291464 | tf_op jit(solution)/shard_map/ppermute | solution.py:420
  209.1 1.3 copy-start.1

commit v2 on v1

v2 whole, which is shorter than its diff:
```python
import functools
import math

import jax
import jax.numpy as jnp
import numpy as np
from jax import lax
from jax.experimental import pallas as pl
from jax.experimental.pallas import tpu as pltpu
from jax.sharding import PartitionSpec as P

MAXS = 8
RBLK = 32
LANES = 128
CHUNKS = 2
UNROLL = 8
VMEM = 56 * 1024 * 1024
F32 = jnp.float32
BF16 = jnp.bfloat16


def realified(table):
    return np.block([[table.real, -table.imag], [table.imag, table.real]])


def unit_table(rows, cols, length, direction):
    product = np.outer(np.asarray(rows), np.asarray(cols)) % length
    return np.exp(direction * 2j * np.pi * product / length)


def as_bf16(table):
    return np.asarray(table, np.float32).astype(BF16)


def range_middle(range_phase, size):
    length = size * size
    k2 = np.arange(size)[:, None, None]
    j1 = np.arange(size)[None, :, None]
    k1 = np.arange(size)[None, None, :]
    wave = np.exp(2j * np.pi * ((j1 * (k2 + size * k1)) % length) / length) / size
    wave_r, wave_i = wave.real.astype(np.float32), wave.imag.astype(np.float32)
    right = np.concatenate(
        [
            np.concatenate([wave_r, -wave_i], axis=2),
            np.concatenate([wave_i, wave_r], axis=2),
        ],
        axis=1,
    )
    phase = range_phase.reshape(size, size).T
    cosine, sine = jnp.cos(phase)[:, None, :], jnp.sin(phase)[:, None, :]
    left_r = wave_r * cosine - wave_i * sine
    left_i = wave_r * sine + wave_i * cosine
    left = jnp.concatenate(
        [
            jnp.concatenate([left_r, -left_i], axis=2),
            jnp.concatenate([left_i, left_r], axis=2),
        ],
        axis=1,
    ).astype(BF16)
    middle = jnp.einsum("kae,kbe->kab", left, as_bf16(right), preferred_element_type=F32)
    return middle.astype(BF16)


def range_kernel(size, splits, x_ref, w_ref, t_ref, v_ref, *refs):
    outs, (one, two) = refs[:splits], refs[splits:]
    halves = x_ref.shape[2] // LANES
    both = 2 * size
    pitch = size + 1

    def lanes(h):
        return slice(h * LANES, (h + 1) * LANES)

    def cast(step, carry):
        for u in range(4):
            line = step * 4 + u
            for h in range(halves):
                for c in range(2):
                    one[h, pl.ds((c * size + line) * pitch, size), :] = x_ref[
                        c, pl.ds(pl.multiple_of(line * size, size), size), lanes(h)
                    ].astype(F32)
        return carry

    lax.fori_loop(0, size // 4, cast, 0)

    def strided(source, target, table):
        def body(step, carry):
            for u in range(UNROLL):
                j1 = step * UNROLL + u
                value = jnp.concatenate(
                    [source[h, pl.ds(j1, both, stride=pitch), :] for h in range(halves)], axis=1
                ).astype(BF16)
                out = jnp.dot(table, value, preferred_element_type=F32)
                for h in range(halves):
                    target[h, pl.ds(j1, both, stride=pitch), :] = out[:, lanes(h)]
            return carry

        lax.fori_loop(0, size // UNROLL, body, 0)

    strided(one, two, w_ref[...])

    def inner(step, carry):
        for u in range(UNROLL):
            k2 = step * UNROLL + u
            value = jnp.concatenate(
                [
                    jnp.concatenate(
                        [two[h, pl.ds((c * size + k2) * pitch, size), :] for c in range(2)], axis=0
                    )
                    for h in range(halves)
                ],
                axis=1,
            ).astype(BF16)
            out = jnp.dot(t_ref[k2], value, preferred_element_type=F32)
            for h in range(halves):
                for d in range(2):
                    one[h, pl.ds((d * size + k2) * pitch, size), :] = out[
                        d * size : (d + 1) * size, lanes(h)
                    ]
        return carry

    lax.fori_loop(0, size // UNROLL, inner, 0)
    strided(one, two, v_ref[...])
    rows = outs[0].shape[2]
    pieces = size // rows

    def give(step, carry):
        for u in range(4):
            line = step * 4 + u
            for piece in range(pieces):
                block = line * (pieces // splits) + piece // splits
                for d in range(2):
                    for h in range(halves):
                        outs[piece % splits][block, d, :, lanes(h)] = two[
                            h, pl.ds((d * size + line) * pitch + piece * rows, rows), :
                        ].astype(BF16)
        return carry

    lax.fori_loop(0, size // 4, give, 0)


def range_compress(echo, middle, chunk, width, blocks, splits):
    length = echo.shape[1]
    size = math.isqrt(length)
    index = np.arange(size)
    forward = as_bf16(realified(unit_table(index, index, size, -1)))
    backward = as_bf16(realified(unit_table(index, index, size, 1)))
    rows = length // blocks // splits
    whole = lambda *shape: pl.BlockSpec(shape, lambda i: (0,) * len(shape))
    scratch = pltpu.VMEM((width // LANES, 2 * (length + size), LANES), F32)
    return pl.pallas_call(
        functools.partial(range_kernel, size, splits),
        grid=(1,),
        in_specs=[
            pl.BlockSpec((2, length, width), lambda i: (0, 0, chunk)),
            whole(2 * size, 2 * size),
            whole(size, 2 * size, 2 * size),
            whole(2 * size, 2 * size),
        ],
        out_specs=[whole(blocks, 2, rows, width)] * splits,
        out_shape=[jax.ShapeDtypeStruct((blocks, 2, rows, width), BF16)] * splits,
        scratch_shapes=[scratch, scratch],
        compiler_params=pltpu.CompilerParams(vmem_limit_bytes=VMEM),
        name="range_compress",
    )(echo, forward, middle, backward)


def doppler_kernel(rows, *refs):
    parts = refs[:CHUNKS]
    w_ref, cos_ref, sin_ref, u_ref, o_ref, held = refs[CHUNKS:]
    sources = parts[0].shape[0]
    halves = parts[0].shape[4] // LANES
    size = cos_ref.shape[0]
    pitch = rows + 1

    def cast(source, carry):
        for q in range(CHUNKS):
            for c in range(2):
                for h in range(halves):
                    base = ((c * CHUNKS + q) * halves + h) * sources
                    held[pl.ds((base + source) * pitch, rows), :] = parts[q][
                        source, 0, c, :, h * LANES : (h + 1) * LANES
                    ].astype(F32)
        return carry

    lax.fori_loop(0, sources, cast, 0)

    def pair(first_row):
        value = jnp.concatenate(
            [held[pl.ds(first_row + i, 2 * size, stride=pitch), :] for i in range(2)], axis=1
        ).astype(BF16)
        first = jnp.dot(w_ref[...], value, preferred_element_type=F32)
        stacked = []
        for i in range(2):
            real = first[:size, i * LANES : (i + 1) * LANES]
            imag = first[size:, i * LANES : (i + 1) * LANES]
            stacked.append(
                jnp.concatenate(
                    [
                        real * cos_ref[...] - imag * sin_ref[...],
                        real * sin_ref[...] + imag * cos_ref[...],
                    ],
                    axis=1,
                ).astype(BF16)
            )
        second = jnp.dot(
            jnp.concatenate(stacked, axis=0), u_ref[...], preferred_element_type=F32
        ).astype(BF16)
        for i in range(2):
            for d in range(2):
                o_ref[0, first_row + i, d] = second[
                    i * size : (i + 1) * size, d * LANES : (d + 1) * LANES
                ]

    def body(step, carry):
        for u in range(4):
            pair(step * 8 + 2 * u)
        return carry

    lax.fori_loop(0, rows // 8, body, 0)


def doppler_tables(size, direction):
    index = np.arange(size)
    table = unit_table(index, index, size, direction)
    turn = unit_table(index, index, size * size, direction) / size
    return table, turn.real.astype(np.float32), turn.imag.astype(np.float32)


def doppler_forward(parts, places, rows, size):
    sources, subs, _, _, width = parts[0].shape
    halves = width // LANES
    table, turn_cos, turn_sin = doppler_tables(size, -1)
    per_source = size // sources
    order = np.asarray(
        [
            per_source * source + q * halves + h
            for q in range(CHUNKS)
            for h in range(halves)
            for source in range(sources)
        ]
    )
    outer = as_bf16(realified(table[:, order]))
    inner = as_bf16(realified(table).T)
    whole = lambda *shape: pl.BlockSpec(shape, lambda i: (0,) * len(shape))
    pieces = [
        pl.BlockSpec(
            (sources, 1, 2, rows, width), functools.partial(lambda at, i: (0, i, 0, at, 0), at)
        )
        for at in places
    ]
    return pl.pallas_call(
        functools.partial(doppler_kernel, rows),
        grid=(subs,),
        in_specs=pieces
        + [
            whole(2 * size, 2 * size),
            whole(size, size),
            whole(size, size),
            whole(2 * size, 2 * size),
        ],
        out_specs=pl.BlockSpec((1, rows, 2, size, size), lambda i: (i, 0, 0, 0, 0)),
        out_shape=jax.ShapeDtypeStruct((subs, rows, 2, size, size), BF16),
        scratch_shapes=[pltpu.VMEM((2 * size * (rows + 1), LANES), F32)],
        compiler_params=pltpu.CompilerParams(vmem_limit_bytes=VMEM),
        name="doppler_forward",
    )(*parts, outer, turn_cos, turn_sin, inner)


def turn_polynomials():
    nodes = 0.25 * (1 - np.cos((np.arange(64) + 0.5) * np.pi / 64)) / 2
    roots = np.sqrt(nodes)
    sine = np.polynomial.polynomial.polyfit(nodes, np.sin(2 * np.pi * roots) / roots, 6)
    cosine = np.polynomial.polynomial.polyfit(nodes, np.cos(2 * np.pi * roots), 6)
    return [round(float(v), 7) for v in sine], [round(float(v), 7) for v in cosine]


def turns(cycles):
    sine_terms, cosine_terms = turn_polynomials()
    part = cycles - jnp.floor(cycles + 0.5)
    square = part * part
    sine = jnp.full_like(square, sine_terms[-1])
    cosine = jnp.full_like(square, cosine_terms[-1])
    for term in reversed(sine_terms[:-1]):
        sine = sine * square + term
    for term in reversed(cosine_terms[:-1]):
        cosine = cosine * square + term
    return cosine, sine * part


def factor_kernel(kappa_ref, phase_ref, o_ref):
    def body(step, carry):
        for u in range(2):
            row = step * 2 + u
            cosine, sine = turns(kappa_ref[row] * phase_ref[0])
            o_ref[0, row, 0] = cosine.astype(BF16)
            o_ref[0, row, 1] = sine.astype(BF16)
        return carry

    lax.fori_loop(0, o_ref.shape[1] // 2, body, 0)


def azimuth_factors(kappa, phase):
    subs, size, _ = phase.shape
    rows = kappa.shape[0]
    return pl.pallas_call(
        factor_kernel,
        grid=(subs,),
        in_specs=[
            pl.BlockSpec(memory_space=pltpu.SMEM),
            pl.BlockSpec((1, size, size), lambda i: (i, 0, 0)),
        ],
        out_specs=pl.BlockSpec((1, rows, 2, size, size), lambda i: (i, 0, 0, 0, 0)),
        out_shape=jax.ShapeDtypeStruct((subs, rows, 2, size, size), BF16),
        compiler_params=pltpu.CompilerParams(vmem_limit_bytes=VMEM),
        name="azimuth_factors",
    )(kappa, phase)


def image_kernel(own, rim, factor_ref, shift_ref, w_ref, cos_ref, sin_ref, u_ref, *refs):
    o_ref, moved, summed, middle, turned = refs
    step = pl.program_id(0)
    subs, rows, _, tile, size = own.shape
    shift = shift_ref[...]
    bits = [((shift >> k) & 1).astype(F32).astype(BF16) > 0.5 for k in range(4)]

    def aperture(index, carry):
        for d in range(2):
            values = [own[index, r, d] for r in range(rows)]
            values += [rim[index, r, d] for r in range(MAXS)]
            four = [jnp.where(bits[2], values[r + 4], values[r]) for r in range(rows + 3)]
            two = [jnp.where(bits[1], four[r + 2], four[r]) for r in range(rows + 1)]
            one = [jnp.where(bits[0], two[r + 1], two[r]) for r in range(rows)]
            for r in range(rows):
                moved[index, d, r] = jnp.where(bits[3], values[r + 8], one[r])
        return carry

    lax.fori_loop(0, subs, aperture, 0)

    def row_sum(turn, carry):
        for u in range(4):
            row = turn * 4 + u
            real = jnp.zeros((tile, size), F32)
            imag = jnp.zeros((tile, size), F32)
            for index in range(subs):
                cosine = factor_ref[index, row, 0].astype(F32)
                sine = factor_ref[index, row, 1].astype(F32)
                a, b = moved[index, 0, row].astype(F32), moved[index, 1, row].astype(F32)
                real = real + (a * cosine - b * sine)
                imag = imag + (a * sine + b * cosine)
            summed[pl.ds(pl.multiple_of(row * tile, tile), tile), :] = jnp.concatenate(
                [real, imag], axis=1
            ).astype(BF16)
        return carry

    lax.fori_loop(0, rows // 4, row_sum, 0)
    first = jnp.dot(summed[...], u_ref[...], preferred_element_type=F32)
    where = pl.ds(pl.multiple_of(step * tile, tile), tile)
    for r in range(rows):
        real = first[r * tile : (r + 1) * tile, :size]
        imag = first[r * tile : (r + 1) * tile, size:]
        middle[r, 0, where, :] = (real * cos_ref[...] - imag * sin_ref[...]).astype(BF16)
        middle[r, 1, where, :] = (real * sin_ref[...] + imag * cos_ref[...]).astype(BF16)

    @pl.when(step == pl.num_programs(0) - 1)
    def _():
        pitch = rows + 1

        def body(turn, carry):
            for u in range(4):
                pair = turn * 4 + u
                value = jnp.concatenate(
                    [
                        jnp.concatenate([middle[pair * 2 + i, c] for c in range(2)], axis=0)
                        for i in range(2)
                    ],
                    axis=1,
                )
                out = jnp.dot(w_ref[...], value, preferred_element_type=F32)
                for i in range(2):
                    turned[pl.ds(pair * 2 + i, 2 * size, stride=pitch), :] = out[
                        :, i * LANES : (i + 1) * LANES
                    ]
            return carry

        lax.fori_loop(0, rows // 8, body, 0)
        groups = o_ref.shape[0]
        per_group = size // groups

        def give(group, carry):
            for d in range(2):
                for j in range(per_group):
                    line = (d * size + group * per_group + j) * pitch
                    o_ref[group, d, :, j * LANES : (j + 1) * LANES] = turned[
                        pl.ds(line, rows), :
                    ].astype(BF16)
            return carry

        lax.fori_loop(0, groups, give, 0)


def image_rows(own, rim, factors, part, shift, groups):
    subs, rows, _, size, _ = own.shape
    tile = 16
    table, turn_cos, turn_sin = doppler_tables(size, 1)
    outer = as_bf16(realified(table))
    inner = as_bf16(realified(table).T)
    whole = lambda *shape: pl.BlockSpec(shape, lambda i: (0,) * len(shape))
    lines = pl.BlockSpec((tile, size), lambda i: (i, 0))
    width = size * size // groups
    return pl.pallas_call(
        image_kernel,
        grid=(size // tile,),
        in_specs=[
            pl.BlockSpec((subs, rows, 2, tile, size), lambda i: (0, 0, 0, i, 0)),
            pl.BlockSpec((subs, MAXS, 2, tile, size), lambda i: (0, 0, 0, i, 0)),
            pl.BlockSpec((subs, rows, 2, tile, size), lambda i: (0, part, 0, i, 0)),
            lines,
            whole(2 * size, 2 * size),
            lines,
            lines,
            whole(2 * size, 2 * size),
        ],
        out_specs=whole(groups, 2, rows, width),
        out_shape=jax.ShapeDtypeStruct((groups, 2, rows, width), BF16),
        scratch_shapes=[
            pltpu.VMEM((subs, 2, rows, tile, size), BF16),
            pltpu.VMEM((rows * tile, 2 * size), BF16),
            pltpu.VMEM((rows, 2, size, size), BF16),
            pltpu.VMEM((2 * size * (rows + 1), LANES), F32),
        ],
        compiler_params=pltpu.CompilerParams(vmem_limit_bytes=VMEM),
        name="image_rows",
    )(own, rim, factors, shift, outer, turn_cos, turn_sin, inner)


def on_device(raw_echo, range_phase, kappa, doppler, migration):
    _, _, range_len, pulse_dev = raw_echo.shape
    puls, subs = lax.axis_size("pul"), lax.axis_size("sub")
    blocks = puls * subs
    rows = range_len // blocks
    half = rows // 2
    pulse_len = pulse_dev * puls
    size = math.isqrt(pulse_len)
    sub_index = lax.axis_index("sub")
    middle = range_middle(range_phase, math.isqrt(range_len))
    echo = raw_echo.reshape(2, range_len, pulse_dev)
    width = pulse_dev // CHUNKS

    def spread(sent):
        got = lax.all_to_all(sent, ("pul", "sub"), 0, 0, tiled=True)
        return got.reshape(puls, subs, 2, sent.shape[2], width)

    (sent,) = range_compress(echo, middle, 0, width, blocks, 1)
    sent, echo = lax.optimization_barrier((sent, echo))
    every = spread(sent)
    sent_low, sent_high = range_compress(echo, middle, 1, width, blocks, 2)
    own_shift = lax.dynamic_slice_in_dim(migration, sub_index, 1, 0)
    shift = own_shift.reshape(size, size).T
    phase = jnp.swapaxes(doppler.reshape(subs, size, size), 1, 2) * (0.5 / math.pi)
    own_kappa = lax.dynamic_slice_in_dim(kappa, sub_index * rows, rows, 0)
    factors = azimuth_factors(own_kappa, phase)
    every, sent_low, factors = lax.optimization_barrier((every, sent_low, factors))
    got_low = spread(sent_low)
    got_low, sent_high = lax.optimization_barrier((got_low, sent_high))
    low = doppler_forward([every, got_low], [0, 0], half, size)
    place = lambda block: (block % subs) * puls + block // subs
    pairs = [(place(block), place(block - 1)) for block in range(1, blocks)]
    rim = lax.ppermute(low[:, :MAXS], ("sub", "pul"), pairs)
    high = doppler_forward([every, spread(sent_high)], [1, 0], half, size)
    upper = lax.all_to_all(
        image_rows(low, high, factors, 0, shift, subs), "sub", 0, 0, tiled=True
    )
    lower = lax.all_to_all(
        image_rows(high, rim, factors, 1, shift, subs), "sub", 0, 0, tiled=True
    )
    image = jnp.stack([upper, lower], axis=2)
    return jnp.swapaxes(image, 0, 1).reshape(2, rows * subs, pulse_len // subs)


def solution(mesh):
    placed = (P(None, "sub", None, "pul"), P(), P("pul"), P(), P("pul", None))
    return jax.shard_map(
        on_device, mesh=mesh, in_specs=placed, out_specs=P(None, "pul", "sub"), check_vma=False
    )
```

time: 270 us -> 216 us (0.80); the launches traced: 270 us -> 213 us
  Pallas kernels: 122 us -> 74.6 us
  blocking collectives: 90.9 us -> 53.2 us
  waiting for transfers between devices: 27.7 us -> 44 us
  starting transfers between devices: 13.8 us -> 25.1 us
    all_to_all x2, blocking collectives: 90.9 us -> 53.2 us  [the longest x1 35.4 us: spread(): got = lax.all_to_all(sent, ('pul', 'sub'), 0, 0, tiled=True)]
    pallas_call x2 -> x3, Pallas kernels: 61.7 us -> 37.5 us  [the longest x2 26 us: range_compress(): pl.pallas_call(functools.partial(range_kernel, size, splits), grid=(1,),...]
    all_to_all x1 -> x3, waiting for transfers between devices: 21.6 us -> 44 us  [the longest x2 40.7 us: spread(): got = lax.all_to_all(sent, ('pul', 'sub'), 0, 0, tiled=True)]
    pallas_call x2, Pallas kernels: 33.1 us -> 16.4 us  [doppler_forward(): pl.pallas_call(functools.partial(doppler_kernel, rows), grid=(subs,), in_...]
    all_to_all x1 -> x3, starting transfers between devices: 11.2 us -> 22.9 us  [the longest x2 18.3 us: spread(): got = lax.all_to_all(sent, ('pul', 'sub'), 0, 0, tiled=True)]
    pallas_call x1 -> x2, Pallas kernels: 27 us -> 20.7 us  [image_rows(): pl.pallas_call(image_kernel, grid=(size // tile,), in_specs=[pl.BlockSpec...]
    ppermute x1, waiting for transfers between devices: 6.12 us -> 0.01 us  [on_device(): rim = lax.ppermute(low[:, :MAXS], ('sub', 'pul'), pairs)]
  transfers between devices with their start and end apart: 2 -> 4, of which waited for: 2 -> 3; matrix products, arithmetic and copies ran while one was open for 1% -> 3% of each run, Pallas kernels for 18% -> 29%
where the time goes in v2:
time: 216 us; the launch traced here: 213 us
  Pallas kernels  74.6 us (35%)
  blocking collectives  53.2 us (25%)
  waiting for transfers between devices  44 us (20%)
  starting transfers between devices  25.1 us (12%)
  local copies, waits for them, and re-layouts  9.42 us (4%)
  other arithmetic  3.58 us (2%)
  matrix products  2.83 us (1%)
    all_to_all x2, waiting for transfers between devices, spread(): got = lax.all_to_all(sent, ('pul', 'sub'), 0, 0, tiled=True)  40.7 us
    all_to_all x1, blocking collectives, spread(): got = lax.all_to_all(sent, ('pul', 'sub'), 0, 0, tiled=True)  35.4 us
    pallas_call x2, Pallas kernels, range_compress(): pl.pallas_call(functools.partial(range_kernel, size, splits), grid=(1,),...  26 us
    pallas_call x2, Pallas kernels, image_rows(): pl.pallas_call(image_kernel, grid=(size // tile,), in_specs=[pl.BlockSpec...  20.7 us
    all_to_all x2, starting transfers between devices, spread(): got = lax.all_to_all(sent, ('pul', 'sub'), 0, 0, tiled=True)  18.3 us
    all_to_all x1, blocking collectives, on_device(): lax.all_to_all(image_rows(high, rim, factors, 1, shift, subs), 'sub', 0,...  17.8 us
    pallas_call x2, Pallas kernels, doppler_forward(): pl.pallas_call(functools.partial(doppler_kernel, rows), grid=(subs,), in_...  16.4 us
    pallas_call x1, Pallas kernels, azimuth_factors(): pl.pallas_call(factor_kernel, grid=(subs,), in_specs=[pl.BlockSpec(memory...  11.5 us
  transfers between devices with their start and end apart: 4, of which 3 were waited for; matrix products, arithmetic and copies ran while one was open for 3% of the time, Pallas kernels for 29%

profile of v2, /device:TPU:7, one launch (start us, length us, event | category | flops | bytes accessed | tf_op | source)
XLA Modules:
  0.0 212.8 jit_solution(4871924846126960160)
XLA Ops:
  0.0 0.0 copy-start
  0.0 0.8 fusion.13
  0.8 0.1 cos.10
  0.9 0.1 copy.29
  1.0 0.1 sin.10
  1.1 0.1 copy.30
  1.1 0.0 copy-start.5
  1.2 3.3 %negate_convert_fusion = (bf16[64,64,64]{2,1,0:T(8,128)(2,1)S(1)}, bf16[64,64,64]{2,1,0:T(8,128)(2,1)S(1)}, bf16[64,64,64]{2,1,0:T(8,128)(2,1)S(1)}) fusion(f32[64,64,64]{2,1,0:T(8,128)} %constant.41.clone, f32[64,64,64]{2,1,0:T(8,128)} %constant.40.clone, f32[64,64]{1,0:T(8,128)S(1)} %copy.30, f32[64,64]{1,0:T(8,128)S(1)} %copy.29), kind=kLoop, calls=%fused_computation.9 | loop fusion | flops 2621440 | bytes 3702784 | tf_op jit(solution)/shard_map/convert.5
  4.5 0.0 copy-done.5
  4.5 2.8 %fusion.9.t_ref = bf16[64,128,128]{2,1,0:T(8,128)(2,1)} fusion(bf16[64,128,128]{2,1,0:T(8,128)(2,1)S(1)} %copy-done.5, bf16[64,64,64]{2,1,0:T(8,128)(2,1)S(1)} %get-tuple-element.25, bf16[64,64,64]{2,1,0:T(8,128)(2,1)S(1)} %get-tuple-element.24, bf16[64,64,64]{2,1,0:T(8,128)(2,1)S(1)} %get-tuple-element.23), kind=kOutput, calls=%fused_computation.13 | convolution fusion | flops 277872640 | bytes 5767168 | tf_op jit(solution)/shard_map/kae,kbe->kab/dot_general | solution.py:60
  7.3 13.0 %range_compress.2 = bf16[128,2,32,256]{3,2,1,0:T(8,128)(2,1)} custom-call(bf16[2,4096,512]{2,1,0:T(8,128)(2,1)} %bitcast.20, bf16[128,128]{1,0:T(8,128)(2,1)} %constant.43.clone.w_ref, bf16[64,128,128]{2,1,0:T(8,128)(2,1)} %fusion.9.t_ref, bf16[128,128]{1,0:T(8,128)(2,1)} %constant.44.clone.v_ref), custom_call_target="tpu_custom_call" | custom-call | tf_op jit(solution)/shard_map/range_compress/pallas_call | solution.py:150
  20.3 11.2 %all-to-all-start = ((bf16[128,2,32,256]{3,2,1,0:T(8,128)(2,1)}), bf16[128,2,32,256]{3,2,1,0:T(8,128)(2,1)}, u32[]{:S(2)}, u32[]{:S(2)}) async-start(bf16[128,2,32,256]{3,2,1,0:T(8,128)(2,1)} %range_compress.2), calls=%async_computation | async-start | bytes 8388608 | tf_op jit(solution)/shard_map/all_to_all | solution.py:450
  31.5 0.0 copy-start.3
  31.6 0.0 copy-start.4
  31.6 13.0 %range_compress.3 = (bf16[128,2,16,256]{3,2,1,0:T(8,128)(2,1)}, bf16[128,2,16,256]{3,2,1,0:T(8,128)(2,1)}) custom-call(bf16[2,4096,512]{2,1,0:T(8,128)(2,1)} %bitcast.21, bf16[128,128]{1,0:T(8,128)(2,1)} %constant.43.clone.w_ref, bf16[64,128,128]{2,1,0:T(8,128)(2,1)} %fusion.9.t_ref, bf16[128,128]{1,0:T(8,128)(2,1)} %constant.44.clone.v_ref), custom_call_target="tpu_custom_call" | custom-call | tf_op jit(solution)/shard_map/range_compress/pallas_call | solution.py:150
  44.6 0.0 copy-done.3
  44.6 0.1 multiply_bitcast_fusion
  44.7 0.8 copy.31
  45.6 0.0 copy-done.4
  45.6 0.7 dynamic_slice.6.kappa_ref
  46.2 0.0 copy-start.2
  46.2 11.5 %azimuth_factors.1.factor_ref = bf16[4,32,2,128,128]{4,3,2,1,0:T(8,128)(2,1)} custom-call(f32[32]{0:T(128)} %dynamic_slice.6.kappa_ref, f32[4,128,128]{2,1,0:T(8,128)} %bitcast.26), custom_call_target="tpu_custom_call" | custom-call | tf_op jit(solution)/shard_map/azimuth_factors/pallas_call | solution.py:305
  57.7 26.2 %all-to-all-done = bf16[128,2,32,256]{3,2,1,0:T(8,128)(2,1)} async-done(((bf16[128,2,32,256]{3,2,1,0:T(8,128)(2,1)}), bf16[128,2,32,256]{3,2,1,0:T(8,128)(2,1)}, u32[]{:S(2)}, u32[]{:S(2)}) %all-to-all-start) | async-done | bytes 4194336 | tf_op jit(solution)/shard_map/all_to_all | solution.py:450
  84.0 0.0 copy-done.2
  84.0 35.4 %all_to_all.25 = bf16[128,2,16,256]{3,2,1,0:T(8,128)(2,1)} all-to-all(bf16[128,2,16,256]{3,2,1,0:T(8,128)(2,1)S(1)} %copy-done.2), channel_id=1, replica_groups=mesh['sub'=4,'pul'=32] {'pul','sub'}, dimensions={0} | all-to-all | bytes 4194304 | tf_op jit(solution)/shard_map/all_to_all | solution.py:450
  119.4 7.0 %all-to-all-start.2 = ((bf16[128,2,16,256]{3,2,1,0:T(8,128)(2,1)}), bf16[128,2,16,256]{3,2,1,0:T(8,128)(2,1)S(1)}, u32[]{:S(2)}, u32[]{:S(2)}) async-start(bf16[128,2,16,256]{3,2,1,0:T(8,128)(2,1)} %get-tuple-element.21), calls=%async_computation.2 | async-start | bytes 4194304 | tf_op jit(solution)/shard_map/all_to_all | solution.py:450
  126.4 8.2 %doppler_forward.2.own = bf16[4,16,2,128,128]{4,3,2,1,0:T(8,128)(2,1)} custom-call(bf16[32,4,2,32,256]{4,3,2,1,0:T(8,128)(2,1)} %bitcast.3.refs_0_, bf16[32,4,2,16,256]{4,3,2,1,0:T(8,128)(2,1)} %bitcast.23, bf16[256,256]{1,0:T(8,128)(2,1)} %constant.45.clone.refs_2_, f32[128,128]{1,0:T(8,128)} %constant.46.clone.refs_3_.cos_ref, ...), custom_call_target="tpu_custom_call" | custom-call | tf_op jit(solution)/shard_map/doppler_forward/pallas_call | solution.py:251
  134.6 3.2 %slice.4 = bf16[4,8,2,128,128]{4,3,2,1,0:T(8,128)(2,1)} slice(bf16[4,16,2,128,128]{4,3,2,1,0:T(8,128)(2,1)} %doppler_forward.2.own), slice={[0:4], [0:8], [0:2], [0:128], [0:128]} | slice | bytes 4194304 | tf_op jit(solution)/shard_map/slice | solution.py:468
  137.8 2.3 %collective-permute-start = (bf16[4,8,2,128,128]{4,3,2,1,0:T(8,128)(2,1)}, bf16[4,8,2,128,128]{4,3,2,1,0:T(8,128)(2,1)}, u32[]{:S(2)}, u32[]{:S(2)}) collective-permute-start(bf16[4,8,2,128,128]{4,3,2,1,0:T(8,128)(2,1)} %slice.4), channel_id=1, source_target_pairs={{32,0},{64,32},{96,64},{1,96},{33,1},{65,33},{97,65},{2,97},{34,2}... | collective-permute-start | bytes 6291464 | tf_op jit(solution)/shard_map/ppermute | solution.py:468
  140.1 0.0 copy-done
  140.1 0.1 constant_dynamic-slice_fusion
  140.2 0.7 copy.32
  140.9 14.4 %all-to-all-done.2 = bf16[128,2,16,256]{3,2,1,0:T(8,128)(2,1)S(1)} async-done(((bf16[128,2,16,256]{3,2,1,0:T(8,128)(2,1)}), bf16[128,2,16,256]{3,2,1,0:T(8,128)(2,1)S(1)}, u32[]{:S(2)}, u32[]{:S(2)}) %all-to-all-start.2) | async-done | bytes 2097184 | tf_op jit(solution)/shard_map/all_to_all | solution.py:450
  155.3 0.0 copy-start.1
  155.3 1.3 copy-done.1
  156.6 8.2 %doppler_forward.3.rim.own = bf16[4,16,2,128,128]{4,3,2,1,0:T(8,128)(2,1)} custom-call(bf16[32,4,2,32,256]{4,3,2,1,0:T(8,128)(2,1)} %bitcast.3.refs_0_, bf16[32,4,2,16,256]{4,3,2,1,0:T(8,128)(2,1)} %bitcast.22, bf16[256,256]{1,0:T(8,128)(2,1)} %constant.45.clone.refs_2_, f32[128,128]{1,0:T(8,128)} %constant.46.clone.refs_3_.cos_ref, ...), custom_call_target="tpu_custom_call" | custom-call | tf_op jit(solution)/shard_map/doppler_forward/pallas_call | solution.py:251
  164.8 10.4 %image_rows.2 = bf16[4,2,16,4096]{3,2,1,0:T(8,128)(2,1)} custom-call(bf16[4,16,2,128,128]{4,3,2,1,0:T(8,128)(2,1)} %doppler_forward.2.own, bf16[4,16,2,128,128]{4,3,2,1,0:T(8,128)(2,1)} %doppler_forward.3.rim.own, bf16[4,32,2,128,128]{4,3,2,1,0:T(8,128)(2,1)} %azimuth_factors.1.factor_ref, s32[128,128]{1,0:T(8,128)} %bitcast.28, ...), custom_call_target="tpu_custom_call" | custom-call | tf_op jit(solution)/shard_map/image_rows/pallas_call | solution.py:410
  175.2 4.6 %all-to-all-start.3 = ((bf16[4,2,16,4096]{3,2,1,0:T(8,128)(2,1)}), bf16[4,2,16,4096]{3,2,1,0:T(8,128)(2,1)S(1)}, u32[]{:S(2)}, u32[]{:S(2)}) async-start(bf16[4,2,16,4096]{3,2,1,0:T(8,128)(2,1)} %image_rows.2), calls=%async_computation.3 | async-start | bytes 2097152 | tf_op jit(solution)/shard_map/all_to_all | solution.py:470
  179.8 0.0 collective-permute-done.rim
  179.8 10.3 %image_rows.3 = bf16[4,2,16,4096]{3,2,1,0:T(8,128)(2,1)} custom-call(bf16[4,16,2,128,128]{4,3,2,1,0:T(8,128)(2,1)} %doppler_forward.3.rim.own, bf16[4,8,2,128,128]{4,3,2,1,0:T(8,128)(2,1)} %collective-permute-done.rim, bf16[4,32,2,128,128]{4,3,2,1,0:T(8,128)(2,1)} %azimuth_factors.1.factor_ref, s32[128,128]{1,0:T(8,128)} %bitcast.29, ...), custom_call_target="tpu_custom_call" | custom-call | tf_op jit(solution)/shard_map/image_rows/pallas_call | solution.py:410
  190.0 3.3 %all-to-all-done.3 = bf16[4,2,16,4096]{3,2,1,0:T(8,128)(2,1)S(1)} async-done(((bf16[4,2,16,4096]{3,2,1,0:T(8,128)(2,1)}), bf16[4,2,16,4096]{3,2,1,0:T(8,128)(2,1)S(1)}, u32[]{:S(2)}, u32[]{:S(2)}) %all-to-all-start.3) | async-done | bytes 1048608 | tf_op jit(solution)/shard_map/all_to_all | solution.py:470
  193.4 17.8 %all_to_all.26 = bf16[4,2,16,4096]{3,2,1,0:T(8,128)(2,1)S(1)} all-to-all(bf16[4,2,16,4096]{3,2,1,0:T(8,128)(2,1)} %image_rows.3), channel_id=1, replica_groups=mesh['sub'=4,'pul'=32] {'sub'}, dimensions={0} | all-to-all | bytes 2097152 | tf_op jit(solution)/shard_map/all_to_all | solution.py:473
  211.1 0.2 maximum_bitcast_fusion
  211.3 1.5 copy.33
  (1 shorter events, 0.0 us)
Async XLA Ops:
  0.0 140.1 %copy-start = (s32[4,16384]{1,0:T(4,128)S(1)}, s32[4,16384]{1,0:T(4,128)}, u32[]{:S(2)}) copy-start(s32[4,16384]{1,0:T(4,128)} %param.32) | copy-start | bytes 786436
  1.1 3.4 %copy-start.5 = (bf16[64,128,128]{2,1,0:T(8,128)(2,1)S(1)}, bf16[64,128,128]{2,1,0:T(8,128)(2,1)}, u32[]{:S(2)}) copy-start(bf16[64,128,128]{2,1,0:T(8,128)(2,1)} %constant.42.clone) | copy-start | bytes 6291460
  20.3 63.7 %all-to-all-start = ((bf16[128,2,32,256]{3,2,1,0:T(8,128)(2,1)}), bf16[128,2,32,256]{3,2,1,0:T(8,128)(2,1)}, u32[]{:S(2)}, u32[]{:S(2)}) async-start(bf16[128,2,32,256]{3,2,1,0:T(8,128)(2,1)} %range_compress.2), calls=%async_computation | async-start | bytes 8388608 | tf_op jit(solution)/shard_map/all_to_all | solution.py:450
  31.5 13.1 %copy-start.3 = (f32[4,16384]{1,0:T(4,128)S(1)}, f32[4,16384]{1,0:T(4,128)}, u32[]{:S(2)}) copy-start(f32[4,16384]{1,0:T(4,128)} %param.31) | copy-start | bytes 786436
  31.6 14.0 %copy-start.4 = (f32[128]{0:T(128)S(1)}, f32[128]{0:T(128)}, u32[]{:S(2)}) copy-start(f32[128]{0:T(128)} %param.30) | copy-start | bytes 1540
  46.2 37.8 %copy-start.2 = (bf16[128,2,16,256]{3,2,1,0:T(8,128)(2,1)S(1)}, bf16[128,2,16,256]{3,2,1,0:T(8,128)(2,1)}, u32[]{:S(2)}) copy-start(bf16[128,2,16,256]{3,2,1,0:T(8,128)(2,1)} %get-tuple-element.18) | copy-start | bytes 6291460
  119.4 35.9 %all-to-all-start.2 = ((bf16[128,2,16,256]{3,2,1,0:T(8,128)(2,1)}), bf16[128,2,16,256]{3,2,1,0:T(8,128)(2,1)S(1)}, u32[]{:S(2)}, u32[]{:S(2)}) async-start(bf16[128,2,16,256]{3,2,1,0:T(8,128)(2,1)} %get-tuple-element.21), calls=%async_computation.2 | async-start | bytes 4194304 | tf_op jit(solution)/shard_map/all_to_all | solution.py:450
  137.8 41.9 %collective-permute-start = (bf16[4,8,2,128,128]{4,3,2,1,0:T(8,128)(2,1)}, bf16[4,8,2,128,128]{4,3,2,1,0:T(8,128)(2,1)}, u32[]{:S(2)}, u32[]{:S(2)}) collective-permute-start(bf16[4,8,2,128,128]{4,3,2,1,0:T(8,128)(2,1)} %slice.4), channel_id=1, source_target_pairs={{32,0},{64,32},{96,64},{1,96},{33,1},{65,33},{97,65},{2,97},{34,2}... | collective-permute-start | bytes 6291464 | tf_op jit(solution)/shard_map/ppermute | solution.py:468
  155.3 1.3 copy-start.1
  175.2 18.2 %all-to-all-start.3 = ((bf16[4,2,16,4096]{3,2,1,0:T(8,128)(2,1)}), bf16[4,2,16,4096]{3,2,1,0:T(8,128)(2,1)S(1)}, u32[]{:S(2)}, u32[]{:S(2)}) async-start(bf16[4,2,16,4096]{3,2,1,0:T(8,128)(2,1)} %image_rows.2), calls=%async_computation.3 | async-start | bytes 2097152 | tf_op jit(solution)/shard_map/all_to_all | solution.py:470

commit v3 on v2

v3 whole, which is shorter than its diff:
```python
import functools
import math

import jax
import jax.numpy as jnp
import numpy as np
from jax import lax
from jax.experimental import pallas as pl
from jax.experimental.pallas import tpu as pltpu
from jax.sharding import PartitionSpec as P

MAXS = 8
RBLK = 32
LANES = 128
UNROLL = 4
VMEM = 56 * 1024 * 1024
F32 = jnp.float32
BF16 = jnp.bfloat16


def realified(table):
    return np.block([[table.real, -table.imag], [table.imag, table.real]])


def unit_table(rows, cols, length, direction):
    product = np.outer(np.asarray(rows), np.asarray(cols)) % length
    return np.exp(direction * 2j * np.pi * product / length)


def as_bf16(table):
    return np.asarray(table, np.float32).astype(BF16)


def middle_kernel(phase_ref, wave_ref, o_ref):
    cosine, sine = turns(phase_ref[...])
    size = phase_ref.shape[1] // 2
    lane = lax.broadcasted_iota(jnp.int32, sine.shape, 1)
    sine = jnp.where(lane < size, sine, -sine)
    for k2 in range(o_ref.shape[0]):
        wave = wave_ref[k2].astype(F32)
        left = wave * cosine[k2 : k2 + 1] + pltpu.roll(wave, size, 1) * sine[k2 : k2 + 1]
        o_ref[k2] = lax.dot_general(
            left.astype(BF16),
            wave_ref[k2],
            (((1,), (1,)), ((), ())),
            preferred_element_type=F32,
        ).astype(BF16)


def range_middle(range_phase, size):
    length = size * size
    k2 = np.arange(size)[:, None, None]
    j1 = np.arange(size)[None, :, None]
    k1 = np.arange(size)[None, None, :]
    wave = np.exp(2j * np.pi * ((j1 * (k2 + size * k1)) % length) / length) / size
    wave = as_bf16(np.stack([realified(wave[k]) for k in range(size)]))
    phase = range_phase.reshape(size, size).T * (0.5 / math.pi)
    group = 16
    block = pl.BlockSpec((group, 2 * size, 2 * size), lambda i: (i, 0, 0))
    return pl.pallas_call(
        middle_kernel,
        grid=(size // group,),
        in_specs=[pl.BlockSpec((group, 2 * size), lambda i: (i, 0)), block],
        out_specs=block,
        out_shape=jax.ShapeDtypeStruct(wave.shape, BF16),
        compiler_params=pltpu.CompilerParams(vmem_limit_bytes=VMEM),
        name="range_middle",
    )(jnp.concatenate([phase, phase], axis=1), wave)


def range_kernel(size, splits, x_ref, w_ref, t_ref, v_ref, *refs):
    outs, (one, two) = refs[:splits], refs[splits:]
    both = 2 * size
    pitch = size + 1

    def cast(step, carry):
        for u in range(8):
            line = step * 8 + u
            for c in range(2):
                one[pl.ds((c * size + line) * pitch, size), :] = x_ref[
                    c, pl.ds(pl.multiple_of(line * size, size), size), :
                ].astype(F32)
        return carry

    lax.fori_loop(0, size // 8, cast, 0)

    def strided(source, target, table):
        def body(step, carry):
            for u in range(UNROLL):
                j1 = (step * UNROLL + u) * 2
                value = jnp.concatenate(
                    [source[pl.ds(j1 + i, both, stride=pitch), :] for i in range(2)], axis=1
                ).astype(BF16)
                out = jnp.dot(table, value, preferred_element_type=F32)
                for i in range(2):
                    target[pl.ds(j1 + i, both, stride=pitch), :] = out[
                        :, i * LANES : (i + 1) * LANES
                    ]
            return carry

        lax.fori_loop(0, size // (2 * UNROLL), body, 0)

    strided(one, two, w_ref[...])

    def inner(step, carry):
        for u in range(2 * UNROLL):
            k2 = step * 2 * UNROLL + u
            value = jnp.concatenate(
                [two[pl.ds((c * size + k2) * pitch, size), :] for c in range(2)], axis=0
            ).astype(BF16)
            out = jnp.dot(t_ref[k2], value, preferred_element_type=F32)
            for d in range(2):
                one[pl.ds((d * size + k2) * pitch, size), :] = out[d * size : (d + 1) * size]
        return carry

    lax.fori_loop(0, size // (2 * UNROLL), inner, 0)
    strided(one, two, v_ref[...])
    rows = outs[0].shape[2]
    pieces = size // rows

    def give(step, carry):
        for u in range(8):
            line = step * 8 + u
            for piece in range(pieces):
                block = line * (pieces // splits) + piece // splits
                for d in range(2):
                    outs[piece % splits][block, d] = two[
                        pl.ds((d * size + line) * pitch + piece * rows, rows), :
                    ].astype(BF16)
        return carry

    lax.fori_loop(0, size // 8, give, 0)


def range_compress(echo, middle, first, count, blocks, splits):
    length = echo.shape[1]
    size = math.isqrt(length)
    index = np.arange(size)
    forward = as_bf16(realified(unit_table(index, index, size, -1)))
    backward = as_bf16(realified(unit_table(index, index, size, 1)))
    rows = length // blocks // splits
    whole = lambda *shape: pl.BlockSpec(shape, lambda i: (0,) * len(shape))
    scratch = pltpu.VMEM((2 * (length + size), LANES), F32)
    return pl.pallas_call(
        functools.partial(range_kernel, size, splits),
        grid=(count,),
        in_specs=[
            pl.BlockSpec((2, length, LANES), lambda i: (0, 0, first + i)),
            whole(2 * size, 2 * size),
            whole(size, 2 * size, 2 * size),
            whole(2 * size, 2 * size),
        ],
        out_specs=[pl.BlockSpec((blocks, 2, rows, LANES), lambda i: (0, 0, 0, i))] * splits,
        out_shape=[jax.ShapeDtypeStruct((blocks, 2, rows, count * LANES), BF16)] * splits,
        scratch_shapes=[scratch, scratch],
        compiler_params=pltpu.CompilerParams(vmem_limit_bytes=VMEM),
        name="range_compress",
    )(echo, forward, middle, backward)


def doppler_kernel(rows, first, rest, w_ref, cos_ref, sin_ref, u_ref, o_ref, *refs):
    held = refs[-1]
    sources = first.shape[0]
    size = cos_ref.shape[0]
    lines = size // sources
    pitch = rows + 1

    def cast(source, carry):
        for line in range(lines):
            for c in range(2):
                if line == 0:
                    value = first[source, 0, c]
                else:
                    value = rest[source, 0, c, :, (line - 1) * LANES : line * LANES]
                base = (c * lines + line) * sources
                held[pl.ds((base + source) * pitch, rows), :] = value.astype(F32)
        return carry

    lax.fori_loop(0, sources, cast, 0)

    def pair(first_row):
        value = jnp.concatenate(
            [held[pl.ds(first_row + i, 2 * size, stride=pitch), :] for i in range(2)], axis=1
        ).astype(BF16)
        first = jnp.dot(w_ref[...], value, preferred_element_type=F32)
        stacked = []
        for i in range(2):
            real = first[:size, i * LANES : (i + 1) * LANES]
            imag = first[size:, i * LANES : (i + 1) * LANES]
            stacked.append(
                jnp.concatenate(
                    [
                        real * cos_ref[...] - imag * sin_ref[...],
                        real * sin_ref[...] + imag * cos_ref[...],
                    ],
                    axis=1,
                ).astype(BF16)
            )
        second = jnp.dot(
            jnp.concatenate(stacked, axis=0), u_ref[...], preferred_element_type=F32
        ).astype(BF16)
        for i in range(2):
            for d in range(2):
                value = second[i * size : (i + 1) * size, d * LANES : (d + 1) * LANES]
                o_ref[0, first_row + i, d] = value

    def body(step, carry):
        for u in range(4):
            pair(step * 8 + 2 * u)
        return carry

    lax.fori_loop(0, rows // 8, body, 0)
    for rim in refs[:-1]:
        rim[0] = o_ref[0, :MAXS]


def doppler_tables(size, direction):
    index = np.arange(size)
    table = unit_table(index, index, size, direction)
    turn = unit_table(index, index, size * size, direction) / size
    return table, turn.real.astype(np.float32), turn.imag.astype(np.float32)


def doppler_forward(first, rest, part, rows, size, with_rim):
    sources, subs, _, _, width = rest.shape
    table, turn_cos, turn_sin = doppler_tables(size, -1)
    lines = size // sources
    order = np.asarray(
        [lines * source + line for line in range(lines) for source in range(sources)]
    )
    outer = as_bf16(realified(table[:, order]))
    inner = as_bf16(realified(table).T)
    whole = lambda *shape: pl.BlockSpec(shape, lambda i: (0,) * len(shape))
    heights = [rows, MAXS] if with_rim else [rows]
    return pl.pallas_call(
        functools.partial(doppler_kernel, rows),
        grid=(subs,),
        in_specs=[
            pl.BlockSpec((sources, 1, 2, rows, LANES), lambda i: (0, i, 0, part, 0)),
            pl.BlockSpec((sources, 1, 2, rows, width), lambda i: (0, i, 0, 0, 0)),
            whole(2 * size, 2 * size),
            whole(size, size),
            whole(size, size),
            whole(2 * size, 2 * size),
        ],
        out_specs=[
            pl.BlockSpec((1, height, 2, size, size), lambda i: (i, 0, 0, 0, 0))
            for height in heights
        ],
        out_shape=[jax.ShapeDtypeStruct((subs, height, 2, size, size), BF16) for height in heights],
        scratch_shapes=[pltpu.VMEM((2 * size * (rows + 1), LANES), F32)],
        compiler_params=pltpu.CompilerParams(vmem_limit_bytes=VMEM),
        name="doppler_forward",
    )(first, rest, outer, turn_cos, turn_sin, inner)


def turn_polynomials():
    nodes = 0.25 * (1 - np.cos((np.arange(64) + 0.5) * np.pi / 64)) / 2
    roots = np.sqrt(nodes)
    sine = np.polynomial.polynomial.polyfit(nodes, np.sin(2 * np.pi * roots) / roots, 6)
    cosine = np.polynomial.polynomial.polyfit(nodes, np.cos(2 * np.pi * roots), 6)
    return [round(float(v), 7) for v in sine], [round(float(v), 7) for v in cosine]


def turns(cycles):
    sine_terms, cosine_terms = turn_polynomials()
    part = cycles - jnp.floor(cycles + 0.5)
    square = part * part
    sine = jnp.full_like(square, sine_terms[-1])
    cosine = jnp.full_like(square, cosine_terms[-1])
    for term in reversed(sine_terms[:-1]):
        sine = sine * square + term
    for term in reversed(cosine_terms[:-1]):
        cosine = cosine * square + term
    return cosine, sine * part


def factor_kernel(kappa_ref, phase_ref, o_ref):
    def body(step, carry):
        for u in range(2):
            row = step * 2 + u
            cosine, sine = turns(kappa_ref[row] * phase_ref[0])
            o_ref[0, row, 0] = cosine.astype(BF16)
            o_ref[0, row, 1] = sine.astype(BF16)
        return carry

    lax.fori_loop(0, o_ref.shape[1] // 2, body, 0)


def azimuth_factors(kappa, phase):
    subs, size, _ = phase.shape
    rows = kappa.shape[0]
    return pl.pallas_call(
        factor_kernel,
        grid=(subs,),
        in_specs=[
            pl.BlockSpec(memory_space=pltpu.SMEM),
            pl.BlockSpec((1, size, size), lambda i: (i, 0, 0)),
        ],
        out_specs=pl.BlockSpec((1, rows, 2, size, size), lambda i: (i, 0, 0, 0, 0)),
        out_shape=jax.ShapeDtypeStruct((subs, rows, 2, size, size), BF16),
        compiler_params=pltpu.CompilerParams(vmem_limit_bytes=VMEM),
        name="azimuth_factors",
    )(kappa, phase)


def image_kernel(earlier, finish, *refs):
    own, rim, factor_ref, shift_ref, cos_ref, sin_ref, u_ref = refs[:7]
    refs = refs[7:]
    if finish:
        mine_ref, w_ref = refs[:2]
        before, refs = refs[2 : 2 + earlier], refs[2 + earlier :]
        outs, (moved, summed, middle, turned) = refs[:-4], refs[-4:]
    else:
        (out, moved, summed) = refs
    step = pl.program_id(0)
    subs, rows, _, tile, size = own.shape
    shift = shift_ref[...]
    bits = [((shift >> k) & 1).astype(F32).astype(BF16) > 0.5 for k in range(4)]

    def aperture(index, carry):
        for d in range(2):
            values = [own[index, r, d] for r in range(rows)]
            values += [rim[index, r, d] for r in range(MAXS)]
            four = [jnp.where(bits[2], values[r + 4], values[r]) for r in range(rows + 3)]
            two = [jnp.where(bits[1], four[r + 2], four[r]) for r in range(rows + 1)]
            one = [jnp.where(bits[0], two[r + 1], two[r]) for r in range(rows)]
            for r in range(rows):
                moved[index, d, r] = jnp.where(bits[3], values[r + 8], one[r])
        return carry

    lax.fori_loop(0, subs, aperture, 0)

    def row_sum(turn, carry):
        for u in range(4):
            row = turn * 4 + u
            real = jnp.zeros((tile, size), F32)
            imag = jnp.zeros((tile, size), F32)
            for index in range(subs):
                cosine = factor_ref[index, row, 0].astype(F32)
                sine = factor_ref[index, row, 1].astype(F32)
                a, b = moved[index, 0, row].astype(F32), moved[index, 1, row].astype(F32)
                real = real + (a * cosine - b * sine)
                imag = imag + (a * sine + b * cosine)
            summed[pl.ds(pl.multiple_of(row * tile, tile), tile), :] = jnp.concatenate(
                [real, imag], axis=1
            ).astype(BF16)
        return carry

    lax.fori_loop(0, rows // 4, row_sum, 0)
    first = jnp.dot(summed[...], u_ref[...], preferred_element_type=F32)
    for r in range(rows):
        real = first[r * tile : (r + 1) * tile, :size]
        imag = first[r * tile : (r + 1) * tile, size:]
        real, imag = (
            (real * cos_ref[...] - imag * sin_ref[...]).astype(BF16),
            (real * sin_ref[...] + imag * cos_ref[...]).astype(BF16),
        )
        if finish:
            where = pl.ds(pl.multiple_of(step * tile, tile), tile)
            middle[r, 0, where, :] = real
            middle[r, 1, where, :] = imag
        else:
            out[r, 0] = real
            out[r, 1] = imag

    if not finish:
        return

    @pl.when(step == pl.num_programs(0) - 1)
    def _():
        held = [(ref, r) for ref in list(before) + [middle] for r in range(ref.shape[0])]
        pitch = len(held) + 1
        for at in range(0, len(held), 2):
            value = jnp.concatenate(
                [
                    jnp.concatenate([ref[r, c] for c in range(2)], axis=0)
                    for ref, r in held[at : at + 2]
                ],
                axis=1,
            )
            result = jnp.dot(w_ref[...], value, preferred_element_type=F32)
            for i in range(2):
                turned[pl.ds(at + i, 2 * size, stride=pitch), :] = result[
                    :, i * LANES : (i + 1) * LANES
                ]
        per_group = size // len(outs)
        for k, piece in enumerate(outs):
            group = mine_ref[0] ^ k
            for d in range(2):
                for j in range(per_group):
                    line = (d * size + group * per_group + j) * pitch
                    piece[d, :, j * LANES : (j + 1) * LANES] = turned[
                        pl.ds(line, len(held)), :
                    ].astype(BF16)


def image_rows(own, own_at, rows, rim, rim_at, factors, part, shift, mine, groups, before):
    subs, _, _, size, _ = own.shape
    tile = 16
    finish = mine is not None
    table, turn_cos, turn_sin = doppler_tables(size, 1)
    outer = as_bf16(realified(table))
    inner = as_bf16(realified(table).T)
    whole = lambda *shape: pl.BlockSpec(shape, lambda i: (0,) * len(shape))
    lines = pl.BlockSpec((tile, size), lambda i: (i, 0))
    width = size * size // groups
    in_specs = [
        pl.BlockSpec((subs, rows, 2, tile, size), lambda i: (0, own_at, 0, i, 0)),
        pl.BlockSpec((subs, MAXS, 2, tile, size), lambda i: (0, rim_at, 0, i, 0)),
        pl.BlockSpec((subs, rows, 2, tile, size), lambda i: (0, part, 0, i, 0)),
        lines,
        lines,
        lines,
        whole(2 * size, 2 * size),
    ]
    operands = [own, rim, factors, shift, turn_cos, turn_sin, inner]
    scratch = [
        pltpu.VMEM((subs, 2, rows, tile, size), BF16),
        pltpu.VMEM((rows * tile, 2 * size), BF16),
    ]
    if finish:
        total = rows + sum(piece.shape[0] for piece in before)
        in_specs += [pl.BlockSpec(memory_space=pltpu.SMEM), whole(2 * size, 2 * size)]
        in_specs += [whole(*piece.shape) for piece in before]
        operands += [mine, outer, *before]
        out_specs = [whole(2, total, width)] * groups
        out_shape = [jax.ShapeDtypeStruct((2, total, width), BF16)] * groups
        scratch += [
            pltpu.VMEM((rows, 2, size, size), BF16),
            pltpu.VMEM((2 * size * (total + 1), LANES), F32),
        ]
    else:
        out_specs = pl.BlockSpec((rows, 2, tile, size), lambda i: (0, 0, i, 0))
        out_shape = jax.ShapeDtypeStruct((rows, 2, size, size), BF16)
    return pl.pallas_call(
        functools.partial(image_kernel, len(before), finish),
        grid=(size // tile,),
        in_specs=in_specs,
        out_specs=out_specs,
        out_shape=out_shape,
        scratch_shapes=scratch,
        compiler_params=pltpu.CompilerParams(vmem_limit_bytes=VMEM),
        name="image_rows",
    )(*operands)


def place_kernel(mine_ref, *refs):
    pieces, o_ref = refs[:-1], refs[-1]
    rows = pieces[0].shape[1]
    groups = len(pieces) // 2
    for half in range(2):
        for k in range(groups):
            line = (mine_ref[0] ^ k) * 2 * rows + half * rows
            o_ref[0, pl.ds(pl.multiple_of(line, rows), rows), :] = pieces[half * groups + k][0]


def place_rows(mine, pieces):
    _, rows, width = pieces[0].shape
    return pl.pallas_call(
        place_kernel,
        grid=(2,),
        in_specs=[pl.BlockSpec(memory_space=pltpu.SMEM)]
        + [pl.BlockSpec((1, rows, width), lambda i: (i, 0, 0))] * len(pieces),
        out_specs=pl.BlockSpec((1, rows * len(pieces), width), lambda i: (i, 0, 0)),
        out_shape=jax.ShapeDtypeStruct((2, rows * len(pieces), width), BF16),
        compiler_params=pltpu.CompilerParams(vmem_limit_bytes=VMEM),
        name="place_rows",
    )(mine, *pieces)


def on_device(raw_echo, range_phase, kappa, doppler, migration):
    _, _, range_len, pulse_dev = raw_echo.shape
    puls, subs = lax.axis_size("pul"), lax.axis_size("sub")
    blocks = puls * subs
    rows = range_len // blocks
    half = rows // 2
    pulse_len = pulse_dev * puls
    size = math.isqrt(pulse_len)
    sub_index = lax.axis_index("sub")
    mine = sub_index.reshape(1).astype(jnp.int32)
    middle = range_middle(range_phase, math.isqrt(range_len))
    echo = raw_echo.reshape(2, range_len, pulse_dev)

    def spread(sent):
        got = lax.all_to_all(sent, ("pul", "sub"), 0, 0, tiled=True)
        return got.reshape((puls, subs) + sent.shape[1:])

    def swap(pieces):
        sent = [
            lax.ppermute(pieces[k], "sub", [(i, i ^ k) for i in range(subs)])
            for k in range(subs - 1, 0, -1)
        ]
        return [pieces[0]] + sent[::-1]

    (sent,) = range_compress(echo, middle, 0, 1, blocks, 1)
    sent, echo = lax.optimization_barrier((sent, echo))
    first = spread(sent)
    count = pulse_dev // LANES - 1
    sent_low, sent_high = range_compress(echo, middle, 1, count, blocks, 2)
    own_shift = lax.dynamic_slice_in_dim(migration, sub_index, 1, 0)
    shift = own_shift.reshape(size, size).T
    phase = jnp.swapaxes(doppler.reshape(subs, size, size), 1, 2) * (0.5 / math.pi)
    own_kappa = lax.dynamic_slice_in_dim(kappa, sub_index * rows, rows, 0)
    factors = azimuth_factors(own_kappa, phase)
    first, sent_low, factors, shift = lax.optimization_barrier((first, sent_low, factors, shift))
    got_low = spread(sent_low)
    got_low, sent_high = lax.optimization_barrier((got_low, sent_high))
    got_high = spread(sent_high)
    low, edge = doppler_forward(first, got_low, 0, half, size, True)
    place = lambda block: (block % subs) * puls + block // subs
    pairs = [(place(block), place(block - 1)) for block in range(1, blocks)]
    rim = lax.ppermute(edge, ("sub", "pul"), pairs)
    top = image_rows(low, 0, MAXS, low, 1, factors, 0, shift, None, subs, [])
    got_high, top = lax.optimization_barrier((got_high, top))
    (high,) = doppler_forward(first, got_high, 1, half, size, False)
    pieces = image_rows(low, 1, MAXS, high, 0, factors, 1, shift, mine, subs, [top])
    upper = swap(pieces)
    pieces = image_rows(high, 0, half, rim, 0, factors, 1, shift, mine, subs, [])
    lower = swap(pieces)
    return place_rows(mine, upper + lower)


def solution(mesh):
    placed = (P(None, "sub", None, "pul"), P(), P("pul"), P(), P("pul", None))
    return jax.shard_map(
        on_device, mesh=mesh, in_specs=placed, out_specs=P(None, "pul", "sub"), check_vma=False
    )
```

time: 216 us -> 232 us (1.074)
  Pallas kernels: 74.6 us -> 92.7 us
  waiting for transfers between devices: 44 us -> 55.9 us
  local copies, waits for them, and re-layouts: 9.42 us -> 4.73 us
  blocking collectives: 53.2 us -> 50 us
  matrix products: 2.83 us -> 0 us
    all_to_all x1 -> x0, blocking collectives: 17.8 us -> none  [on_device(): lax.all_to_all(image_rows(high, rim, factors, 1, shift, subs), 'sub', 0,...]
    pallas_call x4 -> x7, Pallas kernels: 46.7 us -> 64.4 us  [the longest x2 30.7 us: range_compress(): pl.pallas_call(functools.partial(range_kernel, size, splits), grid=(count...]
    all_to_all x1, blocking collectives: 35.4 us -> 50 us  [spread(): got = lax.all_to_all(sent, ('pul', 'sub'), 0, 0, tiled=True)]
    ppermute x1 -> x7, waiting for transfers between devices: 0.01 us -> 11.8 us  [the longest x6 11.8 us: swap(): lax.ppermute(pieces[k], 'sub', [(i, i ^ k) for i in range(subs)])]
    ppermute x1 -> x7, starting transfers between devices: 2.26 us -> 7.13 us  [the longest x6 4.87 us: swap(): lax.ppermute(pieces[k], 'sub', [(i, i ^ k) for i in range(subs)])]
    all_to_all x1 -> x0, starting transfers between devices: 4.58 us -> none  [on_device(): lax.all_to_all(image_rows(low, high, factors, 0, shift, subs), 'sub', 0,...]
    all_to_all x2, waiting for transfers between devices: 40.7 us -> 44.1 us  [spread(): got = lax.all_to_all(sent, ('pul', 'sub'), 0, 0, tiled=True)]
    another operation x1 -> x0, other arithmetic: 3.32 us -> none
  transfers between devices with their start and end apart: 4 -> 9, of which waited for: 3 -> 3; matrix products, arithmetic and copies ran while one was open for 3% -> 1% of each run, Pallas kernels for 29% -> 33%
where the time goes in v3:
time: 232 us; the launch traced here: 230 us
  Pallas kernels  92.7 us (40%)
  waiting for transfers between devices  55.9 us (24%)
  blocking collectives  50 us (22%)
  starting transfers between devices  25.4 us (11%)
  local copies, waits for them, and re-layouts  4.73 us (2%)
    all_to_all x1, blocking collectives, spread(): got = lax.all_to_all(sent, ('pul', 'sub'), 0, 0, tiled=True)  50 us
    all_to_all x2, waiting for transfers between devices, spread(): got = lax.all_to_all(sent, ('pul', 'sub'), 0, 0, tiled=True)  44.1 us
    pallas_call x2, Pallas kernels, range_compress(): pl.pallas_call(functools.partial(range_kernel, size, splits), grid=(count...  30.7 us
    pallas_call x3, Pallas kernels, image_rows(): pl.pallas_call(functools.partial(image_kernel, len(before), finish), grid...  26.3 us
    all_to_all x2, starting transfers between devices, spread(): got = lax.all_to_all(sent, ('pul', 'sub'), 0, 0, tiled=True)  18.3 us
    pallas_call x2, Pallas kernels, doppler_forward(): pl.pallas_call(functools.partial(doppler_kernel, rows), grid=(subs,), in_...  16.8 us
    ppermute x6, waiting for transfers between devices, swap(): lax.ppermute(pieces[k], 'sub', [(i, i ^ k) for i in range(subs)])  11.8 us
    pallas_call x1, Pallas kernels, azimuth_factors(): pl.pallas_call(factor_kernel, grid=(subs,), in_specs=[pl.BlockSpec(memory...  11.4 us
  transfers between devices with their start and end apart: 9, of which 3 were waited for; matrix products, arithmetic and copies ran while one was open for 1% of the time, Pallas kernels for 33%

profile of v3, /device:TPU:7, one launch (start us, length us, event | category | flops | bytes accessed | tf_op | source)
XLA Modules:
  0.0 230.4 jit_solution(9769022049124214535)
XLA Ops:
  0.0 0.0 copy-start
  0.0 0.8 broadcast_multiply_fusion
  0.8 0.1 mul.27
  0.8 0.1 copy.30
  0.9 0.7 pad_maximum_fusion.phase_ref
  1.6 4.8 %range_middle.1.t_ref = bf16[64,128,128]{2,1,0:T(8,128)(2,1)} custom-call(f32[64,128]{1,0:T(8,128)} %pad_maximum_fusion.phase_ref, bf16[64,128,128]{2,1,0:T(8,128)(2,1)} %constant.37.clone.wave_ref), custom_call_target="tpu_custom_call" | custom-call | tf_op jit(solution)/shard_map/range_middle/pallas_call | solution.py:60
  6.4 9.4 %range_compress.2 = bf16[128,2,32,128]{3,2,1,0:T(8,128)(2,1)} custom-call(bf16[2,4096,512]{2,1,0:T(8,128)(2,1)} %bitcast.14, bf16[128,128]{1,0:T(8,128)(2,1)} %constant.38.clone.w_ref, bf16[64,128,128]{2,1,0:T(8,128)(2,1)} %range_middle.1.t_ref, bf16[128,128]{1,0:T(8,128)(2,1)} %constant.39.clone.v_ref), custom_call_target="tpu_custom_call" | custom-call | tf_op jit(solution)/shard_map/range_compress/pallas_call | solution.py:144
  15.8 10.8 %all-to-all-start = ((bf16[128,2,32,128]{3,2,1,0:T(8,128)(2,1)}), bf16[128,2,32,128]{3,2,1,0:T(8,128)(2,1)S(1)}, u32[]{:S(2)}, u32[]{:S(2)}) async-start(bf16[128,2,32,128]{3,2,1,0:T(8,128)(2,1)} %range_compress.2), calls=%async_computation | async-start | bytes 4194304 | tf_op jit(solution)/shard_map/all_to_all | solution.py:486
  26.6 0.0 copy-done
  26.6 0.1 constant_dynamic-slice_fusion
  26.7 0.7 copy.32
  27.4 0.0 copy-done.9
  27.4 0.1 multiply_bitcast_fusion
  27.5 0.8 copy.31
  28.4 21.3 %range_compress.3 = (bf16[128,2,16,384]{3,2,1,0:T(8,128)(2,1)}, bf16[128,2,16,384]{3,2,1,0:T(8,128)(2,1)}) custom-call(bf16[2,4096,512]{2,1,0:T(8,128)(2,1)} %bitcast.15, bf16[128,128]{1,0:T(8,128)(2,1)} %constant.38.clone.w_ref, bf16[64,128,128]{2,1,0:T(8,128)(2,1)} %range_middle.1.t_ref, bf16[128,128]{1,0:T(8,128)(2,1)} %constant.39.clone.v_ref), custom_call_target="tpu_custom_call" | custom-call | tf_op jit(solution)/shard_map/range_compress/pallas_call | solution.py:144
  49.7 0.0 copy-done.10
  49.7 0.6 dynamic_slice.6.kappa_ref
  50.2 11.4 %azimuth_factors.1.refs_2_ = bf16[4,32,2,128,128]{4,3,2,1,0:T(8,128)(2,1)} custom-call(f32[32]{0:T(128)} %dynamic_slice.6.kappa_ref, f32[4,128,128]{2,1,0:T(8,128)} %bitcast.23), custom_call_target="tpu_custom_call" | custom-call | tf_op jit(solution)/shard_map/azimuth_factors/pallas_call | solution.py:293
  61.7 0.0 all-to-all-done
  61.7 50.0 %all_to_all.15 = bf16[128,2,16,384]{3,2,1,0:T(8,128)(2,1)} all-to-all(bf16[128,2,16,384]{3,2,1,0:T(8,128)(2,1)} %get-tuple-element.31), channel_id=1, replica_groups=mesh['sub'=4,'pul'=32] {'pul','sub'}, dimensions={0} | all-to-all | bytes 6291456 | tf_op jit(solution)/shard_map/all_to_all | solution.py:486
  111.7 0.0 copy-done.1
  111.7 7.5 %all-to-all-start.2 = ((bf16[128,2,16,384]{3,2,1,0:T(8,128)(2,1)}), bf16[128,2,16,384]{3,2,1,0:T(8,128)(2,1)S(1)}, u32[]{:S(2)}, u32[]{:S(2)}) async-start(bf16[128,2,16,384]{3,2,1,0:T(8,128)(2,1)} %get-tuple-element.35), calls=%async_computation.2 | async-start | bytes 6291456 | tf_op jit(solution)/shard_map/all_to_all | solution.py:486
  119.2 8.6 %doppler_forward.2 = (bf16[4,16,2,128,128]{4,3,2,1,0:T(8,128)(2,1)}, bf16[4,8,2,128,128]{4,3,2,1,0:T(8,128)(2,1)}) custom-call(bf16[32,4,2,32,128]{4,3,2,1,0:T(8,128)(2,1)} %bitcast.16, bf16[32,4,2,16,384]{4,3,2,1,0:T(8,128)(2,1)} %bitcast.19, bf16[256,256]{1,0:T(8,128)(2,1)} %constant.40.clone.w_ref, f32[128,128]{1,0:T(8,128)} %constant.41.clone.cos_ref.refs_4_, ...), custom_call_target="tpu_custom_call" | custom-call | tf_op jit(solution)/shard_map/doppler_forward/pallas_call | solution.py:235
  127.9 2.3 collective-permute-start.3
  130.1 7.6 %image_rows.3.refs_9_ = bf16[8,2,128,128]{3,2,1,0:T(8,128)(2,1)} custom-call(bf16[4,16,2,128,128]{4,3,2,1,0:T(8,128)(2,1)} %get-tuple-element.34.refs_0_.refs_1_, bf16[4,16,2,128,128]{4,3,2,1,0:T(8,128)(2,1)} %get-tuple-element.34.refs_0_.refs_1_, bf16[4,32,2,128,128]{4,3,2,1,0:T(8,128)(2,1)} %azimuth_factors.1.refs_2_, s32[128,128]{1,0:T(8,128)} %bitcast.20, ...), custom_call_target="tpu_custom_call" | custom-call | tf_op jit(solution)/shard_map/image_rows/pallas_call | solution.py:436
  137.8 44.1 %all-to-all-done.2 = bf16[128,2,16,384]{3,2,1,0:T(8,128)(2,1)S(1)} async-done(((bf16[128,2,16,384]{3,2,1,0:T(8,128)(2,1)}), bf16[128,2,16,384]{3,2,1,0:T(8,128)(2,1)S(1)}, u32[]{:S(2)}, u32[]{:S(2)}) %all-to-all-start.2) | async-done | bytes 3145760 | tf_op jit(solution)/shard_map/all_to_all | solution.py:486
  181.8 1.6 copy-done.2
  183.5 8.2 %doppler_forward.3.refs_1_.refs_0_ = bf16[4,16,2,128,128]{4,3,2,1,0:T(8,128)(2,1)} custom-call(bf16[32,4,2,32,128]{4,3,2,1,0:T(8,128)(2,1)} %bitcast.17, bf16[32,4,2,16,384]{4,3,2,1,0:T(8,128)(2,1)} %bitcast.18, bf16[256,256]{1,0:T(8,128)(2,1)} %constant.40.clone.w_ref, f32[128,128]{1,0:T(8,128)} %constant.41.clone.cos_ref.refs_4_, ...), custom_call_target="tpu_custom_call" | custom-call | tf_op jit(solution)/shard_map/doppler_forward/pallas_call | solution.py:235
  191.7 8.5 %image_rows.4 = (bf16[2,16,4096]{2,1,0:T(8,128)(2,1)}, bf16[2,16,4096]{2,1,0:T(8,128)(2,1)}, bf16[2,16,4096]{2,1,0:T(8,128)(2,1)}, bf16[2,16,4096]{2,1,0:T(8,128)(2,1)}) custom-call(bf16[4,16,2,128,128]{4,3,2,1,0:T(8,128)(2,1)} %get-tuple-element.34.refs_0_.refs_1_, bf16[4,16,2,128,128]{4,3,2,1,0:T(8,128)(2,1)} %doppler_forward.3.refs_1_.refs_0_, ...), custom_call_target="tpu_custom_call" | custom-call | tf_op jit(solution)/shard_map/image_rows/pallas_call | solution.py:436
  200.2 1.0 collective-permute-start
  201.2 0.0 collective-permute-start.1
  201.2 1.7 collective-permute-start.2
  202.9 0.0 collective-permute-done.3.refs_1_
  202.9 10.1 %image_rows.5 = (bf16[2,16,4096]{2,1,0:T(8,128)(2,1)}, bf16[2,16,4096]{2,1,0:T(8,128)(2,1)}, bf16[2,16,4096]{2,1,0:T(8,128)(2,1)}, bf16[2,16,4096]{2,1,0:T(8,128)(2,1)}) custom-call(bf16[4,16,2,128,128]{4,3,2,1,0:T(8,128)(2,1)} %doppler_forward.3.refs_1_.refs_0_, bf16[4,8,2,128,128]{4,3,2,1,0:T(8,128)(2,1)} %collective-permute-done.3.refs_1_, ...), custom_call_target="tpu_custom_call" | custom-call | tf_op jit(solution)/shard_map/image_rows/pallas_call | solution.py:436
  213.0 0.2 collective-permute-start.4
  213.2 0.0 collective-permute-start.5
  213.2 0.0 collective-permute-done.refs_1_
  213.2 2.0 collective-permute-start.6
  215.2 0.0 collective-permute-done.1.refs_2_
  215.2 0.0 collective-permute-done.2.refs_3_
  215.2 0.0 collective-permute-done.4.refs_5_
  215.2 0.0 copy-start.6
  215.2 5.7 %collective-permute-done.5.refs_6_ = bf16[2,16,4096]{2,1,0:T(8,128)(2,1)S(1)} collective-permute-done((bf16[2,16,4096]{2,1,0:T(8,128)(2,1)}, bf16[2,16,4096]{2,1,0:T(8,128)(2,1)S(1)}, u32[]{:S(2)}, u32[]{:S(2)}) %collective-permute-start.5) | collective-permute-done | bytes 262176 | tf_op jit(solution)/shard_map/ppermute | solution.py:491
  220.9 6.1 %collective-permute-done.6.refs_7_ = bf16[2,16,4096]{2,1,0:T(8,128)(2,1)S(1)} collective-permute-done((bf16[2,16,4096]{2,1,0:T(8,128)(2,1)}, bf16[2,16,4096]{2,1,0:T(8,128)(2,1)S(1)}, u32[]{:S(2)}, u32[]{:S(2)}) %collective-permute-start.6) | collective-permute-done | bytes 262176 | tf_op jit(solution)/shard_map/ppermute | solution.py:491
  227.0 0.0 copy-done.3
  227.0 0.0 copy-done.5
  227.1 0.7 copy-done.8
  227.7 2.7 %place_rows.1 = bf16[2,128,4096]{2,1,0:T(8,128)(2,1)} custom-call(s32[1]{0:T(128)} %bitcast.refs_7_.mine_ref, bf16[2,16,4096]{2,1,0:T(8,128)(2,1)} %get-tuple-element.40.refs_0_, bf16[2,16,4096]{2,1,0:T(8,128)(2,1)} %copy-done.3, bf16[2,16,4096]{2,1,0:T(8,128)(2,1)} %copy-done.4, bf16[2,16,4096]{2,1,0:T(8,128)(2,1)} %copy-done.5, ...), custom_call_target="tpu_custom_call" | custom-call | tf_op jit(solution)/shard_map/place_rows/pallas_call | solution.py:460
  (13 shorter events, 0.0 us)
Async XLA Ops:
  0.0 26.6 %copy-start = (s32[4,16384]{1,0:T(4,128)S(1)}, s32[4,16384]{1,0:T(4,128)}, u32[]{:S(2)}) copy-start(s32[4,16384]{1,0:T(4,128)} %param.33) | copy-start | bytes 786436
  15.8 11.6 %copy-start.9 = (f32[4,16384]{1,0:T(4,128)S(1)}, f32[4,16384]{1,0:T(4,128)}, u32[]{:S(2)}) copy-start(f32[4,16384]{1,0:T(4,128)} %param.32) | copy-start | bytes 786436
  15.8 45.9 %all-to-all-start = ((bf16[128,2,32,128]{3,2,1,0:T(8,128)(2,1)}), bf16[128,2,32,128]{3,2,1,0:T(8,128)(2,1)S(1)}, u32[]{:S(2)}, u32[]{:S(2)}) async-start(bf16[128,2,32,128]{3,2,1,0:T(8,128)(2,1)} %range_compress.2), calls=%async_computation | async-start | bytes 4194304 | tf_op jit(solution)/shard_map/all_to_all | solution.py:486
  28.4 21.3 %copy-start.10 = (f32[128]{0:T(128)S(1)}, f32[128]{0:T(128)}, u32[]{:S(2)}) copy-start(f32[128]{0:T(128)} %param.31) | copy-start | bytes 1540
  61.7 50.0 %copy-start.1 = (bf16[128,2,32,128]{3,2,1,0:T(8,128)(2,1)}, bf16[128,2,32,128]{3,2,1,0:T(8,128)(2,1)S(1)}, u32[]{:S(2)}) copy-start(bf16[128,2,32,128]{3,2,1,0:T(8,128)(2,1)S(1)} %all-to-all-done) | copy-start | bytes 6291460
  111.7 70.2 %all-to-all-start.2 = ((bf16[128,2,16,384]{3,2,1,0:T(8,128)(2,1)}), bf16[128,2,16,384]{3,2,1,0:T(8,128)(2,1)S(1)}, u32[]{:S(2)}, u32[]{:S(2)}) async-start(bf16[128,2,16,384]{3,2,1,0:T(8,128)(2,1)} %get-tuple-element.35), calls=%async_computation.2 | async-start | bytes 6291456 | tf_op jit(solution)/shard_map/all_to_all | solution.py:486
  127.9 75.0 %collective-permute-start.3 = (bf16[4,8,2,128,128]{4,3,2,1,0:T(8,128)(2,1)}, bf16[4,8,2,128,128]{4,3,2,1,0:T(8,128)(2,1)}, u32[]{:S(2)}, u32[]{:S(2)}) collective-permute-start(bf16[4,8,2,128,128]{4,3,2,1,0:T(8,128)(2,1)} %get-tuple-element.44), channel_id=1, source_target_pairs={{32,0},{64,32},{96,64},{1,96},{33,1},{65,33},{97,65},{2,97},{34,2}... | collective-permute-start | bytes 6291464 | tf_op jit(solution)/shard_map/ppermute | solution.py:513
  181.8 1.6 copy-start.2
  200.2 13.0 %collective-permute-start = (bf16[2,16,4096]{2,1,0:T(8,128)(2,1)}, bf16[2,16,4096]{2,1,0:T(8,128)(2,1)S(1)}, u32[]{:S(2)}, u32[]{:S(2)}) collective-permute-start(bf16[2,16,4096]{2,1,0:T(8,128)(2,1)} %get-tuple-element.41), channel_id=1, source_target_pairs={{0,32},{32,0},{64,96},{96,64},{1,33},{33,1},{65,97},{97,65},{2,34}... | collective-permute-start | bytes 786440 | tf_op jit(solution)/shard_map/ppermute | solution.py:491
  201.2 14.0 %collective-permute-start.1 = (bf16[2,16,4096]{2,1,0:T(8,128)(2,1)}, bf16[2,16,4096]{2,1,0:T(8,128)(2,1)S(1)}, u32[]{:S(2)}, u32[]{:S(2)}) collective-permute-start(bf16[2,16,4096]{2,1,0:T(8,128)(2,1)} %get-tuple-element.42), channel_id=1, source_target_pairs={{0,64},{32,96},{64,0},{96,32},{1,65},{33,97},{65,1},{97,33},{2,66}... | collective-permute-start | bytes 786440 | tf_op jit(solution)/shard_map/ppermute | solution.py:491
  201.2 14.0 %collective-permute-start.2 = (bf16[2,16,4096]{2,1,0:T(8,128)(2,1)}, bf16[2,16,4096]{2,1,0:T(8,128)(2,1)S(1)}, u32[]{:S(2)}, u32[]{:S(2)}) collective-permute-start(bf16[2,16,4096]{2,1,0:T(8,128)(2,1)} %get-tuple-element.43), channel_id=1, source_target_pairs={{0,96},{32,64},{64,32},{96,0},{1,97},{33,65},{65,33},{97,1},{2,98}... | collective-permute-start | bytes 786440 | tf_op jit(solution)/shard_map/ppermute | solution.py:491
  213.0 2.2 collective-permute-start.4
  213.2 7.7 %collective-permute-start.5 = (bf16[2,16,4096]{2,1,0:T(8,128)(2,1)}, bf16[2,16,4096]{2,1,0:T(8,128)(2,1)S(1)}, u32[]{:S(2)}, u32[]{:S(2)}) collective-permute-start(bf16[2,16,4096]{2,1,0:T(8,128)(2,1)} %get-tuple-element.47), channel_id=1, source_target_pairs={{0,64},{32,96},{64,0},{96,32},{1,65},{33,97},{65,1},{97,33},{2,66}... | collective-permute-start | bytes 786440 | tf_op jit(solution)/shard_map/ppermute | solution.py:491
  213.2 13.8 %copy-start.3 = (bf16[2,16,4096]{2,1,0:T(8,128)(2,1)}, bf16[2,16,4096]{2,1,0:T(8,128)(2,1)S(1)}, u32[]{:S(2)}) copy-start(bf16[2,16,4096]{2,1,0:T(8,128)(2,1)S(1)} %collective-permute-done.refs_1_) | copy-start | bytes 786436
  213.2 13.8 %collective-permute-start.6 = (bf16[2,16,4096]{2,1,0:T(8,128)(2,1)}, bf16[2,16,4096]{2,1,0:T(8,128)(2,1)S(1)}, u32[]{:S(2)}, u32[]{:S(2)}) collective-permute-start(bf16[2,16,4096]{2,1,0:T(8,128)(2,1)} %get-tuple-element.48), channel_id=1, source_target_pairs={{0,96},{32,64},{64,32},{96,0},{1,97},{33,65},{65,33},{97,1},{2,98}... | collective-permute-start | bytes 786440 | tf_op jit(solution)/shard_map/ppermute | solution.py:491
  215.2 11.9 %copy-start.4 = (bf16[2,16,4096]{2,1,0:T(8,128)(2,1)}, bf16[2,16,4096]{2,1,0:T(8,128)(2,1)S(1)}, u32[]{:S(2)}) copy-start(bf16[2,16,4096]{2,1,0:T(8,128)(2,1)S(1)} %collective-permute-done.1.refs_2_) | copy-start | bytes 786436
  215.2 11.9 %copy-start.5 = (bf16[2,16,4096]{2,1,0:T(8,128)(2,1)}, bf16[2,16,4096]{2,1,0:T(8,128)(2,1)S(1)}, u32[]{:S(2)}) copy-start(bf16[2,16,4096]{2,1,0:T(8,128)(2,1)S(1)} %collective-permute-done.2.refs_3_) | copy-start | bytes 786436
  215.2 11.8 %copy-start.6 = (bf16[2,16,4096]{2,1,0:T(8,128)(2,1)}, bf16[2,16,4096]{2,1,0:T(8,128)(2,1)S(1)}, u32[]{:S(2)}) copy-start(bf16[2,16,4096]{2,1,0:T(8,128)(2,1)S(1)} %collective-permute-done.4.refs_5_) | copy-start | bytes 786436
  220.9 6.1 %copy-start.7 = (bf16[2,16,4096]{2,1,0:T(8,128)(2,1)}, bf16[2,16,4096]{2,1,0:T(8,128)(2,1)S(1)}, u32[]{:S(2)}) copy-start(bf16[2,16,4096]{2,1,0:T(8,128)(2,1)S(1)} %collective-permute-done.5.refs_6_) | copy-start | bytes 786436
  227.0 0.7 copy-start.8

commit v4 on v3

--- a/solution.py
+++ b/solution.py
@@ -13,6 +13,7 @@
 RBLK = 32
 LANES = 128
 UNROLL = 4
+TILE = 32
 VMEM = 56 * 1024 * 1024
 F32 = jnp.float32
 BF16 = jnp.bfloat16
@@ -201,8 +202,10 @@
         ).astype(BF16)
         for i in range(2):
             for d in range(2):
-                value = second[i * size : (i + 1) * size, d * LANES : (d + 1) * LANES]
-                o_ref[0, first_row + i, d] = value
+                for tile in range(size // TILE):
+                    line = i * size + tile * TILE
+                    value = second[line : line + TILE, d * LANES : (d + 1) * LANES]
+                    o_ref[tile, 0, first_row + i, d] = value
 
     def body(step, carry):
         for u in range(4):
@@ -211,7 +214,7 @@
 
     lax.fori_loop(0, rows // 8, body, 0)
     for rim in refs[:-1]:
-        rim[0] = o_ref[0, :MAXS]
+        rim[:, 0] = o_ref[:, 0, :MAXS]
 
 
 def doppler_tables(size, direction):
@@ -244,10 +247,13 @@
             whole(2 * size, 2 * size),
         ],
         out_specs=[
-            pl.BlockSpec((1, height, 2, size, size), lambda i: (i, 0, 0, 0, 0))
+            pl.BlockSpec((size // TILE, 1, height, 2, TILE, size), lambda i: (0, i, 0, 0, 0, 0))
             for height in heights
         ],
-        out_shape=[jax.ShapeDtypeStruct((subs, height, 2, size, size), BF16) for height in heights],
+        out_shape=[
+            jax.ShapeDtypeStruct((size // TILE, subs, height, 2, TILE, size), BF16)
+            for height in heights
+        ],
         scratch_shapes=[pltpu.VMEM((2 * size * (rows + 1), LANES), F32)],
         compiler_params=pltpu.CompilerParams(vmem_limit_bytes=VMEM),
         name="doppler_forward",
@@ -279,12 +285,13 @@
     def body(step, carry):
         for u in range(2):
             row = step * 2 + u
-            cosine, sine = turns(kappa_ref[row] * phase_ref[0])
-            o_ref[0, row, 0] = cosine.astype(BF16)
-            o_ref[0, row, 1] = sine.astype(BF16)
-        return carry
-
-    lax.fori_loop(0, o_ref.shape[1] // 2, body, 0)
+            for tile in range(o_ref.shape[0]):
+                cosine, sine = turns(kappa_ref[row] * phase_ref[0, tile * TILE : (tile + 1) * TILE])
+                o_ref[tile, 0, row, 0] = cosine.astype(BF16)
+                o_ref[tile, 0, row, 1] = sine.astype(BF16)
+        return carry
+
+    lax.fori_loop(0, o_ref.shape[2] // 2, body, 0)
 
 
 def azimuth_factors(kappa, phase):
@@ -297,8 +304,10 @@
             pl.BlockSpec(memory_space=pltpu.SMEM),
             pl.BlockSpec((1, size, size), lambda i: (i, 0, 0)),
         ],
-        out_specs=pl.BlockSpec((1, rows, 2, size, size), lambda i: (i, 0, 0, 0, 0)),
-        out_shape=jax.ShapeDtypeStruct((subs, rows, 2, size, size), BF16),
+        out_specs=pl.BlockSpec(
+            (size // TILE, 1, rows, 2, TILE, size), lambda i: (0, i, 0, 0, 0, 0)
+        ),
+        out_shape=jax.ShapeDtypeStruct((size // TILE, subs, rows, 2, TILE, size), BF16),
         compiler_params=pltpu.CompilerParams(vmem_limit_bytes=VMEM),
         name="azimuth_factors",
     )(kappa, phase)
@@ -314,14 +323,14 @@
     else:
         (out, moved, summed) = refs
     step = pl.program_id(0)
-    subs, rows, _, tile, size = own.shape
+    _, subs, rows, _, tile, size = own.shape
     shift = shift_ref[...]
     bits = [((shift >> k) & 1).astype(F32).astype(BF16) > 0.5 for k in range(4)]
 
     def aperture(index, carry):
         for d in range(2):
-            values = [own[index, r, d] for r in range(rows)]
-            values += [rim[index, r, d] for r in range(MAXS)]
+            values = [own[0, index, r, d] for r in range(rows)]
+            values += [rim[0, index, r, d] for r in range(MAXS)]
             four = [jnp.where(bits[2], values[r + 4], values[r]) for r in range(rows + 3)]
             two = [jnp.where(bits[1], four[r + 2], four[r]) for r in range(rows + 1)]
             one = [jnp.where(bits[0], two[r + 1], two[r]) for r in range(rows)]
@@ -337,8 +346,8 @@
             real = jnp.zeros((tile, size), F32)
             imag = jnp.zeros((tile, size), F32)
             for index in range(subs):
-                cosine = factor_ref[index, row, 0].astype(F32)
-                sine = factor_ref[index, row, 1].astype(F32)
+                cosine = factor_ref[0, index, row, 0].astype(F32)
+                sine = factor_ref[0, index, row, 1].astype(F32)
                 a, b = moved[index, 0, row].astype(F32), moved[index, 1, row].astype(F32)
                 real = real + (a * cosine - b * sine)
                 imag = imag + (a * sine + b * cosine)
@@ -396,8 +405,7 @@
 
 
 def image_rows(own, own_at, rows, rim, rim_at, factors, part, shift, mine, groups, before):
-    subs, _, _, size, _ = own.shape
-    tile = 16
+    _, subs, _, _, tile, size = own.shape
     finish = mine is not None
     table, turn_cos, turn_sin = doppler_tables(size, 1)
     outer = as_bf16(realified(table))
@@ -406,9 +414,9 @@
     lines = pl.BlockSpec((tile, size), lambda i: (i, 0))
     width = size * size // groups
     in_specs = [
-        pl.BlockSpec((subs, rows, 2, tile, size), lambda i: (0, own_at, 0, i, 0)),
-        pl.BlockSpec((subs, MAXS, 2, tile, size), lambda i: (0, rim_at, 0, i, 0)),
-        pl.BlockSpec((subs, rows, 2, tile, size), lambda i: (0, part, 0, i, 0)),
+        pl.BlockSpec((1, subs, rows, 2, tile, size), lambda i: (i, 0, own_at, 0, 0, 0)),
+        pl.BlockSpec((1, subs, MAXS, 2, tile, size), lambda i: (i, 0, rim_at, 0, 0, 0)),
+        pl.BlockSpec((1, subs, rows, 2, tile, size), lambda i: (i, 0, part, 0, 0, 0)),
         lines,
         lines,
         lines,
@@ -502,16 +510,20 @@
     shift = own_shift.reshape(size, size).T
     phase = jnp.swapaxes(doppler.reshape(subs, size, size), 1, 2) * (0.5 / math.pi)
     own_kappa = lax.dynamic_slice_in_dim(kappa, sub_index * rows, rows, 0)
-    factors = azimuth_factors(own_kappa, phase)
-    first, sent_low, factors, shift = lax.optimization_barrier((first, sent_low, factors, shift))
+    first, sent_low, phase, own_kappa, shift = lax.optimization_barrier(
+        (first, sent_low, phase, own_kappa, shift)
+    )
     got_low = spread(sent_low)
     got_low, sent_high = lax.optimization_barrier((got_low, sent_high))
     got_high = spread(sent_high)
     low, edge = doppler_forward(first, got_low, 0, half, size, True)
+    low, own_kappa = lax.optimization_barrier((low, own_kappa))
+    factors = azimuth_factors(own_kappa, phase)
     place = lambda block: (block % subs) * puls + block // subs
     pairs = [(place(block), place(block - 1)) for block in range(1, blocks)]
+    top = image_rows(low, 0, MAXS, low, 1, factors, 0, shift, None, subs, [])
+    top, edge = lax.optimization_barrier((top, edge))
     rim = lax.ppermute(edge, ("sub", "pul"), pairs)
-    top = image_rows(low, 0, MAXS, low, 1, factors, 0, shift, None, subs, [])
     got_high, top = lax.optimization_barrier((got_high, top))
     (high,) = doppler_forward(first, got_high, 1, half, size, False)
     pieces = image_rows(low, 1, MAXS, high, 0, factors, 1, shift, mine, subs, [top])

time: 232 us -> 219 us (0.944)
  Pallas kernels: 92.7 us -> 86.6 us
  waiting for transfers between devices: 55.9 us -> 52.7 us
  blocking collectives: 50 us -> 47.4 us
    pallas_call x3, Pallas kernels: 26.3 us -> 20 us  [image_rows(): pl.pallas_call(functools.partial(image_kernel, len(before), finish), grid...]
    all_to_all x2, waiting for transfers between devices: 44.1 us -> 39.6 us  [spread(): got = lax.all_to_all(sent, ('pul', 'sub'), 0, 0, tiled=True)]
    all_to_all x1, blocking collectives: 50 us -> 47.4 us  [spread(): got = lax.all_to_all(sent, ('pul', 'sub'), 0, 0, tiled=True)]
  transfers between devices with their start and end apart: 9 -> 9, of which waited for: 3 -> 5; matrix products, arithmetic and copies ran while one was open for 1% -> 1% of each run, Pallas kernels for 33% -> 32%
where the time goes in v4:
time: 219 us
  Pallas kernels  86.6 us (40%)
  waiting for transfers between devices  52.7 us (24%)
  blocking collectives  47.4 us (22%)
  starting transfers between devices  25.4 us (12%)
  local copies, waits for them, and re-layouts  4.78 us (2%)
    all_to_all x1, blocking collectives, spread(): got = lax.all_to_all(sent, ('pul', 'sub'), 0, 0, tiled=True)  47.4 us
    all_to_all x2, waiting for transfers between devices, spread(): got = lax.all_to_all(sent, ('pul', 'sub'), 0, 0, tiled=True)  39.6 us
    pallas_call x2, Pallas kernels, range_compress(): pl.pallas_call(functools.partial(range_kernel, size, splits), grid=(count...  30.8 us
    pallas_call x3, Pallas kernels, image_rows(): pl.pallas_call(functools.partial(image_kernel, len(before), finish), grid...  20 us
    all_to_all x2, starting transfers between devices, spread(): got = lax.all_to_all(sent, ('pul', 'sub'), 0, 0, tiled=True)  18.3 us
    pallas_call x2, Pallas kernels, doppler_forward(): pl.pallas_call(functools.partial(doppler_kernel, rows), grid=(subs,), in_...  17 us
    ppermute x6, waiting for transfers between devices, swap(): lax.ppermute(pieces[k], 'sub', [(i, i ^ k) for i in range(subs)])  13.1 us
    pallas_call x1, Pallas kernels, azimuth_factors(): pl.pallas_call(factor_kernel, grid=(subs,), in_specs=[pl.BlockSpec(memory...  11.4 us
  transfers between devices with their start and end apart: 9, of which 5 were waited for; matrix products, arithmetic and copies ran while one was open for 1% of the time, Pallas kernels for 32%

profile of v4, /device:TPU:7, one launch (start us, length us, event | category | flops | bytes accessed | tf_op | source)
XLA Modules:
  0.0 218.6 jit_solution(8041128937063640811)
XLA Ops:
  0.0 0.0 copy-start
  0.0 0.8 broadcast_multiply_fusion
  0.8 0.1 mul.29
  0.8 0.1 copy.30
  0.9 0.7 pad_maximum_fusion.phase_ref
  1.6 4.8 %range_middle.1.t_ref = bf16[64,128,128]{2,1,0:T(8,128)(2,1)} custom-call(f32[64,128]{1,0:T(8,128)} %pad_maximum_fusion.phase_ref, bf16[64,128,128]{2,1,0:T(8,128)(2,1)} %constant.37.clone.wave_ref), custom_call_target="tpu_custom_call" | custom-call | tf_op jit(solution)/shard_map/range_middle/pallas_call | solution.py:61
  6.4 9.5 %range_compress.2 = bf16[128,2,32,128]{3,2,1,0:T(8,128)(2,1)} custom-call(bf16[2,4096,512]{2,1,0:T(8,128)(2,1)} %bitcast.14, bf16[128,128]{1,0:T(8,128)(2,1)} %constant.38.clone.w_ref, bf16[64,128,128]{2,1,0:T(8,128)(2,1)} %range_middle.1.t_ref, bf16[128,128]{1,0:T(8,128)(2,1)} %constant.39.clone.v_ref), custom_call_target="tpu_custom_call" | custom-call | tf_op jit(solution)/shard_map/range_compress/pallas_call | solution.py:145
  15.9 10.8 %all-to-all-start = ((bf16[128,2,32,128]{3,2,1,0:T(8,128)(2,1)}), bf16[128,2,32,128]{3,2,1,0:T(8,128)(2,1)S(1)}, u32[]{:S(2)}, u32[]{:S(2)}) async-start(bf16[128,2,32,128]{3,2,1,0:T(8,128)(2,1)} %range_compress.2), calls=%async_computation | async-start | bytes 4194304 | tf_op jit(solution)/shard_map/all_to_all | solution.py:494
  26.7 0.0 copy-done
  26.7 0.1 constant_dynamic-slice_fusion
  26.8 0.7 copy.32
  27.5 0.0 copy-done.9
  27.5 0.1 multiply_bitcast_fusion
  27.6 0.8 copy.31
  28.4 21.3 %range_compress.3 = (bf16[128,2,16,384]{3,2,1,0:T(8,128)(2,1)}, bf16[128,2,16,384]{3,2,1,0:T(8,128)(2,1)}) custom-call(bf16[2,4096,512]{2,1,0:T(8,128)(2,1)} %bitcast.15, bf16[128,128]{1,0:T(8,128)(2,1)} %constant.38.clone.w_ref, bf16[64,128,128]{2,1,0:T(8,128)(2,1)} %range_middle.1.t_ref, bf16[128,128]{1,0:T(8,128)(2,1)} %constant.39.clone.v_ref), custom_call_target="tpu_custom_call" | custom-call | tf_op jit(solution)/shard_map/range_compress/pallas_call | solution.py:145
  49.7 0.0 copy-done.10
  49.7 0.6 dynamic_slice.6.kappa_ref
  50.4 4.8 %all-to-all-done = bf16[128,2,32,128]{3,2,1,0:T(8,128)(2,1)S(1)} async-done(((bf16[128,2,32,128]{3,2,1,0:T(8,128)(2,1)}), bf16[128,2,32,128]{3,2,1,0:T(8,128)(2,1)S(1)}, u32[]{:S(2)}, u32[]{:S(2)}) %all-to-all-start) | async-done | bytes 2097184 | tf_op jit(solution)/shard_map/all_to_all | solution.py:494
  55.2 47.4 %all_to_all.15 = bf16[128,2,16,384]{3,2,1,0:T(8,128)(2,1)} all-to-all(bf16[128,2,16,384]{3,2,1,0:T(8,128)(2,1)} %get-tuple-element.36), channel_id=1, replica_groups=mesh['sub'=4,'pul'=32] {'pul','sub'}, dimensions={0} | all-to-all | bytes 6291456 | tf_op jit(solution)/shard_map/all_to_all | solution.py:494
  102.6 0.0 copy-done.1
  102.6 7.5 %all-to-all-start.2 = ((bf16[128,2,16,384]{3,2,1,0:T(8,128)(2,1)}), bf16[128,2,16,384]{3,2,1,0:T(8,128)(2,1)S(1)}, u32[]{:S(2)}, u32[]{:S(2)}) async-start(bf16[128,2,16,384]{3,2,1,0:T(8,128)(2,1)} %get-tuple-element.42), calls=%async_computation.2 | async-start | bytes 6291456 | tf_op jit(solution)/shard_map/all_to_all | solution.py:494
  110.2 8.8 %doppler_forward.2 = (bf16[4,4,16,2,32,128]{5,4,3,2,1,0:T(8,128)(2,1)}, bf16[4,4,8,2,32,128]{5,4,3,2,1,0:T(8,128)(2,1)}) custom-call(bf16[32,4,2,32,128]{4,3,2,1,0:T(8,128)(2,1)} %bitcast.16, bf16[32,4,2,16,384]{4,3,2,1,0:T(8,128)(2,1)} %bitcast.19, bf16[256,256]{1,0:T(8,128)(2,1)} %constant.40.clone.w_ref, f32[128,128]{1,0:T(8,128)} %constant.41.clone.cos_ref.refs_4_, ...), custom_call_target="tpu_custom_call" | custom-call | tf_op jit(solution)/shard_map/doppler_forward/pallas_call | solution.py:238
  118.9 11.4 %azimuth_factors.1.refs_2_ = bf16[4,4,32,2,32,128]{5,4,3,2,1,0:T(8,128)(2,1)} custom-call(f32[32]{0:T(128)} %dynamic_slice.6.kappa_ref, f32[4,128,128]{2,1,0:T(8,128)} %bitcast.23), custom_call_target="tpu_custom_call" | custom-call | tf_op jit(solution)/shard_map/azimuth_factors/pallas_call | solution.py:300
  130.3 5.4 %image_rows.3.refs_9_ = bf16[8,2,128,128]{3,2,1,0:T(8,128)(2,1)} custom-call(bf16[4,4,16,2,32,128]{5,4,3,2,1,0:T(8,128)(2,1)} %get-tuple-element.41.refs_0_.refs_1_, bf16[4,4,16,2,32,128]{5,4,3,2,1,0:T(8,128)(2,1)} %get-tuple-element.41.refs_0_.refs_1_, bf16[4,4,32,2,32,128]{5,4,3,2,1,0:T(8,128)(2,1)} %azimuth_factors.1.refs_2_, s32[128,128]{1,0:T(8,128)} %bitcast.20, ...), custom_call_target="tpu_custom_call" | custom-call | tf_op jit(solution)/shard_map/image_rows/pallas_call | solution.py:444
  135.7 2.3 %collective-permute-start.3 = (bf16[4,4,8,2,32,128]{5,4,3,2,1,0:T(8,128)(2,1)}, bf16[4,4,8,2,32,128]{5,4,3,2,1,0:T(8,128)(2,1)}, u32[]{:S(2)}, u32[]{:S(2)}) collective-permute-start(bf16[4,4,8,2,32,128]{5,4,3,2,1,0:T(8,128)(2,1)} %get-tuple-element.54), channel_id=1, source_target_pairs={{32,0},{64,32},{96,64},{1,96},{33,1},{65,33},{97,65},{2,97},{34,2}... | collective-permute-start | bytes 6291464 | tf_op jit(solution)/shard_map/ppermute | solution.py:526
  138.0 34.8 %all-to-all-done.2 = bf16[128,2,16,384]{3,2,1,0:T(8,128)(2,1)S(1)} async-done(((bf16[128,2,16,384]{3,2,1,0:T(8,128)(2,1)}), bf16[128,2,16,384]{3,2,1,0:T(8,128)(2,1)S(1)}, u32[]{:S(2)}, u32[]{:S(2)}) %all-to-all-start.2) | async-done | bytes 3145760 | tf_op jit(solution)/shard_map/all_to_all | solution.py:494
  172.8 1.6 copy-done.2
  174.4 8.2 %doppler_forward.3.refs_1_.refs_0_ = bf16[4,4,16,2,32,128]{5,4,3,2,1,0:T(8,128)(2,1)} custom-call(bf16[32,4,2,32,128]{4,3,2,1,0:T(8,128)(2,1)} %bitcast.17, bf16[32,4,2,16,384]{4,3,2,1,0:T(8,128)(2,1)} %bitcast.18, bf16[256,256]{1,0:T(8,128)(2,1)} %constant.40.clone.w_ref, f32[128,128]{1,0:T(8,128)} %constant.41.clone.cos_ref.refs_4_, ...), custom_call_target="tpu_custom_call" | custom-call | tf_op jit(solution)/shard_map/doppler_forward/pallas_call | solution.py:238
  182.6 6.4 %image_rows.4 = (bf16[2,16,4096]{2,1,0:T(8,128)(2,1)}, bf16[2,16,4096]{2,1,0:T(8,128)(2,1)}, bf16[2,16,4096]{2,1,0:T(8,128)(2,1)}, bf16[2,16,4096]{2,1,0:T(8,128)(2,1)}) custom-call(bf16[4,4,16,2,32,128]{5,4,3,2,1,0:T(8,128)(2,1)} %get-tuple-element.41.refs_0_.refs_1_, bf16[4,4,16,2,32,128]{5,4,3,2,1,0:T(8,128)(2,1)} %doppler_forward.3.refs_1_.refs_0_, ...), custom_call_target="tpu_custom_call" | custom-call | tf_op jit(solution)/shard_map/image_rows/pallas_call | solution.py:444
  189.1 1.0 collective-permute-start
  190.1 0.0 collective-permute-start.1
  190.1 1.7 collective-permute-start.2
  191.8 0.0 collective-permute-done.3.refs_1_
  191.8 8.1 %image_rows.5 = (bf16[2,16,4096]{2,1,0:T(8,128)(2,1)}, bf16[2,16,4096]{2,1,0:T(8,128)(2,1)}, bf16[2,16,4096]{2,1,0:T(8,128)(2,1)}, bf16[2,16,4096]{2,1,0:T(8,128)(2,1)}) custom-call(bf16[4,4,16,2,32,128]{5,4,3,2,1,0:T(8,128)(2,1)} %doppler_forward.3.refs_1_.refs_0_, bf16[4,4,8,2,32,128]{5,4,3,2,1,0:T(8,128)(2,1)} %collective-permute-done.3.refs_1_, ...), custom_call_target="tpu_custom_call" | custom-call | tf_op jit(solution)/shard_map/image_rows/pallas_call | solution.py:444
  199.9 0.2 collective-permute-start.4
  200.0 0.0 collective-permute-start.5
  200.1 0.0 collective-permute-done.refs_1_
  200.1 2.0 collective-permute-start.6
  202.0 0.0 collective-permute-done.1.refs_2_
  202.0 2.4 %collective-permute-done.2.refs_3_ = bf16[2,16,4096]{2,1,0:T(8,128)(2,1)S(1)} collective-permute-done((bf16[2,16,4096]{2,1,0:T(8,128)(2,1)}, bf16[2,16,4096]{2,1,0:T(8,128)(2,1)S(1)}, u32[]{:S(2)}, u32[]{:S(2)}) %collective-permute-start.2) | collective-permute-done | bytes 262176 | tf_op jit(solution)/shard_map/ppermute | solution.py:499
  204.4 0.0 collective-permute-done.4.refs_5_
  204.4 5.0 %collective-permute-done.5.refs_6_ = bf16[2,16,4096]{2,1,0:T(8,128)(2,1)S(1)} collective-permute-done((bf16[2,16,4096]{2,1,0:T(8,128)(2,1)}, bf16[2,16,4096]{2,1,0:T(8,128)(2,1)S(1)}, u32[]{:S(2)}, u32[]{:S(2)}) %collective-permute-start.5) | collective-permute-done | bytes 262176 | tf_op jit(solution)/shard_map/ppermute | solution.py:499
  209.4 5.8 %collective-permute-done.6.refs_7_ = bf16[2,16,4096]{2,1,0:T(8,128)(2,1)S(1)} collective-permute-done((bf16[2,16,4096]{2,1,0:T(8,128)(2,1)}, bf16[2,16,4096]{2,1,0:T(8,128)(2,1)S(1)}, u32[]{:S(2)}, u32[]{:S(2)}) %collective-permute-start.6) | collective-permute-done | bytes 262176 | tf_op jit(solution)/shard_map/ppermute | solution.py:499
  215.2 0.0 copy-done.3
  215.2 0.0 copy-done.4
  215.2 0.0 copy-done.5
  215.2 0.7 copy-done.8
  215.9 2.7 %place_rows.1 = bf16[2,128,4096]{2,1,0:T(8,128)(2,1)} custom-call(s32[1]{0:T(128)} %bitcast.refs_7_.mine_ref, bf16[2,16,4096]{2,1,0:T(8,128)(2,1)} %get-tuple-element.50.refs_0_, bf16[2,16,4096]{2,1,0:T(8,128)(2,1)} %copy-done.3, bf16[2,16,4096]{2,1,0:T(8,128)(2,1)} %copy-done.4, bf16[2,16,4096]{2,1,0:T(8,128)(2,1)} %copy-done.5, ...), custom_call_target="tpu_custom_call" | custom-call | tf_op jit(solution)/shard_map/place_rows/pallas_call | solution.py:468
  (13 shorter events, 0.0 us)
Async XLA Ops:
  0.0 26.7 %copy-start = (s32[4,16384]{1,0:T(4,128)S(1)}, s32[4,16384]{1,0:T(4,128)}, u32[]{:S(2)}) copy-start(s32[4,16384]{1,0:T(4,128)} %param.33) | copy-start | bytes 786436
  15.9 11.6 %copy-start.9 = (f32[4,16384]{1,0:T(4,128)S(1)}, f32[4,16384]{1,0:T(4,128)}, u32[]{:S(2)}) copy-start(f32[4,16384]{1,0:T(4,128)} %param.32) | copy-start | bytes 786436
  15.9 39.3 %all-to-all-start = ((bf16[128,2,32,128]{3,2,1,0:T(8,128)(2,1)}), bf16[128,2,32,128]{3,2,1,0:T(8,128)(2,1)S(1)}, u32[]{:S(2)}, u32[]{:S(2)}) async-start(bf16[128,2,32,128]{3,2,1,0:T(8,128)(2,1)} %range_compress.2), calls=%async_computation | async-start | bytes 4194304 | tf_op jit(solution)/shard_map/all_to_all | solution.py:494
  28.4 21.3 %copy-start.10 = (f32[128]{0:T(128)S(1)}, f32[128]{0:T(128)}, u32[]{:S(2)}) copy-start(f32[128]{0:T(128)} %param.31) | copy-start | bytes 1540
  55.2 47.4 %copy-start.1 = (bf16[128,2,32,128]{3,2,1,0:T(8,128)(2,1)}, bf16[128,2,32,128]{3,2,1,0:T(8,128)(2,1)S(1)}, u32[]{:S(2)}) copy-start(bf16[128,2,32,128]{3,2,1,0:T(8,128)(2,1)S(1)} %all-to-all-done) | copy-start | bytes 6291460
  102.6 70.2 %all-to-all-start.2 = ((bf16[128,2,16,384]{3,2,1,0:T(8,128)(2,1)}), bf16[128,2,16,384]{3,2,1,0:T(8,128)(2,1)S(1)}, u32[]{:S(2)}, u32[]{:S(2)}) async-start(bf16[128,2,16,384]{3,2,1,0:T(8,128)(2,1)} %get-tuple-element.42), calls=%async_computation.2 | async-start | bytes 6291456 | tf_op jit(solution)/shard_map/all_to_all | solution.py:494
  135.7 56.1 %collective-permute-start.3 = (bf16[4,4,8,2,32,128]{5,4,3,2,1,0:T(8,128)(2,1)}, bf16[4,4,8,2,32,128]{5,4,3,2,1,0:T(8,128)(2,1)}, u32[]{:S(2)}, u32[]{:S(2)}) collective-permute-start(bf16[4,4,8,2,32,128]{5,4,3,2,1,0:T(8,128)(2,1)} %get-tuple-element.54), channel_id=1, source_target_pairs={{32,0},{64,32},{96,64},{1,96},{33,1},{65,33},{97,65},{2,97},{34,2}... | collective-permute-start | bytes 6291464 | tf_op jit(solution)/shard_map/ppermute | solution.py:526
  172.8 1.6 copy-start.2
  189.1 11.0 %collective-permute-start = (bf16[2,16,4096]{2,1,0:T(8,128)(2,1)}, bf16[2,16,4096]{2,1,0:T(8,128)(2,1)S(1)}, u32[]{:S(2)}, u32[]{:S(2)}) collective-permute-start(bf16[2,16,4096]{2,1,0:T(8,128)(2,1)} %get-tuple-element.51), channel_id=1, source_target_pairs={{0,32},{32,0},{64,96},{96,64},{1,33},{33,1},{65,97},{97,65},{2,34}... | collective-permute-start | bytes 786440 | tf_op jit(solution)/shard_map/ppermute | solution.py:499
  190.1 12.0 %collective-permute-start.1 = (bf16[2,16,4096]{2,1,0:T(8,128)(2,1)}, bf16[2,16,4096]{2,1,0:T(8,128)(2,1)S(1)}, u32[]{:S(2)}, u32[]{:S(2)}) collective-permute-start(bf16[2,16,4096]{2,1,0:T(8,128)(2,1)} %get-tuple-element.52), channel_id=1, source_target_pairs={{0,64},{32,96},{64,0},{96,32},{1,65},{33,97},{65,1},{97,33},{2,66}... | collective-permute-start | bytes 786440 | tf_op jit(solution)/shard_map/ppermute | solution.py:499
  190.1 14.3 %collective-permute-start.2 = (bf16[2,16,4096]{2,1,0:T(8,128)(2,1)}, bf16[2,16,4096]{2,1,0:T(8,128)(2,1)S(1)}, u32[]{:S(2)}, u32[]{:S(2)}) collective-permute-start(bf16[2,16,4096]{2,1,0:T(8,128)(2,1)} %get-tuple-element.53), channel_id=1, source_target_pairs={{0,96},{32,64},{64,32},{96,0},{1,97},{33,65},{65,33},{97,1},{2,98}... | collective-permute-start | bytes 786440 | tf_op jit(solution)/shard_map/ppermute | solution.py:499
  199.9 4.5 %collective-permute-start.4 = (bf16[2,16,4096]{2,1,0:T(8,128)(2,1)}, bf16[2,16,4096]{2,1,0:T(8,128)(2,1)S(1)}, u32[]{:S(2)}, u32[]{:S(2)}) collective-permute-start(bf16[2,16,4096]{2,1,0:T(8,128)(2,1)} %get-tuple-element.56), channel_id=1, source_target_pairs={{0,32},{32,0},{64,96},{96,64},{1,33},{33,1},{65,97},{97,65},{2,34}... | collective-permute-start | bytes 786440 | tf_op jit(solution)/shard_map/ppermute | solution.py:499
  200.0 9.3 %collective-permute-start.5 = (bf16[2,16,4096]{2,1,0:T(8,128)(2,1)}, bf16[2,16,4096]{2,1,0:T(8,128)(2,1)S(1)}, u32[]{:S(2)}, u32[]{:S(2)}) collective-permute-start(bf16[2,16,4096]{2,1,0:T(8,128)(2,1)} %get-tuple-element.57), channel_id=1, source_target_pairs={{0,64},{32,96},{64,0},{96,32},{1,65},{33,97},{65,1},{97,33},{2,66}... | collective-permute-start | bytes 786440 | tf_op jit(solution)/shard_map/ppermute | solution.py:499
  200.1 15.1 %copy-start.3 = (bf16[2,16,4096]{2,1,0:T(8,128)(2,1)}, bf16[2,16,4096]{2,1,0:T(8,128)(2,1)S(1)}, u32[]{:S(2)}) copy-start(bf16[2,16,4096]{2,1,0:T(8,128)(2,1)S(1)} %collective-permute-done.refs_1_) | copy-start | bytes 786436
  200.1 15.1 %collective-permute-start.6 = (bf16[2,16,4096]{2,1,0:T(8,128)(2,1)}, bf16[2,16,4096]{2,1,0:T(8,128)(2,1)S(1)}, u32[]{:S(2)}, u32[]{:S(2)}) collective-permute-start(bf16[2,16,4096]{2,1,0:T(8,128)(2,1)} %get-tuple-element.58), channel_id=1, source_target_pairs={{0,96},{32,64},{64,32},{96,0},{1,97},{33,65},{65,33},{97,1},{2,98}... | collective-permute-start | bytes 786440 | tf_op jit(solution)/shard_map/ppermute | solution.py:499
  202.0 13.2 %copy-start.4 = (bf16[2,16,4096]{2,1,0:T(8,128)(2,1)}, bf16[2,16,4096]{2,1,0:T(8,128)(2,1)S(1)}, u32[]{:S(2)}) copy-start(bf16[2,16,4096]{2,1,0:T(8,128)(2,1)S(1)} %collective-permute-done.1.refs_2_) | copy-start | bytes 786436
  204.4 10.8 %copy-start.5 = (bf16[2,16,4096]{2,1,0:T(8,128)(2,1)}, bf16[2,16,4096]{2,1,0:T(8,128)(2,1)S(1)}, u32[]{:S(2)}) copy-start(bf16[2,16,4096]{2,1,0:T(8,128)(2,1)S(1)} %collective-permute-done.2.refs_3_) | copy-start | bytes 786436
  204.4 10.8 %copy-start.6 = (bf16[2,16,4096]{2,1,0:T(8,128)(2,1)}, bf16[2,16,4096]{2,1,0:T(8,128)(2,1)S(1)}, u32[]{:S(2)}) copy-start(bf16[2,16,4096]{2,1,0:T(8,128)(2,1)S(1)} %collective-permute-done.4.refs_5_) | copy-start | bytes 786436
  209.4 5.8 %copy-start.7 = (bf16[2,16,4096]{2,1,0:T(8,128)(2,1)}, bf16[2,16,4096]{2,1,0:T(8,128)(2,1)S(1)}, u32[]{:S(2)}) copy-start(bf16[2,16,4096]{2,1,0:T(8,128)(2,1)S(1)} %collective-permute-done.5.refs_6_) | copy-start | bytes 786436
  215.2 0.7 copy-start.8

commit v5 on v4

--- a/solution.py
+++ b/solution.py
@@ -522,9 +522,8 @@
     place = lambda block: (block % subs) * puls + block // subs
     pairs = [(place(block), place(block - 1)) for block in range(1, blocks)]
     top = image_rows(low, 0, MAXS, low, 1, factors, 0, shift, None, subs, [])
-    top, edge = lax.optimization_barrier((top, edge))
+    got_high, top, edge = lax.optimization_barrier((got_high, top, edge))
     rim = lax.ppermute(edge, ("sub", "pul"), pairs)
-    got_high, top = lax.optimization_barrier((got_high, top))
     (high,) = doppler_forward(first, got_high, 1, half, size, False)
     pieces = image_rows(low, 1, MAXS, high, 0, factors, 1, shift, mine, subs, [top])
     upper = swap(pieces)

time: 219 us -> 213 us (0.973); the launches traced: 219 us -> 210 us
  waiting for transfers between devices: 52.7 us -> 44.1 us
    all_to_all x2, waiting for transfers between devices: 39.6 us -> 19.4 us  [spread(): got = lax.all_to_all(sent, ('pul', 'sub'), 0, 0, tiled=True)]
    ppermute x1, waiting for transfers between devices: 0.01 us -> 13 us  [on_device(): rim = lax.ppermute(edge, ('sub', 'pul'), pairs)]
  transfers between devices with their start and end apart: 9 -> 9, of which waited for: 5 -> 5; matrix products, arithmetic and copies ran while one was open for 1% -> 1% of each run, Pallas kernels for 32% -> 33%
where the time goes in v5:
time: 213 us; the launch traced here: 210 us
  Pallas kernels  86.7 us (41%)
  blocking collectives  47.4 us (22%)
  waiting for transfers between devices  44.1 us (21%)
  starting transfers between devices  25.8 us (12%)
  local copies, waits for them, and re-layouts  4.51 us (2%)
    all_to_all x1, blocking collectives, spread(): got = lax.all_to_all(sent, ('pul', 'sub'), 0, 0, tiled=True)  47.4 us
    pallas_call x2, Pallas kernels, range_compress(): pl.pallas_call(functools.partial(range_kernel, size, splits), grid=(count...  30.8 us
    pallas_call x3, Pallas kernels, image_rows(): pl.pallas_call(functools.partial(image_kernel, len(before), finish), grid...  20.1 us
    all_to_all x2, waiting for transfers between devices, spread(): got = lax.all_to_all(sent, ('pul', 'sub'), 0, 0, tiled=True)  19.4 us
    all_to_all x2, starting transfers between devices, spread(): got = lax.all_to_all(sent, ('pul', 'sub'), 0, 0, tiled=True)  18.3 us
    pallas_call x2, Pallas kernels, doppler_forward(): pl.pallas_call(functools.partial(doppler_kernel, rows), grid=(subs,), in_...  17 us
    ppermute x1, waiting for transfers between devices, on_device(): rim = lax.ppermute(edge, ('sub', 'pul'), pairs)  13 us
    ppermute x6, waiting for transfers between devices, swap(): lax.ppermute(pieces[k], 'sub', [(i, i ^ k) for i in range(subs)])  11.8 us
  transfers between devices with their start and end apart: 9, of which 5 were waited for; matrix products, arithmetic and copies ran while one was open for 1% of the time, Pallas kernels for 33%

profile of v5, /device:TPU:7, one launch (start us, length us, event | category | flops | bytes accessed | tf_op | source)
XLA Modules:
  0.0 210.3 jit_solution(3217792092734514781)
XLA Ops:
  0.0 0.0 copy-start
  0.0 0.8 broadcast_multiply_fusion
  0.8 0.1 mul.29
  0.8 0.1 copy.30
  0.9 0.7 pad_maximum_fusion.phase_ref
  1.6 4.8 %range_middle.1.t_ref = bf16[64,128,128]{2,1,0:T(8,128)(2,1)} custom-call(f32[64,128]{1,0:T(8,128)} %pad_maximum_fusion.phase_ref, bf16[64,128,128]{2,1,0:T(8,128)(2,1)} %constant.37.clone.wave_ref), custom_call_target="tpu_custom_call" | custom-call | tf_op jit(solution)/shard_map/range_middle/pallas_call | solution.py:61
  6.4 9.5 %range_compress.2 = bf16[128,2,32,128]{3,2,1,0:T(8,128)(2,1)} custom-call(bf16[2,4096,512]{2,1,0:T(8,128)(2,1)} %bitcast.14, bf16[128,128]{1,0:T(8,128)(2,1)} %constant.38.clone.w_ref, bf16[64,128,128]{2,1,0:T(8,128)(2,1)} %range_middle.1.t_ref, bf16[128,128]{1,0:T(8,128)(2,1)} %constant.39.clone.v_ref), custom_call_target="tpu_custom_call" | custom-call | tf_op jit(solution)/shard_map/range_compress/pallas_call | solution.py:145
  15.9 10.8 %all-to-all-start = ((bf16[128,2,32,128]{3,2,1,0:T(8,128)(2,1)}), bf16[128,2,32,128]{3,2,1,0:T(8,128)(2,1)S(1)}, u32[]{:S(2)}, u32[]{:S(2)}) async-start(bf16[128,2,32,128]{3,2,1,0:T(8,128)(2,1)} %range_compress.2), calls=%async_computation | async-start | bytes 4194304 | tf_op jit(solution)/shard_map/all_to_all | solution.py:494
  26.7 0.0 copy-done
  26.7 0.1 constant_dynamic-slice_fusion
  26.8 0.7 copy.32
  27.5 0.0 copy-done.10
  27.5 0.1 multiply_bitcast_fusion
  27.6 0.8 copy.31
  28.5 21.3 %range_compress.3 = (bf16[128,2,16,384]{3,2,1,0:T(8,128)(2,1)}, bf16[128,2,16,384]{3,2,1,0:T(8,128)(2,1)}) custom-call(bf16[2,4096,512]{2,1,0:T(8,128)(2,1)} %bitcast.15, bf16[128,128]{1,0:T(8,128)(2,1)} %constant.38.clone.w_ref, bf16[64,128,128]{2,1,0:T(8,128)(2,1)} %range_middle.1.t_ref, bf16[128,128]{1,0:T(8,128)(2,1)} %constant.39.clone.v_ref), custom_call_target="tpu_custom_call" | custom-call | tf_op jit(solution)/shard_map/range_compress/pallas_call | solution.py:145
  49.8 0.0 copy-done.11
  49.8 0.7 dynamic_slice.6.kappa_ref
  50.4 4.8 %all-to-all-done = bf16[128,2,32,128]{3,2,1,0:T(8,128)(2,1)S(1)} async-done(((bf16[128,2,32,128]{3,2,1,0:T(8,128)(2,1)}), bf16[128,2,32,128]{3,2,1,0:T(8,128)(2,1)S(1)}, u32[]{:S(2)}, u32[]{:S(2)}) %all-to-all-start) | async-done | bytes 2097184 | tf_op jit(solution)/shard_map/all_to_all | solution.py:494
  55.2 47.4 %all_to_all.15 = bf16[128,2,16,384]{3,2,1,0:T(8,128)(2,1)} all-to-all(bf16[128,2,16,384]{3,2,1,0:T(8,128)(2,1)} %get-tuple-element.35), channel_id=1, replica_groups=mesh['sub'=4,'pul'=32] {'pul','sub'}, dimensions={0} | all-to-all | bytes 6291456 | tf_op jit(solution)/shard_map/all_to_all | solution.py:494
  102.6 0.0 copy-done.1
  102.6 7.5 %all-to-all-start.2 = ((bf16[128,2,16,384]{3,2,1,0:T(8,128)(2,1)}), bf16[128,2,16,384]{3,2,1,0:T(8,128)(2,1)S(1)}, u32[]{:S(2)}, u32[]{:S(2)}) async-start(bf16[128,2,16,384]{3,2,1,0:T(8,128)(2,1)} %get-tuple-element.41), calls=%async_computation.2 | async-start | bytes 6291456 | tf_op jit(solution)/shard_map/all_to_all | solution.py:494
  110.2 8.7 %doppler_forward.2 = (bf16[4,4,16,2,32,128]{5,4,3,2,1,0:T(8,128)(2,1)}, bf16[4,4,8,2,32,128]{5,4,3,2,1,0:T(8,128)(2,1)}) custom-call(bf16[32,4,2,32,128]{4,3,2,1,0:T(8,128)(2,1)} %bitcast.16, bf16[32,4,2,16,384]{4,3,2,1,0:T(8,128)(2,1)} %bitcast.19, bf16[256,256]{1,0:T(8,128)(2,1)} %constant.40.clone.w_ref, f32[128,128]{1,0:T(8,128)} %constant.41.clone.cos_ref.refs_4_, ...), custom_call_target="tpu_custom_call" | custom-call | tf_op jit(solution)/shard_map/doppler_forward/pallas_call | solution.py:238
  118.9 11.4 %azimuth_factors.1.refs_2_ = bf16[4,4,32,2,32,128]{5,4,3,2,1,0:T(8,128)(2,1)} custom-call(f32[32]{0:T(128)} %dynamic_slice.6.kappa_ref, f32[4,128,128]{2,1,0:T(8,128)} %bitcast.23), custom_call_target="tpu_custom_call" | custom-call | tf_op jit(solution)/shard_map/azimuth_factors/pallas_call | solution.py:300
  130.3 5.4 %image_rows.3.refs_9_ = bf16[8,2,128,128]{3,2,1,0:T(8,128)(2,1)} custom-call(bf16[4,4,16,2,32,128]{5,4,3,2,1,0:T(8,128)(2,1)} %get-tuple-element.40.refs_0_.refs_1_, bf16[4,4,16,2,32,128]{5,4,3,2,1,0:T(8,128)(2,1)} %get-tuple-element.40.refs_0_.refs_1_, bf16[4,4,32,2,32,128]{5,4,3,2,1,0:T(8,128)(2,1)} %azimuth_factors.1.refs_2_, s32[128,128]{1,0:T(8,128)} %bitcast.20, ...), custom_call_target="tpu_custom_call" | custom-call | tf_op jit(solution)/shard_map/image_rows/pallas_call | solution.py:444
  135.7 14.6 %all-to-all-done.2 = bf16[128,2,16,384]{3,2,1,0:T(8,128)(2,1)S(1)} async-done(((bf16[128,2,16,384]{3,2,1,0:T(8,128)(2,1)}), bf16[128,2,16,384]{3,2,1,0:T(8,128)(2,1)S(1)}, u32[]{:S(2)}, u32[]{:S(2)}) %all-to-all-start.2) | async-done | bytes 3145760 | tf_op jit(solution)/shard_map/all_to_all | solution.py:494
  150.3 2.9 %collective-permute-start.3 = (bf16[4,4,8,2,32,128]{5,4,3,2,1,0:T(8,128)(2,1)}, bf16[4,4,8,2,32,128]{5,4,3,2,1,0:T(8,128)(2,1)S(1)}, u32[]{:S(2)}, u32[]{:S(2)}) collective-permute-start(bf16[4,4,8,2,32,128]{5,4,3,2,1,0:T(8,128)(2,1)} %get-tuple-element.52), channel_id=1, source_target_pairs={{32,0},{64,32},{96,64},{1,96},{33,1},{65,33},{97,65},{2,97},{34,2}... | collective-permute-start | bytes 6291464 | tf_op jit(solution)/shard_map/ppermute | solution.py:526
  153.2 0.0 copy-done.2
  153.3 8.2 %doppler_forward.3.refs_1_.refs_0_ = bf16[4,4,16,2,32,128]{5,4,3,2,1,0:T(8,128)(2,1)} custom-call(bf16[32,4,2,32,128]{4,3,2,1,0:T(8,128)(2,1)} %bitcast.17, bf16[32,4,2,16,384]{4,3,2,1,0:T(8,128)(2,1)} %bitcast.18, bf16[256,256]{1,0:T(8,128)(2,1)} %constant.40.clone.w_ref, f32[128,128]{1,0:T(8,128)} %constant.41.clone.cos_ref.refs_4_, ...), custom_call_target="tpu_custom_call" | custom-call | tf_op jit(solution)/shard_map/doppler_forward/pallas_call | solution.py:238
  161.5 6.5 %image_rows.4 = (bf16[2,16,4096]{2,1,0:T(8,128)(2,1)}, bf16[2,16,4096]{2,1,0:T(8,128)(2,1)}, bf16[2,16,4096]{2,1,0:T(8,128)(2,1)}, bf16[2,16,4096]{2,1,0:T(8,128)(2,1)}) custom-call(bf16[4,4,16,2,32,128]{5,4,3,2,1,0:T(8,128)(2,1)} %get-tuple-element.40.refs_0_.refs_1_, bf16[4,4,16,2,32,128]{5,4,3,2,1,0:T(8,128)(2,1)} %doppler_forward.3.refs_1_.refs_0_, ...), custom_call_target="tpu_custom_call" | custom-call | tf_op jit(solution)/shard_map/image_rows/pallas_call | solution.py:444
  168.0 0.8 collective-permute-start
  168.8 0.1 collective-permute-start.1
  168.9 1.6 collective-permute-start.2
  170.5 13.0 %collective-permute-done.3.refs_1_ = bf16[4,4,8,2,32,128]{5,4,3,2,1,0:T(8,128)(2,1)S(1)} collective-permute-done((bf16[4,4,8,2,32,128]{5,4,3,2,1,0:T(8,128)(2,1)}, bf16[4,4,8,2,32,128]{5,4,3,2,1,0:T(8,128)(2,1)S(1)}, u32[]{:S(2)}, u32[]{:S(2)}) %collective-permute-start.3) | collective-permute-done | bytes 2097184 | tf_op jit(solution)/shard_map/ppermute | solution.py:526
  183.5 1.3 copy-done.3
  184.8 8.1 %image_rows.5 = (bf16[2,16,4096]{2,1,0:T(8,128)(2,1)}, bf16[2,16,4096]{2,1,0:T(8,128)(2,1)}, bf16[2,16,4096]{2,1,0:T(8,128)(2,1)}, bf16[2,16,4096]{2,1,0:T(8,128)(2,1)}) custom-call(bf16[4,4,16,2,32,128]{5,4,3,2,1,0:T(8,128)(2,1)} %doppler_forward.3.refs_1_.refs_0_, bf16[4,4,8,2,32,128]{5,4,3,2,1,0:T(8,128)(2,1)} %copy-done.3, ...), custom_call_target="tpu_custom_call" | custom-call | tf_op jit(solution)/shard_map/image_rows/pallas_call | solution.py:444
  193.0 0.0 collective-permute-start.4
  193.0 0.1 collective-permute-start.5
  193.1 0.0 collective-permute-done.refs_1_
  193.1 2.0 collective-permute-start.6
  195.1 0.0 collective-permute-done.1.refs_2_
  195.1 0.0 collective-permute-done.2.refs_3_
  195.1 0.0 collective-permute-done.4.refs_5_
  195.2 5.6 %collective-permute-done.5.refs_6_ = bf16[2,16,4096]{2,1,0:T(8,128)(2,1)S(1)} collective-permute-done((bf16[2,16,4096]{2,1,0:T(8,128)(2,1)}, bf16[2,16,4096]{2,1,0:T(8,128)(2,1)S(1)}, u32[]{:S(2)}, u32[]{:S(2)}) %collective-permute-start.5) | collective-permute-done | bytes 262176 | tf_op jit(solution)/shard_map/ppermute | solution.py:499
  200.7 6.2 %collective-permute-done.6.refs_7_ = bf16[2,16,4096]{2,1,0:T(8,128)(2,1)S(1)} collective-permute-done((bf16[2,16,4096]{2,1,0:T(8,128)(2,1)}, bf16[2,16,4096]{2,1,0:T(8,128)(2,1)S(1)}, u32[]{:S(2)}, u32[]{:S(2)}) %collective-permute-start.6) | collective-permute-done | bytes 262176 | tf_op jit(solution)/shard_map/ppermute | solution.py:499
  206.9 0.0 copy-done.4
  206.9 0.0 copy-done.6
  207.0 0.7 copy-done.9
  207.6 2.7 %place_rows.1 = bf16[2,128,4096]{2,1,0:T(8,128)(2,1)} custom-call(s32[1]{0:T(128)} %bitcast.refs_7_.mine_ref, bf16[2,16,4096]{2,1,0:T(8,128)(2,1)} %get-tuple-element.48.refs_0_, bf16[2,16,4096]{2,1,0:T(8,128)(2,1)} %copy-done.4, bf16[2,16,4096]{2,1,0:T(8,128)(2,1)} %copy-done.5, bf16[2,16,4096]{2,1,0:T(8,128)(2,1)} %copy-done.6, ...), custom_call_target="tpu_custom_call" | custom-call | tf_op jit(solution)/shard_map/place_rows/pallas_call | solution.py:468
  (15 shorter events, 0.0 us)
Async XLA Ops:
  0.0 26.7 %copy-start = (s32[4,16384]{1,0:T(4,128)S(1)}, s32[4,16384]{1,0:T(4,128)}, u32[]{:S(2)}) copy-start(s32[4,16384]{1,0:T(4,128)} %param.33) | copy-start | bytes 786436
  15.9 11.6 %copy-start.10 = (f32[4,16384]{1,0:T(4,128)S(1)}, f32[4,16384]{1,0:T(4,128)}, u32[]{:S(2)}) copy-start(f32[4,16384]{1,0:T(4,128)} %param.32) | copy-start | bytes 786436
  15.9 39.3 %all-to-all-start = ((bf16[128,2,32,128]{3,2,1,0:T(8,128)(2,1)}), bf16[128,2,32,128]{3,2,1,0:T(8,128)(2,1)S(1)}, u32[]{:S(2)}, u32[]{:S(2)}) async-start(bf16[128,2,32,128]{3,2,1,0:T(8,128)(2,1)} %range_compress.2), calls=%async_computation | async-start | bytes 4194304 | tf_op jit(solution)/shard_map/all_to_all | solution.py:494
  28.4 21.3 %copy-start.11 = (f32[128]{0:T(128)S(1)}, f32[128]{0:T(128)}, u32[]{:S(2)}) copy-start(f32[128]{0:T(128)} %param.31) | copy-start | bytes 1540
  55.2 47.4 %copy-start.1 = (bf16[128,2,32,128]{3,2,1,0:T(8,128)(2,1)}, bf16[128,2,32,128]{3,2,1,0:T(8,128)(2,1)S(1)}, u32[]{:S(2)}) copy-start(bf16[128,2,32,128]{3,2,1,0:T(8,128)(2,1)S(1)} %all-to-all-done) | copy-start | bytes 6291460
  102.6 47.7 %all-to-all-start.2 = ((bf16[128,2,16,384]{3,2,1,0:T(8,128)(2,1)}), bf16[128,2,16,384]{3,2,1,0:T(8,128)(2,1)S(1)}, u32[]{:S(2)}, u32[]{:S(2)}) async-start(bf16[128,2,16,384]{3,2,1,0:T(8,128)(2,1)} %get-tuple-element.41), calls=%async_computation.2 | async-start | bytes 6291456 | tf_op jit(solution)/shard_map/all_to_all | solution.py:494
  150.3 2.9 %copy-start.2 = (bf16[128,2,16,384]{3,2,1,0:T(8,128)(2,1)}, bf16[128,2,16,384]{3,2,1,0:T(8,128)(2,1)S(1)}, u32[]{:S(2)}) copy-start(bf16[128,2,16,384]{3,2,1,0:T(8,128)(2,1)S(1)} %all-to-all-done.2) | copy-start | bytes 9437188
  150.3 33.2 %collective-permute-start.3 = (bf16[4,4,8,2,32,128]{5,4,3,2,1,0:T(8,128)(2,1)}, bf16[4,4,8,2,32,128]{5,4,3,2,1,0:T(8,128)(2,1)S(1)}, u32[]{:S(2)}, u32[]{:S(2)}) collective-permute-start(bf16[4,4,8,2,32,128]{5,4,3,2,1,0:T(8,128)(2,1)} %get-tuple-element.52), channel_id=1, source_target_pairs={{32,0},{64,32},{96,64},{1,96},{33,1},{65,33},{97,65},{2,97},{34,2}... | collective-permute-start | bytes 6291464 | tf_op jit(solution)/shard_map/ppermute | solution.py:526
  168.0 25.1 %collective-permute-start = (bf16[2,16,4096]{2,1,0:T(8,128)(2,1)}, bf16[2,16,4096]{2,1,0:T(8,128)(2,1)S(1)}, u32[]{:S(2)}, u32[]{:S(2)}) collective-permute-start(bf16[2,16,4096]{2,1,0:T(8,128)(2,1)} %get-tuple-element.49), channel_id=1, source_target_pairs={{0,32},{32,0},{64,96},{96,64},{1,33},{33,1},{65,97},{97,65},{2,34}... | collective-permute-start | bytes 786440 | tf_op jit(solution)/shard_map/ppermute | solution.py:499
  168.8 26.3 %collective-permute-start.1 = (bf16[2,16,4096]{2,1,0:T(8,128)(2,1)}, bf16[2,16,4096]{2,1,0:T(8,128)(2,1)S(1)}, u32[]{:S(2)}, u32[]{:S(2)}) collective-permute-start(bf16[2,16,4096]{2,1,0:T(8,128)(2,1)} %get-tuple-element.50), channel_id=1, source_target_pairs={{0,64},{32,96},{64,0},{96,32},{1,65},{33,97},{65,1},{97,33},{2,66}... | collective-permute-start | bytes 786440 | tf_op jit(solution)/shard_map/ppermute | solution.py:499
  168.9 26.3 %collective-permute-start.2 = (bf16[2,16,4096]{2,1,0:T(8,128)(2,1)}, bf16[2,16,4096]{2,1,0:T(8,128)(2,1)S(1)}, u32[]{:S(2)}, u32[]{:S(2)}) collective-permute-start(bf16[2,16,4096]{2,1,0:T(8,128)(2,1)} %get-tuple-element.51), channel_id=1, source_target_pairs={{0,96},{32,64},{64,32},{96,0},{1,97},{33,65},{65,33},{97,1},{2,98}... | collective-permute-start | bytes 786440 | tf_op jit(solution)/shard_map/ppermute | solution.py:499
  183.5 1.3 copy-start.3
  193.0 2.2 %collective-permute-start.4 = (bf16[2,16,4096]{2,1,0:T(8,128)(2,1)}, bf16[2,16,4096]{2,1,0:T(8,128)(2,1)S(1)}, u32[]{:S(2)}, u32[]{:S(2)}) collective-permute-start(bf16[2,16,4096]{2,1,0:T(8,128)(2,1)} %get-tuple-element.54), channel_id=1, source_target_pairs={{0,32},{32,0},{64,96},{96,64},{1,33},{33,1},{65,97},{97,65},{2,34}... | collective-permute-start | bytes 786440 | tf_op jit(solution)/shard_map/ppermute | solution.py:499
  193.0 7.7 %collective-permute-start.5 = (bf16[2,16,4096]{2,1,0:T(8,128)(2,1)}, bf16[2,16,4096]{2,1,0:T(8,128)(2,1)S(1)}, u32[]{:S(2)}, u32[]{:S(2)}) collective-permute-start(bf16[2,16,4096]{2,1,0:T(8,128)(2,1)} %get-tuple-element.55), channel_id=1, source_target_pairs={{0,64},{32,96},{64,0},{96,32},{1,65},{33,97},{65,1},{97,33},{2,66}... | collective-permute-start | bytes 786440 | tf_op jit(solution)/shard_map/ppermute | solution.py:499
  193.1 13.8 %copy-start.4 = (bf16[2,16,4096]{2,1,0:T(8,128)(2,1)}, bf16[2,16,4096]{2,1,0:T(8,128)(2,1)S(1)}, u32[]{:S(2)}) copy-start(bf16[2,16,4096]{2,1,0:T(8,128)(2,1)S(1)} %collective-permute-done.refs_1_) | copy-start | bytes 786436
  193.1 13.8 %collective-permute-start.6 = (bf16[2,16,4096]{2,1,0:T(8,128)(2,1)}, bf16[2,16,4096]{2,1,0:T(8,128)(2,1)S(1)}, u32[]{:S(2)}, u32[]{:S(2)}) collective-permute-start(bf16[2,16,4096]{2,1,0:T(8,128)(2,1)} %get-tuple-element.56), channel_id=1, source_target_pairs={{0,96},{32,64},{64,32},{96,0},{1,97},{33,65},{65,33},{97,1},{2,98}... | collective-permute-start | bytes 786440 | tf_op jit(solution)/shard_map/ppermute | solution.py:499
  195.1 11.8 %copy-start.5 = (bf16[2,16,4096]{2,1,0:T(8,128)(2,1)}, bf16[2,16,4096]{2,1,0:T(8,128)(2,1)S(1)}, u32[]{:S(2)}) copy-start(bf16[2,16,4096]{2,1,0:T(8,128)(2,1)S(1)} %collective-permute-done.1.refs_2_) | copy-start | bytes 786436
  195.1 11.8 %copy-start.6 = (bf16[2,16,4096]{2,1,0:T(8,128)(2,1)}, bf16[2,16,4096]{2,1,0:T(8,128)(2,1)S(1)}, u32[]{:S(2)}) copy-start(bf16[2,16,4096]{2,1,0:T(8,128)(2,1)S(1)} %collective-permute-done.2.refs_3_) | copy-start | bytes 786436
  195.1 11.8 %copy-start.7 = (bf16[2,16,4096]{2,1,0:T(8,128)(2,1)}, bf16[2,16,4096]{2,1,0:T(8,128)(2,1)S(1)}, u32[]{:S(2)}) copy-start(bf16[2,16,4096]{2,1,0:T(8,128)(2,1)S(1)} %collective-permute-done.4.refs_5_) | copy-start | bytes 786436
  200.7 6.2 %copy-start.8 = (bf16[2,16,4096]{2,1,0:T(8,128)(2,1)}, bf16[2,16,4096]{2,1,0:T(8,128)(2,1)S(1)}, u32[]{:S(2)}) copy-start(bf16[2,16,4096]{2,1,0:T(8,128)(2,1)S(1)} %collective-permute-done.5.refs_6_) | copy-start | bytes 786436
  206.9 0.7 copy-start.9

commit v6 on v4

--- a/solution.py
+++ b/solution.py
@@ -164,15 +164,14 @@
     sources = first.shape[0]
     size = cos_ref.shape[0]
     lines = size // sources
+    early = first.shape[4] // LANES
     pitch = rows + 1
 
     def cast(source, carry):
         for line in range(lines):
             for c in range(2):
-                if line == 0:
-                    value = first[source, 0, c]
-                else:
-                    value = rest[source, 0, c, :, (line - 1) * LANES : line * LANES]
+                part, at = (first, line) if line < early else (rest, line - early)
+                value = part[source, 0, c, :, at * LANES : (at + 1) * LANES]
                 base = (c * lines + line) * sources
                 held[pl.ds((base + source) * pitch, rows), :] = value.astype(F32)
         return carry
@@ -239,7 +238,9 @@
         functools.partial(doppler_kernel, rows),
         grid=(subs,),
         in_specs=[
-            pl.BlockSpec((sources, 1, 2, rows, LANES), lambda i: (0, i, 0, part, 0)),
+            pl.BlockSpec(
+                (sources, 1, 2, rows, first.shape[4]), lambda i: (0, i, 0, part, 0)
+            ),
             pl.BlockSpec((sources, 1, 2, rows, width), lambda i: (0, i, 0, 0, 0)),
             whole(2 * size, 2 * size),
             whole(size, size),
@@ -501,29 +502,26 @@
         ]
         return [pieces[0]] + sent[::-1]
 
-    (sent,) = range_compress(echo, middle, 0, 1, blocks, 1)
+    early = pulse_dev // LANES // 2
+    (sent,) = range_compress(echo, middle, 0, early, blocks, 1)
     sent, echo = lax.optimization_barrier((sent, echo))
     first = spread(sent)
-    count = pulse_dev // LANES - 1
-    sent_low, sent_high = range_compress(echo, middle, 1, count, blocks, 2)
+    count = pulse_dev // LANES - early
+    sent_low, sent_high = range_compress(echo, middle, early, count, blocks, 2)
     own_shift = lax.dynamic_slice_in_dim(migration, sub_index, 1, 0)
     shift = own_shift.reshape(size, size).T
     phase = jnp.swapaxes(doppler.reshape(subs, size, size), 1, 2) * (0.5 / math.pi)
     own_kappa = lax.dynamic_slice_in_dim(kappa, sub_index * rows, rows, 0)
-    first, sent_low, phase, own_kappa, shift = lax.optimization_barrier(
-        (first, sent_low, phase, own_kappa, shift)
-    )
+    factors = azimuth_factors(own_kappa, phase)
+    first, sent_low, factors, shift = lax.optimization_barrier((first, sent_low, factors, shift))
     got_low = spread(sent_low)
     got_low, sent_high = lax.optimization_barrier((got_low, sent_high))
     got_high = spread(sent_high)
     low, edge = doppler_forward(first, got_low, 0, half, size, True)
-    low, own_kappa = lax.optimization_barrier((low, own_kappa))
-    factors = azimuth_factors(own_kappa, phase)
     place = lambda block: (block % subs) * puls + block // subs
     pairs = [(place(block), place(block - 1)) for block in range(1, blocks)]
+    rim = lax.ppermute(edge, ("sub", "pul"), pairs)
     top = image_rows(low, 0, MAXS, low, 1, factors, 0, shift, None, subs, [])
-    top, edge = lax.optimization_barrier((top, edge))
-    rim = lax.ppermute(edge, ("sub", "pul"), pairs)
     got_high, top = lax.optimization_barrier((got_high, top))
     (high,) = doppler_forward(first, got_high, 1, half, size, False)
     pieces = image_rows(low, 1, MAXS, high, 0, factors, 1, shift, mine, subs, [top])

time: 219 us -> 206 us (0.941); the launches traced: 219 us -> 202 us
  blocking collectives: 47.4 us -> 35.4 us
  waiting for transfers between devices: 52.7 us -> 48.8 us
    all_to_all x1, blocking collectives: 47.4 us -> 35.4 us  [spread(): got = lax.all_to_all(sent, ('pul', 'sub'), 0, 0, tiled=True)]
    all_to_all x2, waiting for transfers between devices: 39.6 us -> 35.6 us  [spread(): got = lax.all_to_all(sent, ('pul', 'sub'), 0, 0, tiled=True)]
where the time goes in v6:
time: 206 us; the launch traced here: 202 us
  Pallas kernels  86.6 us (42%)
  waiting for transfers between devices  48.8 us (24%)
  blocking collectives  35.4 us (17%)
  starting transfers between devices  25.5 us (12%)
  local copies, waits for them, and re-layouts  4.44 us (2%)
    all_to_all x2, waiting for transfers between devices, spread(): got = lax.all_to_all(sent, ('pul', 'sub'), 0, 0, tiled=True)  35.6 us
    all_to_all x1, blocking collectives, spread(): got = lax.all_to_all(sent, ('pul', 'sub'), 0, 0, tiled=True)  35.4 us
    pallas_call x2, Pallas kernels, range_compress(): pl.pallas_call(functools.partial(range_kernel, size, splits), grid=(count...  30.8 us
    pallas_call x3, Pallas kernels, image_rows(): pl.pallas_call(functools.partial(image_kernel, len(before), finish), grid...  20 us
    all_to_all x2, starting transfers between devices, spread(): got = lax.all_to_all(sent, ('pul', 'sub'), 0, 0, tiled=True)  18.3 us
    pallas_call x2, Pallas kernels, doppler_forward(): pl.pallas_call(functools.partial(doppler_kernel, rows), grid=(subs,), in_...  16.8 us
    ppermute x6, waiting for transfers between devices, swap(): lax.ppermute(pieces[k], 'sub', [(i, i ^ k) for i in range(subs)])  13.1 us
    pallas_call x1, Pallas kernels, azimuth_factors(): pl.pallas_call(factor_kernel, grid=(subs,), in_specs=[pl.BlockSpec(memory...  11.5 us
  transfers between devices with their start and end apart: 9, of which 5 were waited for; matrix products, arithmetic and copies ran while one was open for 1% of the time, Pallas kernels for 32%

profile of v6, /device:TPU:7, one launch (start us, length us, event | category | flops | bytes accessed | tf_op | source)
XLA Modules:
  0.0 202.4 jit_solution(14373874594627450466)
XLA Ops:
  0.0 0.0 copy-start
  0.0 0.8 broadcast_multiply_fusion
  0.8 0.1 mul.27
  0.8 0.1 copy.30
  0.9 0.7 pad_maximum_fusion.phase_ref
  1.6 4.8 %range_middle.1.t_ref = bf16[64,128,128]{2,1,0:T(8,128)(2,1)} custom-call(f32[64,128]{1,0:T(8,128)} %pad_maximum_fusion.phase_ref, bf16[64,128,128]{2,1,0:T(8,128)(2,1)} %constant.37.clone.wave_ref), custom_call_target="tpu_custom_call" | custom-call | tf_op jit(solution)/shard_map/range_middle/pallas_call | solution.py:61
  6.4 15.3 %range_compress.2 = bf16[128,2,32,256]{3,2,1,0:T(8,128)(2,1)} custom-call(bf16[2,4096,512]{2,1,0:T(8,128)(2,1)} %bitcast.14, bf16[128,128]{1,0:T(8,128)(2,1)} %constant.38.clone.w_ref, bf16[64,128,128]{2,1,0:T(8,128)(2,1)} %range_middle.1.t_ref, bf16[128,128]{1,0:T(8,128)(2,1)} %constant.39.clone.v_ref), custom_call_target="tpu_custom_call" | custom-call | tf_op jit(solution)/shard_map/range_compress/pallas_call | solution.py:145
  21.7 11.2 %all-to-all-start = ((bf16[128,2,32,256]{3,2,1,0:T(8,128)(2,1)}), bf16[128,2,32,256]{3,2,1,0:T(8,128)(2,1)}, u32[]{:S(2)}, u32[]{:S(2)}) async-start(bf16[128,2,32,256]{3,2,1,0:T(8,128)(2,1)} %range_compress.2), calls=%async_computation | async-start | bytes 8388608 | tf_op jit(solution)/shard_map/all_to_all | solution.py:495
  33.0 0.0 copy-done
  33.0 0.1 constant_dynamic-slice_fusion
  33.1 0.7 copy.32
  33.8 0.0 copy-done.9
  33.8 0.1 multiply_bitcast_fusion
  33.9 0.8 copy.31
  34.7 15.4 %range_compress.3 = (bf16[128,2,16,256]{3,2,1,0:T(8,128)(2,1)}, bf16[128,2,16,256]{3,2,1,0:T(8,128)(2,1)}) custom-call(bf16[2,4096,512]{2,1,0:T(8,128)(2,1)} %bitcast.15, bf16[128,128]{1,0:T(8,128)(2,1)} %constant.38.clone.w_ref, bf16[64,128,128]{2,1,0:T(8,128)(2,1)} %range_middle.1.t_ref, bf16[128,128]{1,0:T(8,128)(2,1)} %constant.39.clone.v_ref), custom_call_target="tpu_custom_call" | custom-call | tf_op jit(solution)/shard_map/range_compress/pallas_call | solution.py:145
  50.2 0.0 copy-done.10
  50.2 0.6 dynamic_slice.6.kappa_ref
  50.8 11.5 %azimuth_factors.1.refs_2_ = bf16[4,4,32,2,32,128]{5,4,3,2,1,0:T(8,128)(2,1)} custom-call(f32[32]{0:T(128)} %dynamic_slice.6.kappa_ref, f32[4,128,128]{2,1,0:T(8,128)} %bitcast.21), custom_call_target="tpu_custom_call" | custom-call | tf_op jit(solution)/shard_map/azimuth_factors/pallas_call | solution.py:301
  62.3 23.1 %all-to-all-done = bf16[128,2,32,256]{3,2,1,0:T(8,128)(2,1)} async-done(((bf16[128,2,32,256]{3,2,1,0:T(8,128)(2,1)}), bf16[128,2,32,256]{3,2,1,0:T(8,128)(2,1)}, u32[]{:S(2)}, u32[]{:S(2)}) %all-to-all-start) | async-done | bytes 4194336 | tf_op jit(solution)/shard_map/all_to_all | solution.py:495
  85.4 0.0 copy-done.2
  85.4 35.4 %all_to_all.15 = bf16[128,2,16,256]{3,2,1,0:T(8,128)(2,1)} all-to-all(bf16[128,2,16,256]{3,2,1,0:T(8,128)(2,1)S(1)} %copy-done.2), channel_id=1, replica_groups=mesh['sub'=4,'pul'=32] {'pul','sub'}, dimensions={0} | all-to-all | bytes 4194304 | tf_op jit(solution)/shard_map/all_to_all | solution.py:495
  120.8 7.0 %all-to-all-start.2 = ((bf16[128,2,16,256]{3,2,1,0:T(8,128)(2,1)}), bf16[128,2,16,256]{3,2,1,0:T(8,128)(2,1)S(1)}, u32[]{:S(2)}, u32[]{:S(2)}) async-start(bf16[128,2,16,256]{3,2,1,0:T(8,128)(2,1)} %get-tuple-element.35), calls=%async_computation.2 | async-start | bytes 4194304 | tf_op jit(solution)/shard_map/all_to_all | solution.py:495
  127.9 8.7 %doppler_forward.2 = (bf16[4,4,16,2,32,128]{5,4,3,2,1,0:T(8,128)(2,1)}, bf16[4,4,8,2,32,128]{5,4,3,2,1,0:T(8,128)(2,1)}) custom-call(bf16[32,4,2,32,256]{4,3,2,1,0:T(8,128)(2,1)} %bitcast.3.first, bf16[32,4,2,16,256]{4,3,2,1,0:T(8,128)(2,1)} %bitcast.16, bf16[256,256]{1,0:T(8,128)(2,1)} %constant.40.clone.w_ref, f32[128,128]{1,0:T(8,128)} %constant.41.clone.cos_ref.refs_4_, ...), custom_call_target="tpu_custom_call" | custom-call | tf_op jit(solution)/shard_map/doppler_forward/pallas_call | solution.py:237
  136.5 2.3 %collective-permute-start.3 = (bf16[4,4,8,2,32,128]{5,4,3,2,1,0:T(8,128)(2,1)}, bf16[4,4,8,2,32,128]{5,4,3,2,1,0:T(8,128)(2,1)}, u32[]{:S(2)}, u32[]{:S(2)}) collective-permute-start(bf16[4,4,8,2,32,128]{5,4,3,2,1,0:T(8,128)(2,1)} %get-tuple-element.44), channel_id=1, source_target_pairs={{32,0},{64,32},{96,64},{1,96},{33,1},{65,33},{97,65},{2,97},{34,2}... | collective-permute-start | bytes 6291464 | tf_op jit(solution)/shard_map/ppermute | solution.py:523
  138.8 5.4 %image_rows.3.refs_9_ = bf16[8,2,128,128]{3,2,1,0:T(8,128)(2,1)} custom-call(bf16[4,4,16,2,32,128]{5,4,3,2,1,0:T(8,128)(2,1)} %get-tuple-element.34.refs_0_.refs_1_, bf16[4,4,16,2,32,128]{5,4,3,2,1,0:T(8,128)(2,1)} %get-tuple-element.34.refs_0_.refs_1_, bf16[4,4,32,2,32,128]{5,4,3,2,1,0:T(8,128)(2,1)} %azimuth_factors.1.refs_2_, s32[128,128]{1,0:T(8,128)} %bitcast.18, ...), custom_call_target="tpu_custom_call" | custom-call | tf_op jit(solution)/shard_map/image_rows/pallas_call | solution.py:445
  144.2 12.5 %all-to-all-done.2 = bf16[128,2,16,256]{3,2,1,0:T(8,128)(2,1)S(1)} async-done(((bf16[128,2,16,256]{3,2,1,0:T(8,128)(2,1)}), bf16[128,2,16,256]{3,2,1,0:T(8,128)(2,1)S(1)}, u32[]{:S(2)}, u32[]{:S(2)}) %all-to-all-start.2) | async-done | bytes 2097184 | tf_op jit(solution)/shard_map/all_to_all | solution.py:495
  156.7 1.4 copy-done.1
  158.1 8.2 %doppler_forward.3.refs_1_.refs_0_ = bf16[4,4,16,2,32,128]{5,4,3,2,1,0:T(8,128)(2,1)} custom-call(bf16[32,4,2,32,256]{4,3,2,1,0:T(8,128)(2,1)} %bitcast.3.first, bf16[32,4,2,16,256]{4,3,2,1,0:T(8,128)(2,1)} %bitcast.17, bf16[256,256]{1,0:T(8,128)(2,1)} %constant.40.clone.w_ref, f32[128,128]{1,0:T(8,128)} %constant.41.clone.cos_ref.refs_4_, ...), custom_call_target="tpu_custom_call" | custom-call | tf_op jit(solution)/shard_map/doppler_forward/pallas_call | solution.py:237
  166.3 6.5 %image_rows.4 = (bf16[2,16,4096]{2,1,0:T(8,128)(2,1)}, bf16[2,16,4096]{2,1,0:T(8,128)(2,1)}, bf16[2,16,4096]{2,1,0:T(8,128)(2,1)}, bf16[2,16,4096]{2,1,0:T(8,128)(2,1)}) custom-call(bf16[4,4,16,2,32,128]{5,4,3,2,1,0:T(8,128)(2,1)} %get-tuple-element.34.refs_0_.refs_1_, bf16[4,4,16,2,32,128]{5,4,3,2,1,0:T(8,128)(2,1)} %doppler_forward.3.refs_1_.refs_0_, ...), custom_call_target="tpu_custom_call" | custom-call | tf_op jit(solution)/shard_map/image_rows/pallas_call | solution.py:445
  172.8 1.1 collective-permute-start
  173.9 0.0 collective-permute-start.1
  173.9 1.7 collective-permute-start.2
  175.6 0.0 collective-permute-done.3.refs_1_
  175.6 8.1 %image_rows.5 = (bf16[2,16,4096]{2,1,0:T(8,128)(2,1)}, bf16[2,16,4096]{2,1,0:T(8,128)(2,1)}, bf16[2,16,4096]{2,1,0:T(8,128)(2,1)}, bf16[2,16,4096]{2,1,0:T(8,128)(2,1)}) custom-call(bf16[4,4,16,2,32,128]{5,4,3,2,1,0:T(8,128)(2,1)} %doppler_forward.3.refs_1_.refs_0_, bf16[4,4,8,2,32,128]{5,4,3,2,1,0:T(8,128)(2,1)} %collective-permute-done.3.refs_1_, ...), custom_call_target="tpu_custom_call" | custom-call | tf_op jit(solution)/shard_map/image_rows/pallas_call | solution.py:445
  183.7 0.2 collective-permute-start.4
  183.9 1.0 collective-permute-start.5
  184.9 0.0 collective-permute-done.refs_1_
  184.9 1.0 collective-permute-start.6
  185.9 0.0 collective-permute-done.1.refs_2_
  185.9 2.4 %collective-permute-done.2.refs_3_ = bf16[2,16,4096]{2,1,0:T(8,128)(2,1)S(1)} collective-permute-done((bf16[2,16,4096]{2,1,0:T(8,128)(2,1)}, bf16[2,16,4096]{2,1,0:T(8,128)(2,1)S(1)}, u32[]{:S(2)}, u32[]{:S(2)}) %collective-permute-start.2) | collective-permute-done | bytes 262176 | tf_op jit(solution)/shard_map/ppermute | solution.py:500
  188.2 0.0 collective-permute-done.4.refs_5_
  188.3 5.0 %collective-permute-done.5.refs_6_ = bf16[2,16,4096]{2,1,0:T(8,128)(2,1)S(1)} collective-permute-done((bf16[2,16,4096]{2,1,0:T(8,128)(2,1)}, bf16[2,16,4096]{2,1,0:T(8,128)(2,1)S(1)}, u32[]{:S(2)}, u32[]{:S(2)}) %collective-permute-start.5) | collective-permute-done | bytes 262176 | tf_op jit(solution)/shard_map/ppermute | solution.py:500
  193.2 5.8 %collective-permute-done.6.refs_7_ = bf16[2,16,4096]{2,1,0:T(8,128)(2,1)S(1)} collective-permute-done((bf16[2,16,4096]{2,1,0:T(8,128)(2,1)}, bf16[2,16,4096]{2,1,0:T(8,128)(2,1)S(1)}, u32[]{:S(2)}, u32[]{:S(2)}) %collective-permute-start.6) | collective-permute-done | bytes 262176 | tf_op jit(solution)/shard_map/ppermute | solution.py:500
  199.0 0.0 copy-done.3
  199.0 0.0 copy-done.4
  199.0 0.0 copy-done.5
  199.0 0.7 copy-done.8
  199.7 2.7 %place_rows.1 = bf16[2,128,4096]{2,1,0:T(8,128)(2,1)} custom-call(s32[1]{0:T(128)} %bitcast.refs_7_.mine_ref, bf16[2,16,4096]{2,1,0:T(8,128)(2,1)} %get-tuple-element.40.refs_0_, bf16[2,16,4096]{2,1,0:T(8,128)(2,1)} %copy-done.3, bf16[2,16,4096]{2,1,0:T(8,128)(2,1)} %copy-done.4, bf16[2,16,4096]{2,1,0:T(8,128)(2,1)} %copy-done.5, ...), custom_call_target="tpu_custom_call" | custom-call | tf_op jit(solution)/shard_map/place_rows/pallas_call | solution.py:469
  (13 shorter events, 0.0 us)
Async XLA Ops:
  0.0 33.0 %copy-start = (s32[4,16384]{1,0:T(4,128)S(1)}, s32[4,16384]{1,0:T(4,128)}, u32[]{:S(2)}) copy-start(s32[4,16384]{1,0:T(4,128)} %param.33) | copy-start | bytes 786436
  21.7 12.1 %copy-start.9 = (f32[4,16384]{1,0:T(4,128)S(1)}, f32[4,16384]{1,0:T(4,128)}, u32[]{:S(2)}) copy-start(f32[4,16384]{1,0:T(4,128)} %param.32) | copy-start | bytes 786436
  21.7 63.7 %all-to-all-start = ((bf16[128,2,32,256]{3,2,1,0:T(8,128)(2,1)}), bf16[128,2,32,256]{3,2,1,0:T(8,128)(2,1)}, u32[]{:S(2)}, u32[]{:S(2)}) async-start(bf16[128,2,32,256]{3,2,1,0:T(8,128)(2,1)} %range_compress.2), calls=%async_computation | async-start | bytes 8388608 | tf_op jit(solution)/shard_map/all_to_all | solution.py:495
  34.7 15.5 %copy-start.10 = (f32[128]{0:T(128)S(1)}, f32[128]{0:T(128)}, u32[]{:S(2)}) copy-start(f32[128]{0:T(128)} %param.31) | copy-start | bytes 1540
  50.8 34.7 %copy-start.2 = (bf16[128,2,16,256]{3,2,1,0:T(8,128)(2,1)S(1)}, bf16[128,2,16,256]{3,2,1,0:T(8,128)(2,1)}, u32[]{:S(2)}) copy-start(bf16[128,2,16,256]{3,2,1,0:T(8,128)(2,1)} %get-tuple-element.31) | copy-start | bytes 6291460
  120.8 35.9 %all-to-all-start.2 = ((bf16[128,2,16,256]{3,2,1,0:T(8,128)(2,1)}), bf16[128,2,16,256]{3,2,1,0:T(8,128)(2,1)S(1)}, u32[]{:S(2)}, u32[]{:S(2)}) async-start(bf16[128,2,16,256]{3,2,1,0:T(8,128)(2,1)} %get-tuple-element.35), calls=%async_computation.2 | async-start | bytes 4194304 | tf_op jit(solution)/shard_map/all_to_all | solution.py:495
  136.5 39.1 %collective-permute-start.3 = (bf16[4,4,8,2,32,128]{5,4,3,2,1,0:T(8,128)(2,1)}, bf16[4,4,8,2,32,128]{5,4,3,2,1,0:T(8,128)(2,1)}, u32[]{:S(2)}, u32[]{:S(2)}) collective-permute-start(bf16[4,4,8,2,32,128]{5,4,3,2,1,0:T(8,128)(2,1)} %get-tuple-element.44), channel_id=1, source_target_pairs={{32,0},{64,32},{96,64},{1,96},{33,1},{65,33},{97,65},{2,97},{34,2}... | collective-permute-start | bytes 6291464 | tf_op jit(solution)/shard_map/ppermute | solution.py:523
  156.7 1.4 copy-start.1
  172.8 12.1 %collective-permute-start = (bf16[2,16,4096]{2,1,0:T(8,128)(2,1)}, bf16[2,16,4096]{2,1,0:T(8,128)(2,1)S(1)}, u32[]{:S(2)}, u32[]{:S(2)}) collective-permute-start(bf16[2,16,4096]{2,1,0:T(8,128)(2,1)} %get-tuple-element.41), channel_id=1, source_target_pairs={{0,32},{32,0},{64,96},{96,64},{1,33},{33,1},{65,97},{97,65},{2,34}... | collective-permute-start | bytes 786440 | tf_op jit(solution)/shard_map/ppermute | solution.py:500
  173.9 12.0 %collective-permute-start.1 = (bf16[2,16,4096]{2,1,0:T(8,128)(2,1)}, bf16[2,16,4096]{2,1,0:T(8,128)(2,1)S(1)}, u32[]{:S(2)}, u32[]{:S(2)}) collective-permute-start(bf16[2,16,4096]{2,1,0:T(8,128)(2,1)} %get-tuple-element.42), channel_id=1, source_target_pairs={{0,64},{32,96},{64,0},{96,32},{1,65},{33,97},{65,1},{97,33},{2,66}... | collective-permute-start | bytes 786440 | tf_op jit(solution)/shard_map/ppermute | solution.py:500
  173.9 14.3 %collective-permute-start.2 = (bf16[2,16,4096]{2,1,0:T(8,128)(2,1)}, bf16[2,16,4096]{2,1,0:T(8,128)(2,1)S(1)}, u32[]{:S(2)}, u32[]{:S(2)}) collective-permute-start(bf16[2,16,4096]{2,1,0:T(8,128)(2,1)} %get-tuple-element.43), channel_id=1, source_target_pairs={{0,96},{32,64},{64,32},{96,0},{1,97},{33,65},{65,33},{97,1},{2,98}... | collective-permute-start | bytes 786440 | tf_op jit(solution)/shard_map/ppermute | solution.py:500
  183.7 4.5 %collective-permute-start.4 = (bf16[2,16,4096]{2,1,0:T(8,128)(2,1)}, bf16[2,16,4096]{2,1,0:T(8,128)(2,1)S(1)}, u32[]{:S(2)}, u32[]{:S(2)}) collective-permute-start(bf16[2,16,4096]{2,1,0:T(8,128)(2,1)} %get-tuple-element.46), channel_id=1, source_target_pairs={{0,32},{32,0},{64,96},{96,64},{1,33},{33,1},{65,97},{97,65},{2,34}... | collective-permute-start | bytes 786440 | tf_op jit(solution)/shard_map/ppermute | solution.py:500
  183.9 9.3 %collective-permute-start.5 = (bf16[2,16,4096]{2,1,0:T(8,128)(2,1)}, bf16[2,16,4096]{2,1,0:T(8,128)(2,1)S(1)}, u32[]{:S(2)}, u32[]{:S(2)}) collective-permute-start(bf16[2,16,4096]{2,1,0:T(8,128)(2,1)} %get-tuple-element.47), channel_id=1, source_target_pairs={{0,64},{32,96},{64,0},{96,32},{1,65},{33,97},{65,1},{97,33},{2,66}... | collective-permute-start | bytes 786440 | tf_op jit(solution)/shard_map/ppermute | solution.py:500
  184.9 14.1 %copy-start.3 = (bf16[2,16,4096]{2,1,0:T(8,128)(2,1)}, bf16[2,16,4096]{2,1,0:T(8,128)(2,1)S(1)}, u32[]{:S(2)}) copy-start(bf16[2,16,4096]{2,1,0:T(8,128)(2,1)S(1)} %collective-permute-done.refs_1_) | copy-start | bytes 786436
  184.9 14.1 %collective-permute-start.6 = (bf16[2,16,4096]{2,1,0:T(8,128)(2,1)}, bf16[2,16,4096]{2,1,0:T(8,128)(2,1)S(1)}, u32[]{:S(2)}, u32[]{:S(2)}) collective-permute-start(bf16[2,16,4096]{2,1,0:T(8,128)(2,1)} %get-tuple-element.48), channel_id=1, source_target_pairs={{0,96},{32,64},{64,32},{96,0},{1,97},{33,65},{65,33},{97,1},{2,98}... | collective-permute-start | bytes 786440 | tf_op jit(solution)/shard_map/ppermute | solution.py:500
  185.9 13.2 %copy-start.4 = (bf16[2,16,4096]{2,1,0:T(8,128)(2,1)}, bf16[2,16,4096]{2,1,0:T(8,128)(2,1)S(1)}, u32[]{:S(2)}) copy-start(bf16[2,16,4096]{2,1,0:T(8,128)(2,1)S(1)} %collective-permute-done.1.refs_2_) | copy-start | bytes 786436
  188.2 10.8 %copy-start.5 = (bf16[2,16,4096]{2,1,0:T(8,128)(2,1)}, bf16[2,16,4096]{2,1,0:T(8,128)(2,1)S(1)}, u32[]{:S(2)}) copy-start(bf16[2,16,4096]{2,1,0:T(8,128)(2,1)S(1)} %collective-permute-done.2.refs_3_) | copy-start | bytes 786436
  188.3 10.8 %copy-start.6 = (bf16[2,16,4096]{2,1,0:T(8,128)(2,1)}, bf16[2,16,4096]{2,1,0:T(8,128)(2,1)S(1)}, u32[]{:S(2)}) copy-start(bf16[2,16,4096]{2,1,0:T(8,128)(2,1)S(1)} %collective-permute-done.4.refs_5_) | copy-start | bytes 786436
  193.2 5.8 %copy-start.7 = (bf16[2,16,4096]{2,1,0:T(8,128)(2,1)}, bf16[2,16,4096]{2,1,0:T(8,128)(2,1)S(1)}, u32[]{:S(2)}) copy-start(bf16[2,16,4096]{2,1,0:T(8,128)(2,1)S(1)} %collective-permute-done.5.refs_6_) | copy-start | bytes 786436
  199.0 0.7 copy-start.8

commit v7 on v6

--- a/solution.py
+++ b/solution.py
@@ -12,8 +12,8 @@
 MAXS = 8
 RBLK = 32
 LANES = 128
-UNROLL = 4
-TILE = 32
+RANGE_UNROLL = 8
+TILE = 64
 VMEM = 56 * 1024 * 1024
 F32 = jnp.float32
 BF16 = jnp.bfloat16
@@ -56,7 +56,7 @@
     wave = np.exp(2j * np.pi * ((j1 * (k2 + size * k1)) % length) / length) / size
     wave = as_bf16(np.stack([realified(wave[k]) for k in range(size)]))
     phase = range_phase.reshape(size, size).T * (0.5 / math.pi)
-    group = 16
+    group = 32
     block = pl.BlockSpec((group, 2 * size, 2 * size), lambda i: (i, 0, 0))
     return pl.pallas_call(
         middle_kernel,
@@ -71,69 +71,82 @@
 
 def range_kernel(size, splits, x_ref, w_ref, t_ref, v_ref, *refs):
     outs, (one, two) = refs[:splits], refs[splits:]
+    halves = x_ref.shape[2] // LANES
     both = 2 * size
     pitch = size + 1
 
+    def lanes(h):
+        return slice(h * LANES, (h + 1) * LANES)
+
     def cast(step, carry):
-        for u in range(8):
-            line = step * 8 + u
-            for c in range(2):
-                one[pl.ds((c * size + line) * pitch, size), :] = x_ref[
-                    c, pl.ds(pl.multiple_of(line * size, size), size), :
-                ].astype(F32)
-        return carry
-
-    lax.fori_loop(0, size // 8, cast, 0)
+        for u in range(4):
+            line = step * 4 + u
+            for h in range(halves):
+                for c in range(2):
+                    one[h, pl.ds((c * size + line) * pitch, size), :] = x_ref[
+                        c, pl.ds(pl.multiple_of(line * size, size), size), lanes(h)
+                    ].astype(F32)
+        return carry
+
+    lax.fori_loop(0, size // 4, cast, 0)
 
     def strided(source, target, table):
         def body(step, carry):
-            for u in range(UNROLL):
-                j1 = (step * UNROLL + u) * 2
+            for u in range(RANGE_UNROLL):
+                j1 = step * RANGE_UNROLL + u
                 value = jnp.concatenate(
-                    [source[pl.ds(j1 + i, both, stride=pitch), :] for i in range(2)], axis=1
+                    [source[h, pl.ds(j1, both, stride=pitch), :] for h in range(halves)], axis=1
                 ).astype(BF16)
                 out = jnp.dot(table, value, preferred_element_type=F32)
-                for i in range(2):
-                    target[pl.ds(j1 + i, both, stride=pitch), :] = out[
-                        :, i * LANES : (i + 1) * LANES
-                    ]
+                for h in range(halves):
+                    target[h, pl.ds(j1, both, stride=pitch), :] = out[:, lanes(h)]
             return carry
 
-        lax.fori_loop(0, size // (2 * UNROLL), body, 0)
+        lax.fori_loop(0, size // RANGE_UNROLL, body, 0)
 
     strided(one, two, w_ref[...])
 
     def inner(step, carry):
-        for u in range(2 * UNROLL):
-            k2 = step * 2 * UNROLL + u
+        for u in range(RANGE_UNROLL):
+            k2 = step * RANGE_UNROLL + u
             value = jnp.concatenate(
-                [two[pl.ds((c * size + k2) * pitch, size), :] for c in range(2)], axis=0
+                [
+                    jnp.concatenate(
+                        [two[h, pl.ds((c * size + k2) * pitch, size), :] for c in range(2)], axis=0
+                    )
+                    for h in range(halves)
+                ],
+                axis=1,
             ).astype(BF16)
             out = jnp.dot(t_ref[k2], value, preferred_element_type=F32)
-            for d in range(2):
-                one[pl.ds((d * size + k2) * pitch, size), :] = out[d * size : (d + 1) * size]
-        return carry
-
-    lax.fori_loop(0, size // (2 * UNROLL), inner, 0)
+            for h in range(halves):
+                for d in range(2):
+                    one[h, pl.ds((d * size + k2) * pitch, size), :] = out[
+                        d * size : (d + 1) * size, lanes(h)
+                    ]
+        return carry
+
+    lax.fori_loop(0, size // RANGE_UNROLL, inner, 0)
     strided(one, two, v_ref[...])
     rows = outs[0].shape[2]
     pieces = size // rows
 
     def give(step, carry):
-        for u in range(8):
-            line = step * 8 + u
+        for u in range(4):
+            line = step * 4 + u
             for piece in range(pieces):
                 block = line * (pieces // splits) + piece // splits
                 for d in range(2):
-                    outs[piece % splits][block, d] = two[
-                        pl.ds((d * size + line) * pitch + piece * rows, rows), :
-                    ].astype(BF16)
-        return carry
-
-    lax.fori_loop(0, size // 8, give, 0)
-
-
-def range_compress(echo, middle, first, count, blocks, splits):
+                    for h in range(halves):
+                        outs[piece % splits][block, d, :, lanes(h)] = two[
+                            h, pl.ds((d * size + line) * pitch + piece * rows, rows), :
+                        ].astype(BF16)
+        return carry
+
+    lax.fori_loop(0, size // 4, give, 0)
+
+
+def range_compress(echo, middle, chunk, width, blocks, splits):
     length = echo.shape[1]
     size = math.isqrt(length)
     index = np.arange(size)
@@ -141,18 +154,18 @@
     backward = as_bf16(realified(unit_table(index, index, size, 1)))
     rows = length // blocks // splits
     whole = lambda *shape: pl.BlockSpec(shape, lambda i: (0,) * len(shape))
-    scratch = pltpu.VMEM((2 * (length + size), LANES), F32)
+    scratch = pltpu.VMEM((width // LANES, 2 * (length + size), LANES), F32)
     return pl.pallas_call(
         functools.partial(range_kernel, size, splits),
-        grid=(count,),
+        grid=(1,),
         in_specs=[
-            pl.BlockSpec((2, length, LANES), lambda i: (0, 0, first + i)),
+            pl.BlockSpec((2, length, width), lambda i: (0, 0, chunk)),
             whole(2 * size, 2 * size),
             whole(size, 2 * size, 2 * size),
             whole(2 * size, 2 * size),
         ],
-        out_specs=[pl.BlockSpec((blocks, 2, rows, LANES), lambda i: (0, 0, 0, i))] * splits,
-        out_shape=[jax.ShapeDtypeStruct((blocks, 2, rows, count * LANES), BF16)] * splits,
+        out_specs=[whole(blocks, 2, rows, width)] * splits,
+        out_shape=[jax.ShapeDtypeStruct((blocks, 2, rows, width), BF16)] * splits,
         scratch_shapes=[scratch, scratch],
         compiler_params=pltpu.CompilerParams(vmem_limit_bytes=VMEM),
         name="range_compress",
@@ -206,12 +219,8 @@
                     value = second[line : line + TILE, d * LANES : (d + 1) * LANES]
                     o_ref[tile, 0, first_row + i, d] = value
 
-    def body(step, carry):
-        for u in range(4):
-            pair(step * 8 + 2 * u)
-        return carry
-
-    lax.fori_loop(0, rows // 8, body, 0)
+    for first_row in range(0, rows, 2):
+        pair(first_row)
     for rim in refs[:-1]:
         rim[:, 0] = o_ref[:, 0, :MAXS]
 
@@ -502,12 +511,11 @@
         ]
         return [pieces[0]] + sent[::-1]
 
-    early = pulse_dev // LANES // 2
-    (sent,) = range_compress(echo, middle, 0, early, blocks, 1)
+    width = pulse_dev // 2
+    (sent,) = range_compress(echo, middle, 0, width, blocks, 1)
     sent, echo = lax.optimization_barrier((sent, echo))
     first = spread(sent)
-    count = pulse_dev // LANES - early
-    sent_low, sent_high = range_compress(echo, middle, early, count, blocks, 2)
+    sent_low, sent_high = range_compress(echo, middle, 1, width, blocks, 2)
     own_shift = lax.dynamic_slice_in_dim(migration, sub_index, 1, 0)
     shift = own_shift.reshape(size, size).T
     phase = jnp.swapaxes(doppler.reshape(subs, size, size), 1, 2) * (0.5 / math.pi)

time: 206 us -> 201 us (0.976)
  Pallas kernels: 86.6 us -> 77.4 us
  waiting for transfers between devices: 48.8 us -> 52.5 us
    pallas_call x2, Pallas kernels: 30.8 us -> 26 us  [range_compress(): pl.pallas_call(functools.partial(range_kernel, size, splits), grid=(1,),...]
    all_to_all x2, waiting for transfers between devices: 35.6 us -> 39.4 us  [spread(): got = lax.all_to_all(sent, ('pul', 'sub'), 0, 0, tiled=True)]
    pallas_call x3, Pallas kernels: 20 us -> 17.7 us  [image_rows(): pl.pallas_call(functools.partial(image_kernel, len(before), finish), grid...]
  transfers between devices with their start and end apart: 9 -> 9, of which waited for: 5 -> 6; matrix products, arithmetic and copies ran while one was open for 1% -> 1% of each run, Pallas kernels for 32% -> 29%
where the time goes in v7:
time: 201 us; the launch traced here: 198 us
  Pallas kernels  77.4 us (39%)
  waiting for transfers between devices  52.5 us (26%)
  blocking collectives  35.4 us (18%)
  starting transfers between devices  26.1 us (13%)
  local copies, waits for them, and re-layouts  4.44 us (2%)
    all_to_all x2, waiting for transfers between devices, spread(): got = lax.all_to_all(sent, ('pul', 'sub'), 0, 0, tiled=True)  39.4 us
    all_to_all x1, blocking collectives, spread(): got = lax.all_to_all(sent, ('pul', 'sub'), 0, 0, tiled=True)  35.4 us
    pallas_call x2, Pallas kernels, range_compress(): pl.pallas_call(functools.partial(range_kernel, size, splits), grid=(1,),...  26 us
    all_to_all x2, starting transfers between devices, spread(): got = lax.all_to_all(sent, ('pul', 'sub'), 0, 0, tiled=True)  18.3 us
    pallas_call x3, Pallas kernels, image_rows(): pl.pallas_call(functools.partial(image_kernel, len(before), finish), grid...  17.7 us
    pallas_call x2, Pallas kernels, doppler_forward(): pl.pallas_call(functools.partial(doppler_kernel, rows), grid=(subs,), in_...  15.3 us
    ppermute x6, waiting for transfers between devices, swap(): lax.ppermute(pieces[k], 'sub', [(i, i ^ k) for i in range(subs)])  12.6 us
    pallas_call x1, Pallas kernels, azimuth_factors(): pl.pallas_call(factor_kernel, grid=(subs,), in_specs=[pl.BlockSpec(memory...  11.7 us
  transfers between devices with their start and end apart: 9, of which 6 were waited for; matrix products, arithmetic and copies ran while one was open for 1% of the time, Pallas kernels for 29%

profile of v7, /device:TPU:7, one launch (start us, length us, event | category | flops | bytes accessed | tf_op | source)
XLA Modules:
  0.0 197.5 jit_solution(13629176374404755806)
XLA Ops:
  0.0 0.0 copy-start
  0.0 0.8 broadcast_multiply_fusion
  0.8 0.1 mul.27
  0.8 0.1 copy.30
  0.9 0.7 pad_maximum_fusion.phase_ref
  1.6 4.0 %range_middle.1.t_ref = bf16[64,128,128]{2,1,0:T(8,128)(2,1)} custom-call(f32[64,128]{1,0:T(8,128)} %pad_maximum_fusion.phase_ref, bf16[64,128,128]{2,1,0:T(8,128)(2,1)} %constant.37.clone.wave_ref), custom_call_target="tpu_custom_call" | custom-call | tf_op jit(solution)/shard_map/range_middle/pallas_call | solution.py:61
  5.6 13.0 %range_compress.2 = bf16[128,2,32,256]{3,2,1,0:T(8,128)(2,1)} custom-call(bf16[2,4096,512]{2,1,0:T(8,128)(2,1)} %bitcast.14, bf16[128,128]{1,0:T(8,128)(2,1)} %constant.38.clone.w_ref, bf16[64,128,128]{2,1,0:T(8,128)(2,1)} %range_middle.1.t_ref, bf16[128,128]{1,0:T(8,128)(2,1)} %constant.39.clone.v_ref), custom_call_target="tpu_custom_call" | custom-call | tf_op jit(solution)/shard_map/range_compress/pallas_call | solution.py:158
  18.6 11.3 %all-to-all-start = ((bf16[128,2,32,256]{3,2,1,0:T(8,128)(2,1)}), bf16[128,2,32,256]{3,2,1,0:T(8,128)(2,1)}, u32[]{:S(2)}, u32[]{:S(2)}) async-start(bf16[128,2,32,256]{3,2,1,0:T(8,128)(2,1)} %range_compress.2), calls=%async_computation | async-start | bytes 8388608 | tf_op jit(solution)/shard_map/all_to_all | solution.py:504
  29.9 0.0 copy-done
  29.9 0.1 constant_dynamic-slice_fusion
  30.0 0.7 copy.32
  30.7 0.0 copy-done.9
  30.7 0.1 multiply_bitcast_fusion
  30.8 0.8 copy.31
  31.6 13.1 %range_compress.3 = (bf16[128,2,16,256]{3,2,1,0:T(8,128)(2,1)}, bf16[128,2,16,256]{3,2,1,0:T(8,128)(2,1)}) custom-call(bf16[2,4096,512]{2,1,0:T(8,128)(2,1)} %bitcast.15, bf16[128,128]{1,0:T(8,128)(2,1)} %constant.38.clone.w_ref, bf16[64,128,128]{2,1,0:T(8,128)(2,1)} %range_middle.1.t_ref, bf16[128,128]{1,0:T(8,128)(2,1)} %constant.39.clone.v_ref), custom_call_target="tpu_custom_call" | custom-call | tf_op jit(solution)/shard_map/range_compress/pallas_call | solution.py:158
  44.7 0.0 copy-done.10
  44.7 0.6 dynamic_slice.6.kappa_ref
  45.3 11.7 %azimuth_factors.1.refs_2_ = bf16[2,4,32,2,64,128]{5,4,3,2,1,0:T(8,128)(2,1)} custom-call(f32[32]{0:T(128)} %dynamic_slice.6.kappa_ref, f32[4,128,128]{2,1,0:T(8,128)} %bitcast.21), custom_call_target="tpu_custom_call" | custom-call | tf_op jit(solution)/shard_map/azimuth_factors/pallas_call | solution.py:310
  57.0 25.3 %all-to-all-done = bf16[128,2,32,256]{3,2,1,0:T(8,128)(2,1)} async-done(((bf16[128,2,32,256]{3,2,1,0:T(8,128)(2,1)}), bf16[128,2,32,256]{3,2,1,0:T(8,128)(2,1)}, u32[]{:S(2)}, u32[]{:S(2)}) %all-to-all-start) | async-done | bytes 4194336 | tf_op jit(solution)/shard_map/all_to_all | solution.py:504
  82.3 0.0 copy-done.2
  82.3 35.4 %all_to_all.15 = bf16[128,2,16,256]{3,2,1,0:T(8,128)(2,1)} all-to-all(bf16[128,2,16,256]{3,2,1,0:T(8,128)(2,1)S(1)} %copy-done.2), channel_id=1, replica_groups=mesh['sub'=4,'pul'=32] {'pul','sub'}, dimensions={0} | all-to-all | bytes 4194304 | tf_op jit(solution)/shard_map/all_to_all | solution.py:504
  117.7 7.0 %all-to-all-start.2 = ((bf16[128,2,16,256]{3,2,1,0:T(8,128)(2,1)}), bf16[128,2,16,256]{3,2,1,0:T(8,128)(2,1)S(1)}, u32[]{:S(2)}, u32[]{:S(2)}) async-start(bf16[128,2,16,256]{3,2,1,0:T(8,128)(2,1)} %get-tuple-element.35), calls=%async_computation.2 | async-start | bytes 4194304 | tf_op jit(solution)/shard_map/all_to_all | solution.py:504
  124.8 8.0 %doppler_forward.2 = (bf16[2,4,16,2,64,128]{5,4,3,2,1,0:T(8,128)(2,1)}, bf16[2,4,8,2,64,128]{5,4,3,2,1,0:T(8,128)(2,1)}) custom-call(bf16[32,4,2,32,256]{4,3,2,1,0:T(8,128)(2,1)} %bitcast.3.first, bf16[32,4,2,16,256]{4,3,2,1,0:T(8,128)(2,1)} %bitcast.16, bf16[256,256]{1,0:T(8,128)(2,1)} %constant.40.clone.w_ref, f32[128,128]{1,0:T(8,128)} %constant.41.clone.cos_ref.refs_4_, ...), custom_call_target="tpu_custom_call" | custom-call | tf_op jit(solution)/shard_map/doppler_forward/pallas_call | solution.py:246
  132.8 2.3 %collective-permute-start.3 = (bf16[2,4,8,2,64,128]{5,4,3,2,1,0:T(8,128)(2,1)}, bf16[2,4,8,2,64,128]{5,4,3,2,1,0:T(8,128)(2,1)}, u32[]{:S(2)}, u32[]{:S(2)}) collective-permute-start(bf16[2,4,8,2,64,128]{5,4,3,2,1,0:T(8,128)(2,1)} %get-tuple-element.44), channel_id=1, source_target_pairs={{32,0},{64,32},{96,64},{1,96},{33,1},{65,33},{97,65},{2,97},{34,2}... | collective-permute-start | bytes 6291464 | tf_op jit(solution)/shard_map/ppermute | solution.py:531
  135.0 4.6 %image_rows.3.refs_9_ = bf16[8,2,128,128]{3,2,1,0:T(8,128)(2,1)} custom-call(bf16[2,4,16,2,64,128]{5,4,3,2,1,0:T(8,128)(2,1)} %get-tuple-element.34.refs_0_.refs_1_, bf16[2,4,16,2,64,128]{5,4,3,2,1,0:T(8,128)(2,1)} %get-tuple-element.34.refs_0_.refs_1_, bf16[2,4,32,2,64,128]{5,4,3,2,1,0:T(8,128)(2,1)} %azimuth_factors.1.refs_2_, s32[128,128]{1,0:T(8,128)} %bitcast.18, ...), custom_call_target="tpu_custom_call" | custom-call | tf_op jit(solution)/shard_map/image_rows/pallas_call | solution.py:454
  139.6 14.0 %all-to-all-done.2 = bf16[128,2,16,256]{3,2,1,0:T(8,128)(2,1)S(1)} async-done(((bf16[128,2,16,256]{3,2,1,0:T(8,128)(2,1)}), bf16[128,2,16,256]{3,2,1,0:T(8,128)(2,1)S(1)}, u32[]{:S(2)}, u32[]{:S(2)}) %all-to-all-start.2) | async-done | bytes 2097184 | tf_op jit(solution)/shard_map/all_to_all | solution.py:504
  153.6 1.4 copy-done.1
  155.0 7.3 %doppler_forward.3.refs_1_.refs_0_ = bf16[2,4,16,2,64,128]{5,4,3,2,1,0:T(8,128)(2,1)} custom-call(bf16[32,4,2,32,256]{4,3,2,1,0:T(8,128)(2,1)} %bitcast.3.first, bf16[32,4,2,16,256]{4,3,2,1,0:T(8,128)(2,1)} %bitcast.17, bf16[256,256]{1,0:T(8,128)(2,1)} %constant.40.clone.w_ref, f32[128,128]{1,0:T(8,128)} %constant.41.clone.cos_ref.refs_4_, ...), custom_call_target="tpu_custom_call" | custom-call | tf_op jit(solution)/shard_map/doppler_forward/pallas_call | solution.py:246
  162.3 5.6 %image_rows.4 = (bf16[2,16,4096]{2,1,0:T(8,128)(2,1)}, bf16[2,16,4096]{2,1,0:T(8,128)(2,1)}, bf16[2,16,4096]{2,1,0:T(8,128)(2,1)}, bf16[2,16,4096]{2,1,0:T(8,128)(2,1)}) custom-call(bf16[2,4,16,2,64,128]{5,4,3,2,1,0:T(8,128)(2,1)} %get-tuple-element.34.refs_0_.refs_1_, bf16[2,4,16,2,64,128]{5,4,3,2,1,0:T(8,128)(2,1)} %doppler_forward.3.refs_1_.refs_0_, ...), custom_call_target="tpu_custom_call" | custom-call | tf_op jit(solution)/shard_map/image_rows/pallas_call | solution.py:454
  168.0 1.1 collective-permute-start
  169.0 0.0 collective-permute-start.1
  169.1 1.7 collective-permute-start.2
  170.8 0.5 collective-permute-done.3.refs_1_
  171.3 7.5 %image_rows.5 = (bf16[2,16,4096]{2,1,0:T(8,128)(2,1)}, bf16[2,16,4096]{2,1,0:T(8,128)(2,1)}, bf16[2,16,4096]{2,1,0:T(8,128)(2,1)}, bf16[2,16,4096]{2,1,0:T(8,128)(2,1)}) custom-call(bf16[2,4,16,2,64,128]{5,4,3,2,1,0:T(8,128)(2,1)} %doppler_forward.3.refs_1_.refs_0_, bf16[2,4,8,2,64,128]{5,4,3,2,1,0:T(8,128)(2,1)} %collective-permute-done.3.refs_1_, ...), custom_call_target="tpu_custom_call" | custom-call | tf_op jit(solution)/shard_map/image_rows/pallas_call | solution.py:454
  178.8 0.0 collective-permute-start.4
  178.8 2.4 %collective-permute-start.5 = (bf16[2,16,4096]{2,1,0:T(8,128)(2,1)}, bf16[2,16,4096]{2,1,0:T(8,128)(2,1)S(1)}, u32[]{:S(2)}, u32[]{:S(2)}) collective-permute-start(bf16[2,16,4096]{2,1,0:T(8,128)(2,1)} %get-tuple-element.47), channel_id=1, source_target_pairs={{0,64},{32,96},{64,0},{96,32},{1,65},{33,97},{65,1},{97,33},{2,66}... | collective-permute-start | bytes 786440 | tf_op jit(solution)/shard_map/ppermute | solution.py:509
  181.1 0.0 collective-permute-done.refs_1_
  181.1 0.4 collective-permute-start.6
  181.5 0.0 collective-permute-done.1.refs_2_
  181.5 1.8 collective-permute-done.2.refs_3_
  183.4 0.0 collective-permute-done.4.refs_5_
  183.4 5.0 %collective-permute-done.5.refs_6_ = bf16[2,16,4096]{2,1,0:T(8,128)(2,1)S(1)} collective-permute-done((bf16[2,16,4096]{2,1,0:T(8,128)(2,1)}, bf16[2,16,4096]{2,1,0:T(8,128)(2,1)S(1)}, u32[]{:S(2)}, u32[]{:S(2)}) %collective-permute-start.5) | collective-permute-done | bytes 262176 | tf_op jit(solution)/shard_map/ppermute | solution.py:509
  188.4 5.8 %collective-permute-done.6.refs_7_ = bf16[2,16,4096]{2,1,0:T(8,128)(2,1)S(1)} collective-permute-done((bf16[2,16,4096]{2,1,0:T(8,128)(2,1)}, bf16[2,16,4096]{2,1,0:T(8,128)(2,1)S(1)}, u32[]{:S(2)}, u32[]{:S(2)}) %collective-permute-start.6) | collective-permute-done | bytes 262176 | tf_op jit(solution)/shard_map/ppermute | solution.py:509
  194.2 0.0 copy-done.3
  194.2 0.0 copy-done.4
  194.2 0.0 copy-done.5
  194.2 0.7 copy-done.8
  194.9 2.7 %place_rows.1 = bf16[2,128,4096]{2,1,0:T(8,128)(2,1)} custom-call(s32[1]{0:T(128)} %bitcast.refs_7_.mine_ref, bf16[2,16,4096]{2,1,0:T(8,128)(2,1)} %get-tuple-element.40.refs_0_, bf16[2,16,4096]{2,1,0:T(8,128)(2,1)} %copy-done.3, bf16[2,16,4096]{2,1,0:T(8,128)(2,1)} %copy-done.4, bf16[2,16,4096]{2,1,0:T(8,128)(2,1)} %copy-done.5, ...), custom_call_target="tpu_custom_call" | custom-call | tf_op jit(solution)/shard_map/place_rows/pallas_call | solution.py:478
  (13 shorter events, 0.0 us)
Async XLA Ops:
  0.0 29.9 %copy-start = (s32[4,16384]{1,0:T(4,128)S(1)}, s32[4,16384]{1,0:T(4,128)}, u32[]{:S(2)}) copy-start(s32[4,16384]{1,0:T(4,128)} %param.33) | copy-start | bytes 786436
  18.6 12.1 %copy-start.9 = (f32[4,16384]{1,0:T(4,128)S(1)}, f32[4,16384]{1,0:T(4,128)}, u32[]{:S(2)}) copy-start(f32[4,16384]{1,0:T(4,128)} %param.32) | copy-start | bytes 786436
  18.6 63.7 %all-to-all-start = ((bf16[128,2,32,256]{3,2,1,0:T(8,128)(2,1)}), bf16[128,2,32,256]{3,2,1,0:T(8,128)(2,1)}, u32[]{:S(2)}, u32[]{:S(2)}) async-start(bf16[128,2,32,256]{3,2,1,0:T(8,128)(2,1)} %range_compress.2), calls=%async_computation | async-start | bytes 8388608 | tf_op jit(solution)/shard_map/all_to_all | solution.py:504
  31.6 13.1 %copy-start.10 = (f32[128]{0:T(128)S(1)}, f32[128]{0:T(128)}, u32[]{:S(2)}) copy-start(f32[128]{0:T(128)} %param.31) | copy-start | bytes 1540
  45.3 37.0 %copy-start.2 = (bf16[128,2,16,256]{3,2,1,0:T(8,128)(2,1)S(1)}, bf16[128,2,16,256]{3,2,1,0:T(8,128)(2,1)}, u32[]{:S(2)}) copy-start(bf16[128,2,16,256]{3,2,1,0:T(8,128)(2,1)} %get-tuple-element.31) | copy-start | bytes 6291460
  117.7 35.9 %all-to-all-start.2 = ((bf16[128,2,16,256]{3,2,1,0:T(8,128)(2,1)}), bf16[128,2,16,256]{3,2,1,0:T(8,128)(2,1)S(1)}, u32[]{:S(2)}, u32[]{:S(2)}) async-start(bf16[128,2,16,256]{3,2,1,0:T(8,128)(2,1)} %get-tuple-element.35), calls=%async_computation.2 | async-start | bytes 4194304 | tf_op jit(solution)/shard_map/all_to_all | solution.py:504
  132.8 38.6 %collective-permute-start.3 = (bf16[2,4,8,2,64,128]{5,4,3,2,1,0:T(8,128)(2,1)}, bf16[2,4,8,2,64,128]{5,4,3,2,1,0:T(8,128)(2,1)}, u32[]{:S(2)}, u32[]{:S(2)}) collective-permute-start(bf16[2,4,8,2,64,128]{5,4,3,2,1,0:T(8,128)(2,1)} %get-tuple-element.44), channel_id=1, source_target_pairs={{32,0},{64,32},{96,64},{1,96},{33,1},{65,33},{97,65},{2,97},{34,2}... | collective-permute-start | bytes 6291464 | tf_op jit(solution)/shard_map/ppermute | solution.py:531
  153.6 1.4 copy-start.1
  168.0 13.2 %collective-permute-start = (bf16[2,16,4096]{2,1,0:T(8,128)(2,1)}, bf16[2,16,4096]{2,1,0:T(8,128)(2,1)S(1)}, u32[]{:S(2)}, u32[]{:S(2)}) collective-permute-start(bf16[2,16,4096]{2,1,0:T(8,128)(2,1)} %get-tuple-element.41), channel_id=1, source_target_pairs={{0,32},{32,0},{64,96},{96,64},{1,33},{33,1},{65,97},{97,65},{2,34}... | collective-permute-start | bytes 786440 | tf_op jit(solution)/shard_map/ppermute | solution.py:509
  169.0 12.5 %collective-permute-start.1 = (bf16[2,16,4096]{2,1,0:T(8,128)(2,1)}, bf16[2,16,4096]{2,1,0:T(8,128)(2,1)S(1)}, u32[]{:S(2)}, u32[]{:S(2)}) collective-permute-start(bf16[2,16,4096]{2,1,0:T(8,128)(2,1)} %get-tuple-element.42), channel_id=1, source_target_pairs={{0,64},{32,96},{64,0},{96,32},{1,65},{33,97},{65,1},{97,33},{2,66}... | collective-permute-start | bytes 786440 | tf_op jit(solution)/shard_map/ppermute | solution.py:509
  169.1 14.3 %collective-permute-start.2 = (bf16[2,16,4096]{2,1,0:T(8,128)(2,1)}, bf16[2,16,4096]{2,1,0:T(8,128)(2,1)S(1)}, u32[]{:S(2)}, u32[]{:S(2)}) collective-permute-start(bf16[2,16,4096]{2,1,0:T(8,128)(2,1)} %get-tuple-element.43), channel_id=1, source_target_pairs={{0,96},{32,64},{64,32},{96,0},{1,97},{33,65},{65,33},{97,1},{2,98}... | collective-permute-start | bytes 786440 | tf_op jit(solution)/shard_map/ppermute | solution.py:509
  178.8 4.6 %collective-permute-start.4 = (bf16[2,16,4096]{2,1,0:T(8,128)(2,1)}, bf16[2,16,4096]{2,1,0:T(8,128)(2,1)S(1)}, u32[]{:S(2)}, u32[]{:S(2)}) collective-permute-start(bf16[2,16,4096]{2,1,0:T(8,128)(2,1)} %get-tuple-element.46), channel_id=1, source_target_pairs={{0,32},{32,0},{64,96},{96,64},{1,33},{33,1},{65,97},{97,65},{2,34}... | collective-permute-start | bytes 786440 | tf_op jit(solution)/shard_map/ppermute | solution.py:509
  178.8 9.6 %collective-permute-start.5 = (bf16[2,16,4096]{2,1,0:T(8,128)(2,1)}, bf16[2,16,4096]{2,1,0:T(8,128)(2,1)S(1)}, u32[]{:S(2)}, u32[]{:S(2)}) collective-permute-start(bf16[2,16,4096]{2,1,0:T(8,128)(2,1)} %get-tuple-element.47), channel_id=1, source_target_pairs={{0,64},{32,96},{64,0},{96,32},{1,65},{33,97},{65,1},{97,33},{2,66}... | collective-permute-start | bytes 786440 | tf_op jit(solution)/shard_map/ppermute | solution.py:509
  181.1 13.0 %copy-start.3 = (bf16[2,16,4096]{2,1,0:T(8,128)(2,1)}, bf16[2,16,4096]{2,1,0:T(8,128)(2,1)S(1)}, u32[]{:S(2)}) copy-start(bf16[2,16,4096]{2,1,0:T(8,128)(2,1)S(1)} %collective-permute-done.refs_1_) | copy-start | bytes 786436
  181.1 13.0 %collective-permute-start.6 = (bf16[2,16,4096]{2,1,0:T(8,128)(2,1)}, bf16[2,16,4096]{2,1,0:T(8,128)(2,1)S(1)}, u32[]{:S(2)}, u32[]{:S(2)}) collective-permute-start(bf16[2,16,4096]{2,1,0:T(8,128)(2,1)} %get-tuple-element.48), channel_id=1, source_target_pairs={{0,96},{32,64},{64,32},{96,0},{1,97},{33,65},{65,33},{97,1},{2,98}... | collective-permute-start | bytes 786440 | tf_op jit(solution)/shard_map/ppermute | solution.py:509
  181.5 12.6 %copy-start.4 = (bf16[2,16,4096]{2,1,0:T(8,128)(2,1)}, bf16[2,16,4096]{2,1,0:T(8,128)(2,1)S(1)}, u32[]{:S(2)}) copy-start(bf16[2,16,4096]{2,1,0:T(8,128)(2,1)S(1)} %collective-permute-done.1.refs_2_) | copy-start | bytes 786436
  183.4 10.8 %copy-start.5 = (bf16[2,16,4096]{2,1,0:T(8,128)(2,1)}, bf16[2,16,4096]{2,1,0:T(8,128)(2,1)S(1)}, u32[]{:S(2)}) copy-start(bf16[2,16,4096]{2,1,0:T(8,128)(2,1)S(1)} %collective-permute-done.2.refs_3_) | copy-start | bytes 786436
  183.4 10.8 %copy-start.6 = (bf16[2,16,4096]{2,1,0:T(8,128)(2,1)}, bf16[2,16,4096]{2,1,0:T(8,128)(2,1)S(1)}, u32[]{:S(2)}) copy-start(bf16[2,16,4096]{2,1,0:T(8,128)(2,1)S(1)} %collective-permute-done.4.refs_5_) | copy-start | bytes 786436
  188.4 5.8 %copy-start.7 = (bf16[2,16,4096]{2,1,0:T(8,128)(2,1)}, bf16[2,16,4096]{2,1,0:T(8,128)(2,1)S(1)}, u32[]{:S(2)}) copy-start(bf16[2,16,4096]{2,1,0:T(8,128)(2,1)S(1)} %collective-permute-done.5.refs_6_) | copy-start | bytes 786436
  194.2 0.7 copy-start.8

commit v8 on v7

--- a/solution.py
+++ b/solution.py
@@ -12,7 +12,7 @@
 MAXS = 8
 RBLK = 32
 LANES = 128
-RANGE_UNROLL = 8
+RANGE_UNROLL = 16
 TILE = 64
 VMEM = 56 * 1024 * 1024
 F32 = jnp.float32
@@ -351,8 +351,8 @@
     lax.fori_loop(0, subs, aperture, 0)
 
     def row_sum(turn, carry):
-        for u in range(4):
-            row = turn * 4 + u
+        for u in range(8):
+            row = turn * 8 + u
             real = jnp.zeros((tile, size), F32)
             imag = jnp.zeros((tile, size), F32)
             for index in range(subs):
@@ -366,7 +366,7 @@
             ).astype(BF16)
         return carry
 
-    lax.fori_loop(0, rows // 4, row_sum, 0)
+    lax.fori_loop(0, rows // 8, row_sum, 0)
     first = jnp.dot(summed[...], u_ref[...], preferred_element_type=F32)
     for r in range(rows):
         real = first[r * tile : (r + 1) * tile, :size]

time: 201 us -> 199 us (0.990)
  Pallas kernels: 77.4 us -> 73.6 us
    pallas_call x2, Pallas kernels: 26 us -> 22.4 us  [range_compress(): pl.pallas_call(functools.partial(range_kernel, size, splits), grid=(1,),...]
  transfers between devices with their start and end apart: 9 -> 9, of which waited for: 6 -> 6; matrix products, arithmetic and copies ran while one was open for 1% -> 1% of each run, Pallas kernels for 29% -> 28%
where the time goes in v8:
time: 199 us; the launch traced here: 196 us
  Pallas kernels  73.6 us (37%)
  waiting for transfers between devices  54.4 us (27%)
  blocking collectives  35.4 us (18%)
  starting transfers between devices  26.1 us (13%)
  local copies, waits for them, and re-layouts  4.44 us (2%)
    all_to_all x2, waiting for transfers between devices, spread(): got = lax.all_to_all(sent, ('pul', 'sub'), 0, 0, tiled=True)  41.2 us
    all_to_all x1, blocking collectives, spread(): got = lax.all_to_all(sent, ('pul', 'sub'), 0, 0, tiled=True)  35.4 us
    pallas_call x2, Pallas kernels, range_compress(): pl.pallas_call(functools.partial(range_kernel, size, splits), grid=(1,),...  22.4 us
    all_to_all x2, starting transfers between devices, spread(): got = lax.all_to_all(sent, ('pul', 'sub'), 0, 0, tiled=True)  18.3 us
    pallas_call x3, Pallas kernels, image_rows(): pl.pallas_call(functools.partial(image_kernel, len(before), finish), grid...  17.5 us
    pallas_call x2, Pallas kernels, doppler_forward(): pl.pallas_call(functools.partial(doppler_kernel, rows), grid=(subs,), in_...  15.3 us
    ppermute x6, waiting for transfers between devices, swap(): lax.ppermute(pieces[k], 'sub', [(i, i ^ k) for i in range(subs)])  12.6 us
    pallas_call x1, Pallas kernels, azimuth_factors(): pl.pallas_call(factor_kernel, grid=(subs,), in_specs=[pl.BlockSpec(memory...  11.7 us
  transfers between devices with their start and end apart: 9, of which 6 were waited for; matrix products, arithmetic and copies ran while one was open for 1% of the time, Pallas kernels for 28%

profile of v8, /device:TPU:7, one launch (start us, length us, event | category | flops | bytes accessed | tf_op | source)
XLA Modules:
  0.0 195.6 jit_solution(15857217194198747577)
XLA Ops:
  0.0 0.0 copy-start
  0.0 0.8 broadcast_multiply_fusion
  0.8 0.1 mul.27
  0.8 0.1 copy.30
  0.9 0.7 pad_maximum_fusion.phase_ref
  1.6 4.0 %range_middle.1.t_ref = bf16[64,128,128]{2,1,0:T(8,128)(2,1)} custom-call(f32[64,128]{1,0:T(8,128)} %pad_maximum_fusion.phase_ref, bf16[64,128,128]{2,1,0:T(8,128)(2,1)} %constant.37.clone.wave_ref), custom_call_target="tpu_custom_call" | custom-call | tf_op jit(solution)/shard_map/range_middle/pallas_call | solution.py:61
  5.6 11.2 %range_compress.2 = bf16[128,2,32,256]{3,2,1,0:T(8,128)(2,1)} custom-call(bf16[2,4096,512]{2,1,0:T(8,128)(2,1)} %bitcast.14, bf16[128,128]{1,0:T(8,128)(2,1)} %constant.38.clone.w_ref, bf16[64,128,128]{2,1,0:T(8,128)(2,1)} %range_middle.1.t_ref, bf16[128,128]{1,0:T(8,128)(2,1)} %constant.39.clone.v_ref), custom_call_target="tpu_custom_call" | custom-call | tf_op jit(solution)/shard_map/range_compress/pallas_call | solution.py:158
  16.8 11.3 %all-to-all-start = ((bf16[128,2,32,256]{3,2,1,0:T(8,128)(2,1)}), bf16[128,2,32,256]{3,2,1,0:T(8,128)(2,1)}, u32[]{:S(2)}, u32[]{:S(2)}) async-start(bf16[128,2,32,256]{3,2,1,0:T(8,128)(2,1)} %range_compress.2), calls=%async_computation | async-start | bytes 8388608 | tf_op jit(solution)/shard_map/all_to_all | solution.py:504
  28.1 0.0 copy-done
  28.1 0.1 constant_dynamic-slice_fusion
  28.1 0.7 copy.32
  28.9 0.0 copy-done.9
  28.9 0.1 multiply_bitcast_fusion
  29.0 0.8 copy.31
  29.8 11.2 %range_compress.3 = (bf16[128,2,16,256]{3,2,1,0:T(8,128)(2,1)}, bf16[128,2,16,256]{3,2,1,0:T(8,128)(2,1)}) custom-call(bf16[2,4096,512]{2,1,0:T(8,128)(2,1)} %bitcast.15, bf16[128,128]{1,0:T(8,128)(2,1)} %constant.38.clone.w_ref, bf16[64,128,128]{2,1,0:T(8,128)(2,1)} %range_middle.1.t_ref, bf16[128,128]{1,0:T(8,128)(2,1)} %constant.39.clone.v_ref), custom_call_target="tpu_custom_call" | custom-call | tf_op jit(solution)/shard_map/range_compress/pallas_call | solution.py:158
  41.0 0.0 copy-done.10
  41.0 0.6 dynamic_slice.6.kappa_ref
  41.6 11.7 %azimuth_factors.1.refs_2_ = bf16[2,4,32,2,64,128]{5,4,3,2,1,0:T(8,128)(2,1)} custom-call(f32[32]{0:T(128)} %dynamic_slice.6.kappa_ref, f32[4,128,128]{2,1,0:T(8,128)} %bitcast.21), custom_call_target="tpu_custom_call" | custom-call | tf_op jit(solution)/shard_map/azimuth_factors/pallas_call | solution.py:310
  53.3 27.2 %all-to-all-done = bf16[128,2,32,256]{3,2,1,0:T(8,128)(2,1)} async-done(((bf16[128,2,32,256]{3,2,1,0:T(8,128)(2,1)}), bf16[128,2,32,256]{3,2,1,0:T(8,128)(2,1)}, u32[]{:S(2)}, u32[]{:S(2)}) %all-to-all-start) | async-done | bytes 4194336 | tf_op jit(solution)/shard_map/all_to_all | solution.py:504
  80.5 0.0 copy-done.2
  80.5 35.4 %all_to_all.15 = bf16[128,2,16,256]{3,2,1,0:T(8,128)(2,1)} all-to-all(bf16[128,2,16,256]{3,2,1,0:T(8,128)(2,1)S(1)} %copy-done.2), channel_id=1, replica_groups=mesh['sub'=4,'pul'=32] {'pul','sub'}, dimensions={0} | all-to-all | bytes 4194304 | tf_op jit(solution)/shard_map/all_to_all | solution.py:504
  115.9 7.0 %all-to-all-start.2 = ((bf16[128,2,16,256]{3,2,1,0:T(8,128)(2,1)}), bf16[128,2,16,256]{3,2,1,0:T(8,128)(2,1)S(1)}, u32[]{:S(2)}, u32[]{:S(2)}) async-start(bf16[128,2,16,256]{3,2,1,0:T(8,128)(2,1)} %get-tuple-element.35), calls=%async_computation.2 | async-start | bytes 4194304 | tf_op jit(solution)/shard_map/all_to_all | solution.py:504
  123.0 8.0 %doppler_forward.2 = (bf16[2,4,16,2,64,128]{5,4,3,2,1,0:T(8,128)(2,1)}, bf16[2,4,8,2,64,128]{5,4,3,2,1,0:T(8,128)(2,1)}) custom-call(bf16[32,4,2,32,256]{4,3,2,1,0:T(8,128)(2,1)} %bitcast.3.first, bf16[32,4,2,16,256]{4,3,2,1,0:T(8,128)(2,1)} %bitcast.16, bf16[256,256]{1,0:T(8,128)(2,1)} %constant.40.clone.w_ref, f32[128,128]{1,0:T(8,128)} %constant.41.clone.cos_ref.refs_4_, ...), custom_call_target="tpu_custom_call" | custom-call | tf_op jit(solution)/shard_map/doppler_forward/pallas_call | solution.py:246
  130.9 2.3 %collective-permute-start.3 = (bf16[2,4,8,2,64,128]{5,4,3,2,1,0:T(8,128)(2,1)}, bf16[2,4,8,2,64,128]{5,4,3,2,1,0:T(8,128)(2,1)}, u32[]{:S(2)}, u32[]{:S(2)}) collective-permute-start(bf16[2,4,8,2,64,128]{5,4,3,2,1,0:T(8,128)(2,1)} %get-tuple-element.44), channel_id=1, source_target_pairs={{32,0},{64,32},{96,64},{1,96},{33,1},{65,33},{97,65},{2,97},{34,2}... | collective-permute-start | bytes 6291464 | tf_op jit(solution)/shard_map/ppermute | solution.py:531
  133.2 4.5 %image_rows.3.refs_9_ = bf16[8,2,128,128]{3,2,1,0:T(8,128)(2,1)} custom-call(bf16[2,4,16,2,64,128]{5,4,3,2,1,0:T(8,128)(2,1)} %get-tuple-element.34.refs_0_.refs_1_, bf16[2,4,16,2,64,128]{5,4,3,2,1,0:T(8,128)(2,1)} %get-tuple-element.34.refs_0_.refs_1_, bf16[2,4,32,2,64,128]{5,4,3,2,1,0:T(8,128)(2,1)} %azimuth_factors.1.refs_2_, s32[128,128]{1,0:T(8,128)} %bitcast.18, ...), custom_call_target="tpu_custom_call" | custom-call | tf_op jit(solution)/shard_map/image_rows/pallas_call | solution.py:454
  137.7 14.1 %all-to-all-done.2 = bf16[128,2,16,256]{3,2,1,0:T(8,128)(2,1)S(1)} async-done(((bf16[128,2,16,256]{3,2,1,0:T(8,128)(2,1)}), bf16[128,2,16,256]{3,2,1,0:T(8,128)(2,1)S(1)}, u32[]{:S(2)}, u32[]{:S(2)}) %all-to-all-start.2) | async-done | bytes 2097184 | tf_op jit(solution)/shard_map/all_to_all | solution.py:504
  151.8 1.4 copy-done.1
  153.2 7.3 %doppler_forward.3.refs_1_.refs_0_ = bf16[2,4,16,2,64,128]{5,4,3,2,1,0:T(8,128)(2,1)} custom-call(bf16[32,4,2,32,256]{4,3,2,1,0:T(8,128)(2,1)} %bitcast.3.first, bf16[32,4,2,16,256]{4,3,2,1,0:T(8,128)(2,1)} %bitcast.17, bf16[256,256]{1,0:T(8,128)(2,1)} %constant.40.clone.w_ref, f32[128,128]{1,0:T(8,128)} %constant.41.clone.cos_ref.refs_4_, ...), custom_call_target="tpu_custom_call" | custom-call | tf_op jit(solution)/shard_map/doppler_forward/pallas_call | solution.py:246
  160.5 5.6 %image_rows.4 = (bf16[2,16,4096]{2,1,0:T(8,128)(2,1)}, bf16[2,16,4096]{2,1,0:T(8,128)(2,1)}, bf16[2,16,4096]{2,1,0:T(8,128)(2,1)}, bf16[2,16,4096]{2,1,0:T(8,128)(2,1)}) custom-call(bf16[2,4,16,2,64,128]{5,4,3,2,1,0:T(8,128)(2,1)} %get-tuple-element.34.refs_0_.refs_1_, bf16[2,4,16,2,64,128]{5,4,3,2,1,0:T(8,128)(2,1)} %doppler_forward.3.refs_1_.refs_0_, ...), custom_call_target="tpu_custom_call" | custom-call | tf_op jit(solution)/shard_map/image_rows/pallas_call | solution.py:454
  166.1 1.1 collective-permute-start
  167.2 0.0 collective-permute-start.1
  167.2 1.7 collective-permute-start.2
  168.9 0.6 collective-permute-done.3.refs_1_
  169.5 7.4 %image_rows.5 = (bf16[2,16,4096]{2,1,0:T(8,128)(2,1)}, bf16[2,16,4096]{2,1,0:T(8,128)(2,1)}, bf16[2,16,4096]{2,1,0:T(8,128)(2,1)}, bf16[2,16,4096]{2,1,0:T(8,128)(2,1)}) custom-call(bf16[2,4,16,2,64,128]{5,4,3,2,1,0:T(8,128)(2,1)} %doppler_forward.3.refs_1_.refs_0_, bf16[2,4,8,2,64,128]{5,4,3,2,1,0:T(8,128)(2,1)} %collective-permute-done.3.refs_1_, ...), custom_call_target="tpu_custom_call" | custom-call | tf_op jit(solution)/shard_map/image_rows/pallas_call | solution.py:454
  176.9 0.0 collective-permute-start.4
  176.9 2.4 %collective-permute-start.5 = (bf16[2,16,4096]{2,1,0:T(8,128)(2,1)}, bf16[2,16,4096]{2,1,0:T(8,128)(2,1)S(1)}, u32[]{:S(2)}, u32[]{:S(2)}) collective-permute-start(bf16[2,16,4096]{2,1,0:T(8,128)(2,1)} %get-tuple-element.47), channel_id=1, source_target_pairs={{0,64},{32,96},{64,0},{96,32},{1,65},{33,97},{65,1},{97,33},{2,66}... | collective-permute-start | bytes 786440 | tf_op jit(solution)/shard_map/ppermute | solution.py:509
  179.3 0.0 collective-permute-done.refs_1_
  179.3 0.4 collective-permute-start.6
  179.7 0.0 collective-permute-done.1.refs_2_
  179.7 1.8 collective-permute-done.2.refs_3_
  181.5 0.0 collective-permute-done.4.refs_5_
  181.5 5.0 %collective-permute-done.5.refs_6_ = bf16[2,16,4096]{2,1,0:T(8,128)(2,1)S(1)} collective-permute-done((bf16[2,16,4096]{2,1,0:T(8,128)(2,1)}, bf16[2,16,4096]{2,1,0:T(8,128)(2,1)S(1)}, u32[]{:S(2)}, u32[]{:S(2)}) %collective-permute-start.5) | collective-permute-done | bytes 262176 | tf_op jit(solution)/shard_map/ppermute | solution.py:509
  186.5 5.8 %collective-permute-done.6.refs_7_ = bf16[2,16,4096]{2,1,0:T(8,128)(2,1)S(1)} collective-permute-done((bf16[2,16,4096]{2,1,0:T(8,128)(2,1)}, bf16[2,16,4096]{2,1,0:T(8,128)(2,1)S(1)}, u32[]{:S(2)}, u32[]{:S(2)}) %collective-permute-start.6) | collective-permute-done | bytes 262176 | tf_op jit(solution)/shard_map/ppermute | solution.py:509
  192.3 0.0 copy-done.4
  192.3 0.0 copy-done.6
  192.3 0.0 copy-done.7
  192.3 0.7 copy-done.8
  193.0 2.7 %place_rows.1 = bf16[2,128,4096]{2,1,0:T(8,128)(2,1)} custom-call(s32[1]{0:T(128)} %bitcast.refs_7_.mine_ref, bf16[2,16,4096]{2,1,0:T(8,128)(2,1)} %get-tuple-element.40.refs_0_, bf16[2,16,4096]{2,1,0:T(8,128)(2,1)} %copy-done.3, bf16[2,16,4096]{2,1,0:T(8,128)(2,1)} %copy-done.4, bf16[2,16,4096]{2,1,0:T(8,128)(2,1)} %copy-done.5, ...), custom_call_target="tpu_custom_call" | custom-call | tf_op jit(solution)/shard_map/place_rows/pallas_call | solution.py:478
  (13 shorter events, 0.0 us)
Async XLA Ops:
  0.0 28.1 %copy-start = (s32[4,16384]{1,0:T(4,128)S(1)}, s32[4,16384]{1,0:T(4,128)}, u32[]{:S(2)}) copy-start(s32[4,16384]{1,0:T(4,128)} %param.33) | copy-start | bytes 786436
  16.8 12.1 %copy-start.9 = (f32[4,16384]{1,0:T(4,128)S(1)}, f32[4,16384]{1,0:T(4,128)}, u32[]{:S(2)}) copy-start(f32[4,16384]{1,0:T(4,128)} %param.32) | copy-start | bytes 786436
  16.8 63.7 %all-to-all-start = ((bf16[128,2,32,256]{3,2,1,0:T(8,128)(2,1)}), bf16[128,2,32,256]{3,2,1,0:T(8,128)(2,1)}, u32[]{:S(2)}, u32[]{:S(2)}) async-start(bf16[128,2,32,256]{3,2,1,0:T(8,128)(2,1)} %range_compress.2), calls=%async_computation | async-start | bytes 8388608 | tf_op jit(solution)/shard_map/all_to_all | solution.py:504
  29.8 11.2 %copy-start.10 = (f32[128]{0:T(128)S(1)}, f32[128]{0:T(128)}, u32[]{:S(2)}) copy-start(f32[128]{0:T(128)} %param.31) | copy-start | bytes 1540
  41.6 38.9 %copy-start.2 = (bf16[128,2,16,256]{3,2,1,0:T(8,128)(2,1)S(1)}, bf16[128,2,16,256]{3,2,1,0:T(8,128)(2,1)}, u32[]{:S(2)}) copy-start(bf16[128,2,16,256]{3,2,1,0:T(8,128)(2,1)} %get-tuple-element.31) | copy-start | bytes 6291460
  115.9 35.9 %all-to-all-start.2 = ((bf16[128,2,16,256]{3,2,1,0:T(8,128)(2,1)}), bf16[128,2,16,256]{3,2,1,0:T(8,128)(2,1)S(1)}, u32[]{:S(2)}, u32[]{:S(2)}) async-start(bf16[128,2,16,256]{3,2,1,0:T(8,128)(2,1)} %get-tuple-element.35), calls=%async_computation.2 | async-start | bytes 4194304 | tf_op jit(solution)/shard_map/all_to_all | solution.py:504
  130.9 38.6 %collective-permute-start.3 = (bf16[2,4,8,2,64,128]{5,4,3,2,1,0:T(8,128)(2,1)}, bf16[2,4,8,2,64,128]{5,4,3,2,1,0:T(8,128)(2,1)}, u32[]{:S(2)}, u32[]{:S(2)}) collective-permute-start(bf16[2,4,8,2,64,128]{5,4,3,2,1,0:T(8,128)(2,1)} %get-tuple-element.44), channel_id=1, source_target_pairs={{32,0},{64,32},{96,64},{1,96},{33,1},{65,33},{97,65},{2,97},{34,2}... | collective-permute-start | bytes 6291464 | tf_op jit(solution)/shard_map/ppermute | solution.py:531
  151.8 1.4 copy-start.1
  166.1 13.2 %collective-permute-start = (bf16[2,16,4096]{2,1,0:T(8,128)(2,1)}, bf16[2,16,4096]{2,1,0:T(8,128)(2,1)S(1)}, u32[]{:S(2)}, u32[]{:S(2)}) collective-permute-start(bf16[2,16,4096]{2,1,0:T(8,128)(2,1)} %get-tuple-element.41), channel_id=1, source_target_pairs={{0,32},{32,0},{64,96},{96,64},{1,33},{33,1},{65,97},{97,65},{2,34}... | collective-permute-start | bytes 786440 | tf_op jit(solution)/shard_map/ppermute | solution.py:509
  167.2 12.5 %collective-permute-start.1 = (bf16[2,16,4096]{2,1,0:T(8,128)(2,1)}, bf16[2,16,4096]{2,1,0:T(8,128)(2,1)S(1)}, u32[]{:S(2)}, u32[]{:S(2)}) collective-permute-start(bf16[2,16,4096]{2,1,0:T(8,128)(2,1)} %get-tuple-element.42), channel_id=1, source_target_pairs={{0,64},{32,96},{64,0},{96,32},{1,65},{33,97},{65,1},{97,33},{2,66}... | collective-permute-start | bytes 786440 | tf_op jit(solution)/shard_map/ppermute | solution.py:509
  167.2 14.3 %collective-permute-start.2 = (bf16[2,16,4096]{2,1,0:T(8,128)(2,1)}, bf16[2,16,4096]{2,1,0:T(8,128)(2,1)S(1)}, u32[]{:S(2)}, u32[]{:S(2)}) collective-permute-start(bf16[2,16,4096]{2,1,0:T(8,128)(2,1)} %get-tuple-element.43), channel_id=1, source_target_pairs={{0,96},{32,64},{64,32},{96,0},{1,97},{33,65},{65,33},{97,1},{2,98}... | collective-permute-start | bytes 786440 | tf_op jit(solution)/shard_map/ppermute | solution.py:509
  176.9 4.6 %collective-permute-start.4 = (bf16[2,16,4096]{2,1,0:T(8,128)(2,1)}, bf16[2,16,4096]{2,1,0:T(8,128)(2,1)S(1)}, u32[]{:S(2)}, u32[]{:S(2)}) collective-permute-start(bf16[2,16,4096]{2,1,0:T(8,128)(2,1)} %get-tuple-element.46), channel_id=1, source_target_pairs={{0,32},{32,0},{64,96},{96,64},{1,33},{33,1},{65,97},{97,65},{2,34}... | collective-permute-start | bytes 786440 | tf_op jit(solution)/shard_map/ppermute | solution.py:509
  176.9 9.6 %collective-permute-start.5 = (bf16[2,16,4096]{2,1,0:T(8,128)(2,1)}, bf16[2,16,4096]{2,1,0:T(8,128)(2,1)S(1)}, u32[]{:S(2)}, u32[]{:S(2)}) collective-permute-start(bf16[2,16,4096]{2,1,0:T(8,128)(2,1)} %get-tuple-element.47), channel_id=1, source_target_pairs={{0,64},{32,96},{64,0},{96,32},{1,65},{33,97},{65,1},{97,33},{2,66}... | collective-permute-start | bytes 786440 | tf_op jit(solution)/shard_map/ppermute | solution.py:509
  179.3 13.0 %copy-start.3 = (bf16[2,16,4096]{2,1,0:T(8,128)(2,1)}, bf16[2,16,4096]{2,1,0:T(8,128)(2,1)S(1)}, u32[]{:S(2)}) copy-start(bf16[2,16,4096]{2,1,0:T(8,128)(2,1)S(1)} %collective-permute-done.refs_1_) | copy-start | bytes 786436
  179.3 13.0 %collective-permute-start.6 = (bf16[2,16,4096]{2,1,0:T(8,128)(2,1)}, bf16[2,16,4096]{2,1,0:T(8,128)(2,1)S(1)}, u32[]{:S(2)}, u32[]{:S(2)}) collective-permute-start(bf16[2,16,4096]{2,1,0:T(8,128)(2,1)} %get-tuple-element.48), channel_id=1, source_target_pairs={{0,96},{32,64},{64,32},{96,0},{1,97},{33,65},{65,33},{97,1},{2,98}... | collective-permute-start | bytes 786440 | tf_op jit(solution)/shard_map/ppermute | solution.py:509
  179.7 12.6 %copy-start.4 = (bf16[2,16,4096]{2,1,0:T(8,128)(2,1)}, bf16[2,16,4096]{2,1,0:T(8,128)(2,1)S(1)}, u32[]{:S(2)}) copy-start(bf16[2,16,4096]{2,1,0:T(8,128)(2,1)S(1)} %collective-permute-done.1.refs_2_) | copy-start | bytes 786436
  181.5 10.8 %copy-start.5 = (bf16[2,16,4096]{2,1,0:T(8,128)(2,1)}, bf16[2,16,4096]{2,1,0:T(8,128)(2,1)S(1)}, u32[]{:S(2)}) copy-start(bf16[2,16,4096]{2,1,0:T(8,128)(2,1)S(1)} %collective-permute-done.2.refs_3_) | copy-start | bytes 786436
  181.5 10.8 %copy-start.6 = (bf16[2,16,4096]{2,1,0:T(8,128)(2,1)}, bf16[2,16,4096]{2,1,0:T(8,128)(2,1)S(1)}, u32[]{:S(2)}) copy-start(bf16[2,16,4096]{2,1,0:T(8,128)(2,1)S(1)} %collective-permute-done.4.refs_5_) | copy-start | bytes 786436
  186.5 5.8 %copy-start.7 = (bf16[2,16,4096]{2,1,0:T(8,128)(2,1)}, bf16[2,16,4096]{2,1,0:T(8,128)(2,1)S(1)}, u32[]{:S(2)}) copy-start(bf16[2,16,4096]{2,1,0:T(8,128)(2,1)S(1)} %collective-permute-done.5.refs_6_) | copy-start | bytes 786436
  192.3 0.7 copy-start.8
